TPU v7x, 32 devices: a whole 2x2x4 slice. The times are simulated.
32 devices in a mesh: seq: 8 (over z, y), kv: 4 (over x, core).
Axes of the slice: x: 2, y: 2, z: 4, core: 2. Of those that a mesh axis runs over, the one named last changes fastest.
Arguments:
- queries: bfloat16 [2048, 28, 128], P('seq', 'kv'), may hold values from -8 to 8
- keys: bfloat16 [2048, 4, 128], P('seq', 'kv'), may hold values from -8 to 8
- values: bfloat16 [2048, 4, 128], P('seq', 'kv'), may hold values from -6 to 6
- out_weight: bfloat16 [3584, 3584], P('kv'), may hold values from -0.5 to 0.5
Outputs:
- layer_output: bfloat16 [2048, 3584], P('seq', 'kv')
All inputs are finite; a program needn't handle non-finite values.
Results may differ from a plain program's by a relative error of at most 0.012.
Values may be sent and summed in bfloat16 or wider, within the bound.
No kernel may reach another device: no remote copies, remote signals or barrier semaphores. Data moves between devices by JAX's collectives and lax.ppermute only.
A program may use at most 64 MiB of HBM per device.

v0:
```python
import math

import jax
import jax.numpy as jnp
from jax import lax
from jax.sharding import PartitionSpec as P

HEAD = 128
GROUP = 7
SPAN = 1024
LOCAL = 32


THETA = 10000000.0
NEG = -1e30


def rotate(block_data, position):
    half_width = block_data.shape[-1] // 2
    ladder = jnp.arange(half_width, dtype=jnp.float32)
    inverse = jnp.exp(ladder * (-2.0 * math.log(THETA) / block_data.shape[-1]))
    angles = position.astype(jnp.float32)[..., None] * inverse
    cosine = jnp.cos(angles)
    sine_part = jnp.sin(angles)
    widened = block_data.astype(jnp.float32)
    first_half = widened[..., :half_width]
    second = widened[..., half_width:]
    return jnp.concatenate(
        [first_half * cosine - second * sine_part, second * cosine + first_half * sine_part],
        axis=-1,
    ).astype(jnp.bfloat16)


def prepare(query_rows, first_token):
    token_count = query_rows.shape[0]
    group_size = query_rows.shape[1]
    lane_count = query_rows.shape[2]
    tokens = first_token + jnp.arange(token_count, dtype=jnp.int32)
    offset = tokens % SPAN

    def spread(position):
        return jnp.broadcast_to(position[:, None], (token_count, group_size))

    inner_query = rotate(query_rows, spread(offset)).reshape(token_count * group_size, lane_count)
    adjacent_query = rotate(query_rows, spread(jnp.minimum(offset + SPAN, SPAN + LOCAL))).reshape(
        token_count * group_size, lane_count
    )
    distant_query = rotate(query_rows, spread(jnp.full_like(offset, SPAN + LOCAL))).reshape(
        token_count * group_size, lane_count
    )
    return (inner_query, adjacent_query, distant_query, jnp.repeat(tokens, group_size))


def absorb(carried, scores, allowed, value_block):
    run_max, run_sum, run_acc = carried
    masked = jnp.where(allowed, scores, NEG)
    new_max = jnp.maximum(run_max, jnp.max(masked, axis=1))
    weights = jnp.where(allowed, jnp.exp(masked - new_max[:, None]), 0.0)
    factor = jnp.exp(run_max - new_max)
    new_sum = factor * run_sum + jnp.sum(weights, axis=1)
    weighted = factor[:, None] * run_acc + jnp.dot(
        weights.astype(jnp.bfloat16), value_block, preferred_element_type=jnp.float32
    )
    return (new_max, new_sum, weighted)


def make_step(query_sets, score_scale, carries, key_piece):
    key_rows, value_rows = key_piece
    piece_len = key_rows.shape[0]
    block_len = math.gcd(piece_len, math.gcd(SPAN, 1024))

    def one_block(block_index, states):
        offset = block_index * block_len
        key_block = lax.dynamic_slice_in_dim(key_rows, offset, block_len, 0)
        value_block = lax.dynamic_slice_in_dim(value_rows, offset, block_len, 0)
        key_tokens = offset + jnp.arange(block_len, dtype=jnp.int32)
        key_spans = key_tokens // SPAN
        first_span = offset // SPAN
        last_span = (offset + block_len - 1) // SPAN
        updated = []
        for query_set, carried in zip(query_sets, states):
            inner_query, adjacent_query, distant_query, row_tokens = query_set
            row_spans = row_tokens // SPAN
            low_span = jnp.min(row_spans)
            high_span = jnp.max(row_spans)

            def skipped(current):
                return current

            def distant(current):
                scores = (
                    jnp.einsum(
                        "rd,kd->rk", distant_query, key_block, preferred_element_type=jnp.float32
                    )
                    * score_scale
                )
                return absorb(current, scores, True, value_block)

            def adjacent(current):
                scores = (
                    jnp.einsum(
                        "rd,kd->rk", adjacent_query, key_block, preferred_element_type=jnp.float32
                    )
                    * score_scale
                )
                return absorb(current, scores, True, value_block)

            def inner(current):
                scores = (
                    jnp.einsum(
                        "rd,kd->rk", inner_query, key_block, preferred_element_type=jnp.float32
                    )
                    * score_scale
                )
                return absorb(
                    current, scores, key_tokens[None, :] <= row_tokens[:, None], value_block
                )

            def blended(current):
                inner_scores = (
                    jnp.einsum(
                        "rd,kd->rk", inner_query, key_block, preferred_element_type=jnp.float32
                    )
                    * score_scale
                )
                adjacent_scores = (
                    jnp.einsum(
                        "rd,kd->rk", adjacent_query, key_block, preferred_element_type=jnp.float32
                    )
                    * score_scale
                )
                distant_scores = (
                    jnp.einsum(
                        "rd,kd->rk", distant_query, key_block, preferred_element_type=jnp.float32
                    )
                    * score_scale
                )
                inner_mask = (key_spans[None, :] == row_spans[:, None]) & (
                    key_tokens[None, :] <= row_tokens[:, None]
                )
                adjacent_mask = key_spans[None, :] == row_spans[:, None] - 1
                distant_mask = key_spans[None, :] < row_spans[:, None] - 1
                scores = jnp.where(
                    inner_mask,
                    inner_scores,
                    jnp.where(adjacent_mask, adjacent_scores, distant_scores),
                )
                return absorb(
                    current, scores, inner_mask | adjacent_mask | distant_mask, value_block
                )

            single = (first_span == last_span) & (low_span == high_span)
            branch = jnp.where(
                offset > jnp.max(row_tokens),
                0,
                jnp.where(
                    last_span < low_span - 1,
                    1,
                    jnp.where(
                        single & (first_span == high_span - 1),
                        2,
                        jnp.where(single & (first_span == high_span), 3, 4),
                    ),
                ),
            )
            updated.append(
                lax.switch(branch, [skipped, distant, adjacent, inner, blended], carried)
            )
        return tuple(updated)

    return lax.fori_loop(0, piece_len // block_len, one_block, carries)


def shards(queries, keys, values, out_weight):
    token_count = queries.shape[0]
    seq_rank = lax.axis_index("seq")
    key_tokens = seq_rank * token_count + jnp.arange(token_count, dtype=jnp.int32)
    key_rot = rotate(keys[:, 0, :], key_tokens % SPAN)
    value_rows = values[:, 0, :]
    score_scale = 1.0 / math.sqrt(HEAD)
    query_sets = (prepare(queries, seq_rank * token_count),)
    initial = tuple(
        (
            (
                jnp.full((query_set[3].shape[0],), NEG, jnp.float32),
                jnp.zeros((query_set[3].shape[0],), jnp.float32),
                jnp.zeros((query_set[3].shape[0], HEAD), jnp.float32),
            )
            for query_set in query_sets
        )
    )
    results = make_step(
        query_sets,
        score_scale,
        initial,
        (
            lax.all_gather(key_rot, "seq", axis=0, tiled=True),
            lax.all_gather(value_rows, "seq", axis=0, tiled=True),
        ),
    )
    attended = [
        (outcome[2] / outcome[1][:, None])
        .astype(jnp.bfloat16)
        .reshape(outcome[1].shape[0] // GROUP, GROUP * HEAD)
        for outcome in results
    ]
    merged = attended[0]
    partial_value = jnp.dot(merged, out_weight, preferred_element_type=jnp.float32)
    return lax.psum_scatter(
        partial_value.astype(jnp.bfloat16), "kv", scatter_dimension=1, tiled=True
    )


def solution(mesh):
    return jax.shard_map(
        shards,
        mesh=mesh,
        in_specs=(P("seq", "kv", None), P("seq", "kv", None), P("seq", "kv", None), P("kv", None)),
        out_specs=P("seq", "kv"),
        check_vma=False,
    )
```

profile of v0, /device:TPU:26, one launch (start us, length us, event | category | flops | bytes accessed | tf_op | source)
XLA Modules:
  0.0 156.8 jit_solution(3660798731074819983)
XLA Ops:
  7.4 0.9 copy.29
  8.7 30.7 %all_gather.6 = bf16[2048,128]{0,1:T(8,128)(2,1)} all-gather(bf16[256,128]{0,1:T(8,128)(2,1)S(1)} %pad_maximum_fusion.3), channel_id=1, replica_groups=mesh['seq'=8,'kv'=4] {'seq'}, dimensions={0}, use_global_device_ids=true | all-gather | bytes 589824 | tf_op jit(solution)/shard_map/all_gather | solution.py:197
  39.5 1.3 copy.30
  40.8 1.2 fusion.66
  45.1 1.0 concatenate.32
  46.0 33.2 %all-gather = bf16[2048,1,128]{2,0,1:T(8,128)(2,1)} all-gather(bf16[256,1,128]{2,0,1:T(8,128)(2,1)S(1)} %copy-done), channel_id=2, replica_groups=mesh['seq'=8,'kv'=4] {'seq'}, dimensions={0}, use_global_device_ids=true | all-gather | bytes 589824 | tf_op jit(solution)/shard_map/all_gather | solution.py:198
  79.8 1.3 pad_maximum_fusion
  81.1 25.8 %while.24 = (s32[]{:T(128)}, f32[1792]{0:T(1024)S(1)}, f32[1792]{0:T(1024)S(1)}, f32[1792,128]{1,0:T(8,128)S(1)}, s32[]{:T(128)}, /*index=5*/bf16[2048,128]{0,1:...) while((s32[]{:T(128)}, f32[1792]{0:T(1024)S(1)}, ...), condition=%wide.region_17.18_spmd.clone.clone, body=%wide.region_1.17_spmd.clone.clone.sunk | while | flops 1941949440 | bytes 57499660 | solution.py:171
  86.3 1.0 constant_dynamic-slice_fusion.5
  87.3 1.0 constant_dynamic-slice_fusion.4
  88.4 4.5 %conditional.4 = ((f32[1792]{0:T(1024)S(1)}, f32[1792]{0:T(1024)S(1)}, f32[1792,128]{1,0:T(8,128)S(1)})) conditional(s32[]{:T(128)} %clamp.17, (f32[1792]{0:T(1024)S(1)}, f32[1792]{0:T(1024)S(1)}, f32[1792,128]{1,0:T(8,128)S(1)}) %tuple.115, (bf16[1792,128]{1,0:T(8,128)(2,1)S(1)}, bf16[1024,128]{1,0:T(8,128)(2,1)S(1)}, ...), branch_computations={%region_4.4_spmd, %region_5.7_spmd, %region_8.10_spmd, %region_11.... | conditional | flops 1941917952 | bytes 55884836 | solution.py:167
  88.5 1.1 multiply_reduce_fusion.1
  89.6 1.2 fusion.19
  90.9 2.0 %fusion.24 = f32[1792,128]{1,0:T(8,128)S(1)} fusion(bf16[1024,128]{1,0:T(8,128)(2,1)S(1)} %get-tuple-element.599, f32[1792,1024]{0,1:T(8,128)S(1)} %get-tuple-element.789, f32[1792]{0:T(1024)S(1)} %max.10, f32[1792,128]{1,0:T(8,128)S(1)} %get-tuple-element.598, f32[1792]{0:T(1024)S(1)} %get-tuple-element.780), kind=kOutput, calls=%fused_computation.22 | convolution fusion | flops 475725824 | bytes 9451520 | tf_op jit(solution)/shard_map/while/body/eval_jaxpr/cond/branch_2_fun/dot_general | solution.py:61
  97.9 1.0 constant_dynamic-slice_fusion.5
  98.9 1.0 constant_dynamic-slice_fusion.4
  100.0 6.7 %conditional.4 = ((f32[1792]{0:T(1024)S(1)}, f32[1792]{0:T(1024)S(1)}, f32[1792,128]{1,0:T(8,128)S(1)})) conditional(s32[]{:T(128)} %clamp.17, (f32[1792]{0:T(1024)S(1)}, f32[1792]{0:T(1024)S(1)}, f32[1792,128]{1,0:T(8,128)S(1)}) %tuple.115, (bf16[1792,128]{1,0:T(8,128)(2,1)S(1)}, bf16[1024,128]{1,0:T(8,128)(2,1)S(1)}, ...), branch_computations={%region_4.4_spmd, %region_5.7_spmd, %region_8.10_spmd, %region_11.... | conditional | flops 1941917952 | bytes 55884836 | solution.py:167
  100.3 1.2 fusion.28
  101.5 2.4 %fusion.30 = f32[1792]{0:T(1024)S(1)} fusion(f32[1792,1024]{0,1:T(8,128)S(1)} %get-tuple-element.791, f32[1792]{0:T(1024)S(1)} %max.11, s32[1792]{0:T(1024)S(1)} %le.20, s32[1024]{0:T(1024)S(1)} %get-tuple-element.601), kind=kLoop, calls=%fused_computation.30 | loop fusion | flops 11008256 | bytes 7365632 | tf_op jit(solution)/shard_map/while/body/eval_jaxpr/cond/branch_3_fun/reduce_sum | solution.py:60
  103.9 2.8 %fusion.33 = f32[1792,128]{1,0:T(8,128)S(1)} fusion(bf16[1024,128]{1,0:T(8,128)(2,1)S(1)} %get-tuple-element.607, f32[1792,1024]{0,1:T(8,128)S(1)} %get-tuple-element.791, f32[1792]{0:T(1024)S(1)} %max.11, s32[1792]{0:T(1024)S(1)} %le.20, s32[1024]{0:T(1024)S(1)} %get-tuple-element.601, f32[1792,128]{1,0:T(8,128)S(1)} %get-tuple-element.606, ...), kind=kOutput, calls=%fused_computation.32 | convolution fusion | flops 481230848 | bytes 9462784 | tf_op jit(solution)/shard_map/while/body/eval_jaxpr/cond/branch_3_fun/dot_general | solution.py:61
  107.8 4.9 %convolution_convert_fusion = bf16[256,3584]{1,0:T(8,128)(2,1)S(1)} fusion(bf16[256,896]{1,0:T(8,128)(2,1)S(1)} %reshape.73, bf16[896,3584]{1,0:T(8,128)(2,1)} %param.14), kind=kOutput, calls=%fused_computation.72 | convolution fusion | flops 1645084672 | bytes 8716288 | tf_op jit(solution)/shard_map/dot_general | solution.py:208
  112.7 2.3 %copy.38 = bf16[256,3584]{0,1:T(8,128)(2,1)} copy(bf16[256,3584]{1,0:T(8,128)(2,1)S(1)} %convolution_convert_fusion) | data formatting | bytes 3670016
  115.0 33.0 %reduce-scatter.4.cloned.1.call-done = bf16[896,256]{1,0:T(8,128)(2,1)} async-done(((bf16[3584,256]{1,0:T(8,128)(2,1)}), bf16[896,256]{1,0:T(8,128)(2,1)}) %reduce-scatter.4.cloned.1.call-update) | async-done | bytes 458768
  148.0 2.0 %copy.39 = bf16[256,896]{1,0:T(8,128)(2,1)} copy(bf16[256,896]{0,1:T(8,128)(2,1)} %bitcast.25) | data formatting | bytes 917504
  (48 shorter events, 8.2 us)
Async XLA Ops:
  6.5 141.5 %reduce-scatter.4.cloned.1.call-start = ((), (), s32[]{:S(2)}) async-start(), calls=%async_computation.1 | async-start | bytes 2293760
  39.5 6.6 %copy-start = (bf16[256,1,128]{2,0,1:T(8,128)(2,1)S(1)}, bf16[256,1,128]{2,0,1:T(8,128)(2,1)}, u32[]{:S(2)}) copy-start(bf16[256,1,128]{2,0,1:T(8,128)(2,1)} %param.13) | copy-start | bytes 196612
Sparse Core Ops, SparseCore 0:
  115.1 32.8 reduce-scatter.3
where the time goes:
time: 160 us; the launch traced here: 157 us
  blocking collectives  63.9 us (40%)
  waiting for transfers between devices  33 us (21%)
  local copies, waits for them, and re-layouts  16.1 us (10%)
  between operations  13.6 us (8%)
  matrix products  12 us (8%)
  other arithmetic  9.51 us (6%)
  loops' own time  8.65 us (5%)
    all_gather x1, blocking collectives, shards(): lax.all_gather(value_rows, 'seq', axis=0, tiled=True)  33.2 us
    unnamed x2, waiting for transfers between devices  33 us
    all_gather x1, blocking collectives, shards(): lax.all_gather(key_rot, 'seq', axis=0, tiled=True)  30.7 us
    another operation x1, loops' own time, make_step(): return lax.fori_loop(0, piece_len // block_len, one_block, carries)  8.48 us
    unnamed x6, local copies, waits for them, and re-layouts  6.49 us
    dot_general x1, matrix products, shards(): jnp.dot(merged, out_weight, preferred_element_type=jnp.float32)  4.88 us
    dot_general x2, matrix products, absorb(): jnp.dot(weights.astype(jnp.bfloat16), value_block, preferred_element_type...  4.81 us
    reduce_sum x2, other arithmetic, absorb(): new_sum = factor * run_sum + jnp.sum(weights, axis=1)  3.63 us
  transfers between devices with their start and end apart: 1, of which 1 were waited for; matrix products, arithmetic and copies ran while one was open for 0% of the time, Pallas kernels for 0%

commit v1 on v0

v1 whole, which is shorter than its diff:
```python
import functools
import math

import jax
import jax.numpy as jnp
import numpy as np
from jax import lax
from jax.experimental import pallas as pl
from jax.experimental.pallas import tpu as pltpu
from jax.sharding import PartitionSpec as P

HEAD = 128
GROUP = 7
SPAN = 1024
LOCAL = 32
THETA = 10000000.0
NEG = -1e30
SCALE = math.log2(math.e) / math.sqrt(HEAD)
ROW_CHUNKS = 2
VMEM = pltpu.MemorySpace.VMEM


def rope_tables(block):
    inverse = np.exp(np.arange(HEAD // 2, dtype=np.float64) * (-2.0 * math.log(THETA) / HEAD))
    inner = np.arange(SPAN)
    first = np.minimum(np.arange(block) + SPAN, SPAN + LOCAL)
    far = np.full((block,), SPAN + LOCAL)
    angles = np.concatenate([inner, first, far])[:, None] * inverse
    cosine, sine = np.cos(angles), np.sin(angles)
    return (
        jnp.asarray(np.concatenate([cosine, cosine], 1), jnp.float32),
        jnp.asarray(np.concatenate([-sine, sine], 1), jnp.float32),
    )


def rotated(x, cosine, sine):
    x = x.astype(jnp.float32)
    return x * cosine + pltpu.roll(x, HEAD // 2, 1) * sine


def prepare_kernel(rank, key_ref, value_ref, cos_ref, sin_ref, out_ref):
    block = key_ref.shape[0]
    out_ref[:block] = rotated(key_ref[...], cos_ref[...], sin_ref[...]).astype(jnp.bfloat16)
    out_ref[block:] = value_ref[...]


def prepare(rank, keys, values, tables):
    block = keys.shape[0]
    per_span = SPAN // block
    table = pl.BlockSpec((block, HEAD), lambda i, rank: (rank[0] % per_span, 0))
    whole = pl.BlockSpec((block, HEAD), lambda i, rank: (0, 0))
    return pl.pallas_call(
        prepare_kernel,
        grid_spec=pltpu.PrefetchScalarGridSpec(
            num_scalar_prefetch=1,
            grid=(1,),
            in_specs=[whole, whole, table, table],
            out_specs=pl.BlockSpec((2 * block, HEAD), lambda i, rank: (0, 0)),
        ),
        out_shape=jax.ShapeDtypeStruct((2 * block, HEAD), jnp.bfloat16),
        name="rotate_keys",
    )(rank, keys, values, *tables)


def attend_kernel(offsets, groups, first, last, block, row_chunk, *refs):
    rank = refs[0][0]
    refs = list(refs[1:])
    query_ref = refs.pop(0)
    table_refs = {group: (refs.pop(0), refs.pop(0)) for group in groups}
    piece_refs = [refs.pop(0) for _ in offsets]
    if not first:
        old_acc, old_stats = refs.pop(0), refs.pop(0)
    rows = query_ref.shape[1]
    per_span = SPAN // block
    owners = [rank ^ offset for offset in offsets]
    lifts = [
        None if offset == 0 else jnp.where(owner <= rank, 0.0, -NEG).astype(jnp.float32)
        for offset, owner in zip(offsets, owners)
    ]
    tables = {group: (c[...], s[...]) for group, (c, s) in table_refs.items()}
    if 0 in offsets:
        causal = lax.broadcasted_iota(jnp.int32, (rows, block), 1) <= lax.broadcasted_iota(
            jnp.int32, (rows, block), 0
        ) + row_chunk * rows
    for head in range(GROUP):
        query = query_ref[head]
        by_group = {
            group: (rotated(query, c, s) * SCALE).astype(jnp.bfloat16)
            for group, (c, s) in tables.items()
        }
        scores = []
        for offset, piece in zip(offsets, piece_refs):
            score = lax.dot_general(
                by_group[offset // per_span],
                piece[:block],
                (((1,), (1,)), ((), ())),
                preferred_element_type=jnp.float32,
            )
            if offset == 0:
                score = jnp.where(causal, score, NEG)
            scores.append(score)
        tops = [jnp.max(score, axis=1, keepdims=True) for score in scores]
        tops = [top if lift is None else top - lift for top, lift in zip(tops, lifts)]
        top = functools.reduce(jnp.maximum, tops)
        if first:
            total = jnp.zeros_like(top)
            acc = jnp.zeros((rows, HEAD), jnp.float32)
        else:
            old_top = old_stats[:, head : head + 1]
            top = jnp.maximum(top, old_top)
            factor = jnp.exp2(old_top - top)
            total = factor * old_stats[:, GROUP + head : GROUP + head + 1]
            acc = factor * old_acc[head]
        for score, lift, piece in zip(scores, lifts, piece_refs):
            weight = jnp.exp2(score - (top if lift is None else top + lift))
            total = total + jnp.sum(weight, axis=1, keepdims=True)
            acc = acc + jnp.dot(
                weight.astype(jnp.bfloat16), piece[block:], preferred_element_type=jnp.float32
            )
        if last:
            (out_ref,) = refs
            out_ref[:, head * HEAD : (head + 1) * HEAD] = (acc / total).astype(jnp.bfloat16)
        else:
            new_acc, new_stats = refs
            new_acc[head] = acc
            new_stats[:, head : head + 1] = top
            new_stats[:, GROUP + head : GROUP + head + 1] = total


def attend(rank, offsets, queries, pieces, tables, state, last, row_chunk=0, row_chunks=1):
    block = pieces[0].shape[0] // 2
    rows = block // row_chunks
    per_span = SPAN // block
    groups = sorted({offset // per_span for offset in offsets})
    first = state is None

    def table_at(group):
        def index(i, rank):
            spans_back = rank[0] // per_span - (rank[0] ^ (group * per_span)) // per_span
            at_first = rank[0] % per_span == 0
            inner = rank[0] % per_span
            near = jnp.where(at_first, per_span, per_span + 1)
            place = jnp.where(spans_back == 1, near, per_span + 1)
            place = jnp.where(spans_back == 0, inner, place)
            return (place * row_chunks + row_chunk, 0)

        return pl.BlockSpec((rows, HEAD), index)

    by_head = pl.BlockSpec((GROUP, rows, HEAD), lambda i, rank: (0, row_chunk, 0))
    by_row = pl.BlockSpec((rows, HEAD), lambda i, rank: (row_chunk, 0))
    in_specs = [by_head]
    args = [queries]
    for group in groups:
        in_specs += [table_at(group)] * 2
        args += list(tables)
    in_specs += [pl.BlockSpec((2 * block, HEAD), lambda i, rank: (0, 0))] * len(pieces)
    args += pieces
    if not first:
        in_specs += [by_head, by_row]
        args += list(state)
    if last:
        out_specs = pl.BlockSpec((rows, GROUP * HEAD), lambda i, rank: (0, 0))
        out_shape = jax.ShapeDtypeStruct((rows, GROUP * HEAD), jnp.bfloat16)
    else:
        out_specs = [
            pl.BlockSpec((GROUP, rows, HEAD), lambda i, rank: (0, 0, 0)),
            pl.BlockSpec((rows, HEAD), lambda i, rank: (0, 0)),
        ]
        out_shape = [
            jax.ShapeDtypeStruct((GROUP, rows, HEAD), jnp.float32),
            jax.ShapeDtypeStruct((rows, HEAD), jnp.float32),
        ]
    kernel = functools.partial(
        attend_kernel, tuple(offsets), tuple(groups), first, last, block, row_chunk
    )
    pairs = GROUP * rows * block * len(pieces)
    return pl.pallas_call(
        kernel,
        grid_spec=pltpu.PrefetchScalarGridSpec(
            num_scalar_prefetch=1, grid=(1,), in_specs=in_specs, out_specs=out_specs
        ),
        out_shape=out_shape,
        cost_estimate=pl.CostEstimate(
            flops=4 * HEAD * pairs, bytes_accessed=2**21, transcendentals=pairs
        ),
        compiler_params=pltpu.CompilerParams(vmem_limit_bytes=24 * 2**20),
        name="attend_" + "_".join(map(str, offsets)),
    )(rank, *args)


def project_kernel(flip, place, own_ref, twin_ref, own_weight, twin_weight, out_ref):
    out_ref[...] = (
        jnp.dot(own_ref[...], own_weight[...], preferred_element_type=jnp.float32)
        + jnp.dot(twin_ref[...], twin_weight[...], preferred_element_type=jnp.float32)
    ).astype(out_ref.dtype)


def project(place, flip, own, twin, own_weight, twin_weight, dtype):
    rows, depth = own.shape
    kv_parts = own_weight.shape[1] // depth
    columns = own_weight.shape[1] // kv_parts
    whole = pl.BlockSpec((rows, depth), lambda i, place: (0, 0))
    weight = pl.BlockSpec((depth, columns), lambda i, place: (0, place[0] ^ flip))
    return pl.pallas_call(
        functools.partial(project_kernel, flip),
        grid_spec=pltpu.PrefetchScalarGridSpec(
            num_scalar_prefetch=1,
            grid=(1,),
            in_specs=[whole, whole, weight, weight],
            out_specs=pl.BlockSpec((rows, columns), lambda i, place: (0, 0)),
        ),
        out_shape=jax.ShapeDtypeStruct((rows, columns), dtype),
        cost_estimate=pl.CostEstimate(
            flops=4 * rows * depth * columns, bytes_accessed=4 * depth * columns, transcendentals=0
        ),
        compiler_params=pltpu.CompilerParams(vmem_limit_bytes=24 * 2**20),
        name="project_%d" % flip,
    )(place, own, twin, own_weight, twin_weight)


def swap(x, axis, size, bits):
    return lax.ppermute(x, axis, [(i, i ^ bits) for i in range(size)])


def make_shards(seq, kv):
    def shards(queries, keys, values, out_weight):
        block = queries.shape[0]
        per_span = SPAN // block
        rank = lax.axis_index("seq").astype(jnp.int32).reshape(1)
        place = lax.axis_index("kv").astype(jnp.int32).reshape(1)
        tables = rope_tables(block)
        by_head = jnp.transpose(queries, (1, 0, 2))
        twin_weight = swap(out_weight, "kv", kv, 1)
        pieces = {0: prepare(rank, keys[:, 0, :], values[:, 0, :], tables)}

        def fetch(offset):
            if offset not in pieces:
                low = offset % per_span
                step = low if low else offset & -offset
                pieces[offset] = swap(fetch(offset - step), "seq", seq, step)
            return pieces[offset]

        order = []
        step = per_span
        while step < seq:
            order.append(step)
            step *= 2
        for offset in order + list(range(1, min(per_span, seq))) + list(range(seq)):
            fetch(offset)
        calls = [[0, 1], [2, 3, 4]]
        while calls[-1][-1] < seq - 1:
            start = calls[-1][-1] + 1
            calls.append(list(range(start, min(start + per_span, seq))))
        state = None
        for offsets in calls[:-1]:
            state = attend(
                rank, offsets, by_head, [pieces[o] for o in offsets], tables, state, False
            )
        results = []
        for chunk in range(ROW_CHUNKS):
            offsets = calls[-1]
            own = attend(
                rank,
                offsets,
                by_head,
                [pieces[o] for o in offsets],
                tables,
                state,
                True,
                chunk,
                ROW_CHUNKS,
            )
            twin = swap(own, "kv", kv, 1)
            away = project(place, 2, own, twin, out_weight, twin_weight, jnp.bfloat16)
            landed = swap(away, "kv", kv, 2)
            home = project(place, 0, own, twin, out_weight, twin_weight, jnp.float32)
            results.append((home, landed))
        return jnp.concatenate(
            [(home + landed.astype(jnp.float32)).astype(jnp.bfloat16) for home, landed in results], 0
        )

    return shards


def solution(mesh):
    return jax.shard_map(
        make_shards(mesh.shape["seq"], mesh.shape["kv"]),
        mesh=mesh,
        in_specs=(P("seq", "kv", None), P("seq", "kv", None), P("seq", "kv", None), P("kv", None)),
        out_specs=P("seq", "kv"),
        check_vma=False,
    )
```

time: 160 us -> 58.1 us (0.36)
  the two profiles are of different devices: /device:TPU:26 before, /device:TPU:0 now
where the time goes in v1:
time: 58.1 us; the launch traced here: 57.7 us
  Pallas kernels  26.6 us (46%)
  starting transfers between devices  14.4 us (25%)
  local copies, waits for them, and re-layouts  8.03 us (14%)
  waiting for transfers between devices  7.62 us (13%)
  other arithmetic  0.91 us (2%)
    pallas_call x4, Pallas kernels, attend(): pl.pallas_call(kernel, grid_spec=pltpu.PrefetchScalarGridSpec(num_scalar_...  15.6 us
    ppermute x12, starting transfers between devices, swap(): return lax.ppermute(x, axis, [(i, i ^ bits) for i in range(size)])  14.4 us
    pallas_call x4, Pallas kernels, project(): pl.pallas_call(functools.partial(project_kernel, flip), grid_spec=pltpu.P...  9.24 us
    unnamed x16, local copies, waits for them, and re-layouts  8.03 us
    ppermute x12, waiting for transfers between devices, swap(): return lax.ppermute(x, axis, [(i, i ^ bits) for i in range(size)])  7.62 us
    pallas_call x1, Pallas kernels, prepare(): pl.pallas_call(prepare_kernel, grid_spec=pltpu.PrefetchScalarGridSpec(num...  1.78 us
  transfers between devices with their start and end apart: 12, of which 3 were waited for; matrix products, arithmetic and copies ran while one was open for 0% of the time, Pallas kernels for 46%

profile of v1, /device:TPU:0, one launch (start us, length us, event | category | flops | bytes accessed | tf_op | source)
XLA Modules:
  0.0 57.7 jit_solution(2393631634180486756)
XLA Ops:
  0.5 1.8 %rotate_keys.1.refs_4_ = bf16[512,128]{1,0:T(8,128)(2,1)} custom-call(s32[1]{0:T(128)} %bitcast.1.rank.refs_0_, bf16[256,128]{1,0:T(8,128)(2,1)} %bitcast.11, bf16[256,128]{1,0:T(8,128)(2,1)} %bitcast.12, f32[1536,128]{1,0:T(8,128)} %constant.13.clone.cos_ref.refs_2_.refs_4_, f32[1536,128]{1,0:T(8,128)} %constant.14.clone.sin_ref.refs_3_.refs_5_), custom_call_target="tpu_custom_call" | custom-call | tf_op jit(solution)/shard_map/rotate_keys/pallas_call | solution.py:52
  2.2 3.6 %collective-permute-start = (bf16[512,128]{1,0:T(8,128)(2,1)}, bf16[512,128]{1,0:T(8,128)(2,1)S(1)}, u32[]{:S(2)}, u32[]{:S(2)}) collective-permute-start(bf16[512,128]{1,0:T(8,128)(2,1)} %rotate_keys.1.refs_4_), channel_id=1, source_target_pairs={{0,16},{4,20},{8,24},{12,28},{16,0},{20,4},{24,8},{28,12},{1,17},{... | collective-permute-start | bytes 393224 | tf_op jit(solution)/shard_map/ppermute | solution.py:222
  5.8 1.5 %collective-permute-start.6 = (bf16[512,128]{1,0:T(8,128)(2,1)}, bf16[512,128]{1,0:T(8,128)(2,1)S(1)}, u32[]{:S(2)}, u32[]{:S(2)}) collective-permute-start(bf16[512,128]{1,0:T(8,128)(2,1)} %rotate_keys.1.refs_4_), channel_id=1, source_target_pairs={{0,4},{4,0},{8,12},{12,8},{16,20},{20,16},{24,28},{28,24},{1,5},{5... | collective-permute-start | bytes 393224 | tf_op jit(solution)/shard_map/ppermute | solution.py:222
  7.3 1.5 %collective-permute-start.5 = (bf16[512,128]{1,0:T(8,128)(2,1)}, bf16[512,128]{1,0:T(8,128)(2,1)S(1)}, u32[]{:S(2)}, u32[]{:S(2)}) collective-permute-start(bf16[512,128]{1,0:T(8,128)(2,1)} %rotate_keys.1.refs_4_), channel_id=1, source_target_pairs={{0,12},{4,8},{8,4},{12,0},{16,28},{20,24},{24,20},{28,16},{1,13},{... | collective-permute-start | bytes 393224 | tf_op jit(solution)/shard_map/ppermute | solution.py:222
  9.3 3.7 %collective-permute-done.refs_8_ = bf16[512,128]{1,0:T(8,128)(2,1)S(1)} collective-permute-done((bf16[512,128]{1,0:T(8,128)(2,1)}, bf16[512,128]{1,0:T(8,128)(2,1)S(1)}, u32[]{:S(2)}, u32[]{:S(2)}) %collective-permute-start) | collective-permute-done | bytes 131104 | tf_op jit(solution)/shard_map/ppermute | solution.py:222
  13.0 1.8 %collective-permute-start.3 = (bf16[512,128]{1,0:T(8,128)(2,1)S(1)}, bf16[512,128]{1,0:T(8,128)(2,1)S(1)}, u32[]{:S(2)}, u32[]{:S(2)}) collective-permute-start(bf16[512,128]{1,0:T(8,128)(2,1)S(1)} %collective-permute-done.refs_8_), channel_id=1, source_target_pairs={{0,12},{4,8},{8,4},{12,0},{16,28},{20,24},{24,20},{28,16},{1,13},{... | collective-permute-start | bytes 393224 | tf_op jit(solution)/shard_map/ppermute | solution.py:222
  14.8 1.2 %collective-permute-start.2 = (bf16[512,128]{1,0:T(8,128)(2,1)S(1)}, bf16[512,128]{1,0:T(8,128)(2,1)S(1)}, u32[]{:S(2)}, u32[]{:S(2)}) collective-permute-start(bf16[512,128]{1,0:T(8,128)(2,1)S(1)} %collective-permute-done.refs_8_), channel_id=1, source_target_pairs={{0,8},{4,12},{8,0},{12,4},{16,24},{20,28},{24,16},{28,20},{1,9},{5... | collective-permute-start | bytes 393224 | tf_op jit(solution)/shard_map/ppermute | solution.py:222
  16.5 1.1 %collective-permute-start.1 = (bf16[512,128]{1,0:T(8,128)(2,1)S(1)}, bf16[512,128]{1,0:T(8,128)(2,1)S(1)}, u32[]{:S(2)}, u32[]{:S(2)}) collective-permute-start(bf16[512,128]{1,0:T(8,128)(2,1)S(1)} %collective-permute-done.refs_8_), channel_id=1, source_target_pairs={{0,4},{4,0},{8,12},{12,8},{16,20},{20,16},{24,28},{28,24},{1,5},{5... | collective-permute-start | bytes 393224 | tf_op jit(solution)/shard_map/ppermute | solution.py:222
  17.6 1.1 %copy-done.1 = f32[1536,128]{1,0:T(8,128)S(1)} copy-done((f32[1536,128]{1,0:T(8,128)S(1)}, f32[1536,128]{1,0:T(8,128)}, u32[]{:S(2)}) %copy-start.1) | copy-done | bytes 786456
  18.7 1.1 %copy-done.2 = f32[1536,128]{1,0:T(8,128)S(1)} copy-done((f32[1536,128]{1,0:T(8,128)S(1)}, f32[1536,128]{1,0:T(8,128)}, u32[]{:S(2)}) %copy-start.2) | copy-done | bytes 786456
  19.8 1.0 %copy-done.3 = bf16[256,7,128]{2,0,1:T(8,128)(2,1)S(1)} copy-done((bf16[256,7,128]{2,0,1:T(8,128)(2,1)S(1)}, bf16[256,7,128]{2,0,1:T(8,128)(2,1)}, u32[]{:S(2)}) %copy-start.3) | copy-done | bytes 458776
  20.9 0.9 %copy-done.5 = bf16[512,128]{1,0:T(8,128)(2,1)S(1)} copy-done((bf16[512,128]{1,0:T(8,128)(2,1)S(1)}, bf16[512,128]{1,0:T(8,128)(2,1)}, u32[]{:S(2)}) %copy-start.5) | copy-done | bytes 131096
  21.8 2.3 %attend_0_1.1 = (f32[7,256,128]{2,1,0:T(8,128)S(1)}, f32[256,128]{1,0:T(8,128)S(1)}) custom-call(s32[1]{0:T(128)} %bitcast.1.rank.refs_0_, bf16[7,256,128]{2,1,0:T(8,128)(2,1)S(1)} %bitcast.7, f32[1536,128]{1,0:T(8,128)S(1)} %copy-done.2, f32[1536,128]{1,0:T(8,128)S(1)} %copy-done.1, bf16[512,128]{1,0:T(8,128)(2,1)S(1)} %copy-done.5, ...), custom_call_target="tpu_custom_call" | custom-call | flops 469762048 | bytes 2097152 | tf_op jit(solution)/shard_map/attend_0_1/pallas_call | solution.py:177
  24.1 1.0 %copy-done.4 = bf16[256,7,128]{2,0,1:T(8,128)(2,1)S(1)} copy-done((bf16[256,7,128]{2,0,1:T(8,128)(2,1)S(1)}, bf16[256,7,128]{2,0,1:T(8,128)(2,1)}, u32[]{:S(2)}) %copy-start.4) | copy-done | bytes 458776
  25.1 6.9 %attend_2_3_4.1 = (f32[7,256,128]{2,1,0:T(8,128)S(1)}, f32[256,128]{1,0:T(8,128)S(1)}) custom-call(s32[1]{0:T(128)} %bitcast.1.rank.refs_0_, bf16[7,256,128]{2,1,0:T(8,128)(2,1)S(1)} %bitcast.8, f32[1536,128]{1,0:T(8,128)S(1)} %copy-done.2, f32[1536,128]{1,0:T(8,128)S(1)} %copy-done.1, f32[1536,128]{1,0:T(8,128)S(1)} %copy-done.2, ...), custom_call_target="tpu_custom_call" | custom-call | flops 704643072 | bytes 2097152 | tf_op jit(solution)/shard_map/attend_2_3_4/pallas_call | solution.py:177
  32.0 3.1 %attend_5_6_7.2.own_ref = bf16[128,896]{1,0:T(8,128)(2,1)S(1)} custom-call(s32[1]{0:T(128)} %bitcast.1.rank.refs_0_, bf16[7,256,128]{2,1,0:T(8,128)(2,1)S(1)} %bitcast.9, f32[1536,128]{1,0:T(8,128)S(1)} %copy-done.2, f32[1536,128]{1,0:T(8,128)S(1)} %copy-done.1, bf16[512,128]{1,0:T(8,128)(2,1)S(1)} %collective-permute-done.1.refs_4_, ...), custom_call_target="tpu_custom_call" | custom-call | flops 352321536 | bytes 2097152 | tf_op jit(solution)/shard_map/attend_5_6_7/pallas_call | solution.py:177
  35.2 3.3 %attend_5_6_7.3.own_ref = bf16[128,896]{1,0:T(8,128)(2,1)S(1)} custom-call(s32[1]{0:T(128)} %bitcast.1.rank.refs_0_, bf16[7,256,128]{2,1,0:T(8,128)(2,1)S(1)} %bitcast.10, f32[1536,128]{1,0:T(8,128)S(1)} %copy-done.2, f32[1536,128]{1,0:T(8,128)S(1)} %copy-done.1, bf16[512,128]{1,0:T(8,128)(2,1)S(1)} %collective-permute-done.1.refs_4_, ...), custom_call_target="tpu_custom_call" | custom-call | flops 352321536 | bytes 2097152 | tf_op jit(solution)/shard_map/attend_5_6_7/pallas_call | solution.py:177
  39.1 2.8 %copy-done = bf16[896,3584]{1,0:T(8,128)(2,1)S(1)} copy-done((bf16[896,3584]{1,0:T(8,128)(2,1)S(1)}, bf16[896,3584]{1,0:T(8,128)(2,1)}, u32[]{:S(2)}) %copy-start) | copy-done | bytes 6422552
  41.9 2.4 %project_2.2 = bf16[128,896]{1,0:T(8,128)(2,1)S(1)} custom-call(s32[1]{0:T(128)} %bitcast.place, bf16[128,896]{1,0:T(8,128)(2,1)S(1)} %attend_5_6_7.2.own_ref, bf16[128,896]{1,0:T(8,128)(2,1)S(1)} %collective-permute-done.7.twin_ref, bf16[896,3584]{1,0:T(8,128)(2,1)S(1)} %copy-done, bf16[896,3584]{1,0:T(8,128)(2,1)} %collective-permute-done.8.twin_weight), custom_call_target="tpu_custom_call" | custom-call | flops 411041792 | bytes 3211264 | tf_op jit(solution)/shard_map/project_2/pallas_call | solution.py:204
  44.3 1.6 %collective-permute-start.9 = (bf16[128,896]{1,0:T(8,128)(2,1)S(1)}, bf16[128,896]{1,0:T(8,128)(2,1)S(1)}, u32[]{:S(2)}, u32[]{:S(2)}) collective-permute-start(bf16[128,896]{1,0:T(8,128)(2,1)S(1)} %project_2.2), channel_id=1, source_target_pairs={{0,2},{1,3},{2,0},{3,1},{4,6},{5,7},{6,4},{7,5},{8,10},{9,11},{10,... | collective-permute-start | bytes 688136 | tf_op jit(solution)/shard_map/ppermute | solution.py:222
  45.9 2.3 %project_2.3 = bf16[128,896]{1,0:T(8,128)(2,1)S(1)} custom-call(s32[1]{0:T(128)} %bitcast.place, bf16[128,896]{1,0:T(8,128)(2,1)S(1)} %attend_5_6_7.3.own_ref, bf16[128,896]{1,0:T(8,128)(2,1)S(1)} %collective-permute-done.10.twin_ref, bf16[896,3584]{1,0:T(8,128)(2,1)S(1)} %bitcast.6, bf16[896,3584]{1,0:T(8,128)(2,1)} %collective-permute-done.8.twin_weight), custom_call_target="tpu_custom_call" | custom-call | flops 411041792 | bytes 3211264 | tf_op jit(solution)/shard_map/project_2/pallas_call | solution.py:204
  48.8 2.3 %project_0.3 = f32[128,896]{1,0:T(8,128)S(1)} custom-call(s32[1]{0:T(128)} %bitcast.place, bf16[128,896]{1,0:T(8,128)(2,1)S(1)} %attend_5_6_7.3.own_ref, bf16[128,896]{1,0:T(8,128)(2,1)S(1)} %collective-permute-done.10.twin_ref, bf16[896,3584]{1,0:T(8,128)(2,1)S(1)} %bitcast.6, bf16[896,3584]{1,0:T(8,128)(2,1)} %collective-permute-done.8.twin_weight), custom_call_target="tpu_custom_call" | custom-call | flops 411041792 | bytes 3211264 | tf_op jit(solution)/shard_map/project_0/pallas_call | solution.py:204
  51.0 2.3 %project_0.2 = f32[128,896]{1,0:T(8,128)S(1)} custom-call(s32[1]{0:T(128)} %bitcast.place, bf16[128,896]{1,0:T(8,128)(2,1)S(1)} %attend_5_6_7.2.own_ref, bf16[128,896]{1,0:T(8,128)(2,1)S(1)} %collective-permute-done.7.twin_ref, bf16[896,3584]{1,0:T(8,128)(2,1)S(1)} %bitcast.6, bf16[896,3584]{1,0:T(8,128)(2,1)} %collective-permute-done.8.twin_weight), custom_call_target="tpu_custom_call" | custom-call | flops 411041792 | bytes 3211264 | tf_op jit(solution)/shard_map/project_0/pallas_call | solution.py:204
  53.4 3.4 %collective-permute-done.11 = bf16[128,896]{1,0:T(8,128)(2,1)S(1)} collective-permute-done((bf16[128,896]{1,0:T(8,128)(2,1)S(1)}, bf16[128,896]{1,0:T(8,128)(2,1)S(1)}, u32[]{:S(2)}, u32[]{:S(2)}) %collective-permute-start.11) | collective-permute-done | bytes 229408 | tf_op jit(solution)/shard_map/ppermute | solution.py:222
  (29 shorter events, 3.5 us)
Async XLA Ops:
  0.0 39.1 %collective-permute-start.8 = (bf16[896,3584]{1,0:T(8,128)(2,1)}, bf16[896,3584]{1,0:T(8,128)(2,1)}, u32[]{:S(2)}, u32[]{:S(2)}) collective-permute-start(bf16[896,3584]{1,0:T(8,128)(2,1)} %own_weight.7), channel_id=1, source_target_pairs={{0,1},{1,0},{2,3},{3,2},{4,5},{5,4},{6,7},{7,6},{8,9},{9,8},{10,11... | collective-permute-start | bytes 19267592 | tf_op jit(solution)/shard_map/ppermute | solution.py:222
  2.2 10.8 %collective-permute-start = (bf16[512,128]{1,0:T(8,128)(2,1)}, bf16[512,128]{1,0:T(8,128)(2,1)S(1)}, u32[]{:S(2)}, u32[]{:S(2)}) collective-permute-start(bf16[512,128]{1,0:T(8,128)(2,1)} %rotate_keys.1.refs_4_), channel_id=1, source_target_pairs={{0,16},{4,20},{8,24},{12,28},{16,0},{20,4},{24,8},{28,12},{1,17},{... | collective-permute-start | bytes 393224 | tf_op jit(solution)/shard_map/ppermute | solution.py:222
  5.8 9.0 %collective-permute-start.6 = (bf16[512,128]{1,0:T(8,128)(2,1)}, bf16[512,128]{1,0:T(8,128)(2,1)S(1)}, u32[]{:S(2)}, u32[]{:S(2)}) collective-permute-start(bf16[512,128]{1,0:T(8,128)(2,1)} %rotate_keys.1.refs_4_), channel_id=1, source_target_pairs={{0,4},{4,0},{8,12},{12,8},{16,20},{20,16},{24,28},{28,24},{1,5},{5... | collective-permute-start | bytes 393224 | tf_op jit(solution)/shard_map/ppermute | solution.py:222
  7.3 9.2 %collective-permute-start.5 = (bf16[512,128]{1,0:T(8,128)(2,1)}, bf16[512,128]{1,0:T(8,128)(2,1)S(1)}, u32[]{:S(2)}, u32[]{:S(2)}) collective-permute-start(bf16[512,128]{1,0:T(8,128)(2,1)} %rotate_keys.1.refs_4_), channel_id=1, source_target_pairs={{0,12},{4,8},{8,4},{12,0},{16,28},{20,24},{24,20},{28,16},{1,13},{... | collective-permute-start | bytes 393224 | tf_op jit(solution)/shard_map/ppermute | solution.py:222
  8.9 15.2 %collective-permute-start.4 = (bf16[512,128]{1,0:T(8,128)(2,1)}, bf16[512,128]{1,0:T(8,128)(2,1)S(1)}, u32[]{:S(2)}, u32[]{:S(2)}) collective-permute-start(bf16[512,128]{1,0:T(8,128)(2,1)} %rotate_keys.1.refs_4_), channel_id=1, source_target_pairs={{0,8},{4,12},{8,0},{12,4},{16,24},{20,28},{24,16},{28,20},{1,9},{5... | collective-permute-start | bytes 393224 | tf_op jit(solution)/shard_map/ppermute | solution.py:222
  13.0 19.0 %collective-permute-start.3 = (bf16[512,128]{1,0:T(8,128)(2,1)S(1)}, bf16[512,128]{1,0:T(8,128)(2,1)S(1)}, u32[]{:S(2)}, u32[]{:S(2)}) collective-permute-start(bf16[512,128]{1,0:T(8,128)(2,1)S(1)} %collective-permute-done.refs_8_), channel_id=1, source_target_pairs={{0,12},{4,8},{8,4},{12,0},{16,28},{20,24},{24,20},{28,16},{1,13},{... | collective-permute-start | bytes 393224 | tf_op jit(solution)/shard_map/ppermute | solution.py:222
  14.8 17.1 %collective-permute-start.2 = (bf16[512,128]{1,0:T(8,128)(2,1)S(1)}, bf16[512,128]{1,0:T(8,128)(2,1)S(1)}, u32[]{:S(2)}, u32[]{:S(2)}) collective-permute-start(bf16[512,128]{1,0:T(8,128)(2,1)S(1)} %collective-permute-done.refs_8_), channel_id=1, source_target_pairs={{0,8},{4,12},{8,0},{12,4},{16,24},{20,28},{24,16},{28,20},{1,9},{5... | collective-permute-start | bytes 393224 | tf_op jit(solution)/shard_map/ppermute | solution.py:222
  16.5 15.5 %collective-permute-start.1 = (bf16[512,128]{1,0:T(8,128)(2,1)S(1)}, bf16[512,128]{1,0:T(8,128)(2,1)S(1)}, u32[]{:S(2)}, u32[]{:S(2)}) collective-permute-start(bf16[512,128]{1,0:T(8,128)(2,1)S(1)} %collective-permute-done.refs_8_), channel_id=1, source_target_pairs={{0,4},{4,0},{8,12},{12,8},{16,20},{20,16},{24,28},{28,24},{1,5},{5... | collective-permute-start | bytes 393224 | tf_op jit(solution)/shard_map/ppermute | solution.py:222
  17.6 1.1 %copy-start.1 = (f32[1536,128]{1,0:T(8,128)S(1)}, f32[1536,128]{1,0:T(8,128)}, u32[]{:S(2)}) copy-start(f32[1536,128]{1,0:T(8,128)} %constant.14.clone.sin_ref.refs_3_.refs_5_) | copy-start | bytes 2359300
  18.7 1.1 %copy-start.2 = (f32[1536,128]{1,0:T(8,128)S(1)}, f32[1536,128]{1,0:T(8,128)}, u32[]{:S(2)}) copy-start(f32[1536,128]{1,0:T(8,128)} %constant.13.clone.cos_ref.refs_2_.refs_4_) | copy-start | bytes 2359300
  19.8 1.0 %copy-start.3 = (bf16[256,7,128]{2,0,1:T(8,128)(2,1)S(1)}, bf16[256,7,128]{2,0,1:T(8,128)(2,1)}, u32[]{:S(2)}) copy-start(bf16[256,7,128]{2,0,1:T(8,128)(2,1)} %param.6) | copy-start | bytes 1376260
  20.9 0.9 %copy-start.5 = (bf16[512,128]{1,0:T(8,128)(2,1)S(1)}, bf16[512,128]{1,0:T(8,128)(2,1)}, u32[]{:S(2)}) copy-start(bf16[512,128]{1,0:T(8,128)(2,1)} %rotate_keys.1.refs_4_) | copy-start | bytes 393220
  24.1 1.0 %copy-start.4 = (bf16[256,7,128]{2,0,1:T(8,128)(2,1)S(1)}, bf16[256,7,128]{2,0,1:T(8,128)(2,1)}, u32[]{:S(2)}) copy-start(bf16[256,7,128]{2,0,1:T(8,128)(2,1)} %param.6) | copy-start | bytes 1376260
  32.0 13.9 %slice-start = ((s8[6422528]{0:T(1024)(128)(4,1)}), s8[2228224]{0:T(1024)(128)(4,1)S(1)}, s32[]{:S(2)}) async-start(s8[6422528]{0:T(1024)(128)(4,1)} %bitcast.5), calls=%async_computation | async-start | bytes 4456448
  35.1 3.9 %collective-permute-start.7 = (bf16[128,896]{1,0:T(8,128)(2,1)S(1)}, bf16[128,896]{1,0:T(8,128)(2,1)S(1)}, u32[]{:S(2)}, u32[]{:S(2)}) collective-permute-start(bf16[128,896]{1,0:T(8,128)(2,1)S(1)} %attend_5_6_7.2.own_ref), channel_id=1, source_target_pairs={{0,1},{1,0},{2,3},{3,2},{4,5},{5,4},{6,7},{7,6},{8,9},{9,8},{10,11... | collective-permute-start | bytes 688136 | tf_op jit(solution)/shard_map/ppermute | solution.py:222
  38.5 7.4 %collective-permute-start.10 = (bf16[128,896]{1,0:T(8,128)(2,1)S(1)}, bf16[128,896]{1,0:T(8,128)(2,1)S(1)}, u32[]{:S(2)}, u32[]{:S(2)}) collective-permute-start(bf16[128,896]{1,0:T(8,128)(2,1)S(1)} %attend_5_6_7.3.own_ref), channel_id=1, source_target_pairs={{0,1},{1,0},{2,3},{3,2},{4,5},{5,4},{6,7},{7,6},{8,9},{9,8},{10,11... | collective-permute-start | bytes 688136 | tf_op jit(solution)/shard_map/ppermute | solution.py:222
  39.1 2.8 %copy-start = (bf16[896,3584]{1,0:T(8,128)(2,1)S(1)}, bf16[896,3584]{1,0:T(8,128)(2,1)}, u32[]{:S(2)}) copy-start(bf16[896,3584]{1,0:T(8,128)(2,1)} %own_weight.7) | copy-start | bytes 19267588
  41.9 4.0 %slice-start.1 = ((s8[6422528]{0:T(1024)(128)(4,1)}), s8[4194304]{0:T(1024)(128)(4,1)S(1)}, s32[]{:S(2)}) async-start(s8[6422528]{0:T(1024)(128)(4,1)} %bitcast.5), calls=%async_computation.1 | async-start | bytes 8388608
  44.3 9.0 %collective-permute-start.9 = (bf16[128,896]{1,0:T(8,128)(2,1)S(1)}, bf16[128,896]{1,0:T(8,128)(2,1)S(1)}, u32[]{:S(2)}, u32[]{:S(2)}) collective-permute-start(bf16[128,896]{1,0:T(8,128)(2,1)S(1)} %project_2.2), channel_id=1, source_target_pairs={{0,2},{1,3},{2,0},{3,1},{4,6},{5,7},{6,4},{7,5},{8,10},{9,11},{10,... | collective-permute-start | bytes 688136 | tf_op jit(solution)/shard_map/ppermute | solution.py:222
  48.2 8.7 %collective-permute-start.11 = (bf16[128,896]{1,0:T(8,128)(2,1)S(1)}, bf16[128,896]{1,0:T(8,128)(2,1)S(1)}, u32[]{:S(2)}, u32[]{:S(2)}) collective-permute-start(bf16[128,896]{1,0:T(8,128)(2,1)S(1)} %project_2.3), channel_id=1, source_target_pairs={{0,2},{1,3},{2,0},{3,1},{4,6},{5,7},{6,4},{7,5},{8,10},{9,11},{10,... | collective-permute-start | bytes 688136 | tf_op jit(solution)/shard_map/ppermute | solution.py:222

commit v2 on v1

v2 whole, which is shorter than its diff:
```python
import functools
import math

import jax
import jax.numpy as jnp
import numpy as np
from jax import lax
from jax.experimental import pallas as pl
from jax.experimental.pallas import tpu as pltpu
from jax.sharding import PartitionSpec as P

HEAD = 128
GROUP = 7
SPAN = 1024
LOCAL = 32
THETA = 10000000.0
NEG = -1e30
SCALE = math.log2(math.e) / math.sqrt(HEAD)
ROW_CHUNKS = 2
VMEM = pltpu.MemorySpace.VMEM
HBM = pltpu.MemorySpace.HBM
LIMIT = 24 * 2**20


def rope_tables(block):
    inverse = np.exp(np.arange(HEAD // 2, dtype=np.float64) * (-2.0 * math.log(THETA) / HEAD))
    inner = np.arange(SPAN)
    first = np.minimum(np.arange(block) + SPAN, SPAN + LOCAL)
    far = np.full((block,), SPAN + LOCAL)
    angles = np.concatenate([inner, first, far])[:, None] * inverse
    cosine, sine = np.cos(angles), np.sin(angles)
    return (
        jnp.asarray(np.concatenate([cosine, cosine], 1), jnp.float32),
        jnp.asarray(np.concatenate([-sine, sine], 1), jnp.float32),
    )


def rotated(x, cosine, sine):
    x = x.astype(jnp.float32)
    return x * cosine + pltpu.roll(x, HEAD // 2, 1) * sine


def in_hbm(x):
    return pltpu.with_memory_space_constraint(x, HBM)


def prepare_kernel(rank_ref, key_hbm, value_hbm, cos_hbm, sin_hbm, out_ref, key_ref, cos_ref, sin_ref, sems):
    block = key_ref.shape[0]
    rows = pl.ds(pl.multiple_of(rank_ref[0] % (SPAN // block) * block, block), block)
    copies = [
        pltpu.make_async_copy(key_hbm, key_ref, sems.at[0]),
        pltpu.make_async_copy(cos_hbm.at[rows], cos_ref, sems.at[1]),
        pltpu.make_async_copy(sin_hbm.at[rows], sin_ref, sems.at[2]),
        pltpu.make_async_copy(value_hbm, out_ref.at[pl.ds(block, block)], sems.at[3]),
    ]
    for copy in copies:
        copy.start()
    for copy in copies:
        copy.wait()
    out_ref[:block] = rotated(key_ref[...], cos_ref[...], sin_ref[...]).astype(jnp.bfloat16)


def prepare(rank, keys, values, tables):
    block = keys.shape[0]
    return pl.pallas_call(
        prepare_kernel,
        in_specs=[pl.BlockSpec(memory_space=pltpu.SMEM)] + [pl.BlockSpec(memory_space=HBM)] * 4,
        out_specs=pl.BlockSpec(memory_space=VMEM),
        out_shape=jax.ShapeDtypeStruct((2 * block, HEAD), jnp.bfloat16),
        scratch_shapes=[
            pltpu.VMEM((block, HEAD), jnp.bfloat16),
            pltpu.VMEM((block, HEAD), jnp.float32),
            pltpu.VMEM((block, HEAD), jnp.float32),
            pltpu.SemaphoreType.DMA((4,)),
        ],
        compiler_params=pltpu.CompilerParams(vmem_limit_bytes=LIMIT),
        name="rotate_keys",
    )(rank, *[in_hbm(x) for x in (keys, values, *tables)])


def scores_of(query, pieces):
    block = pieces[0].shape[0] // 2
    return [
        lax.dot_general(
            q, piece[:block], (((1,), (1,)), ((), ())), preferred_element_type=jnp.float32
        )
        for q, piece in zip(query, pieces)
    ]


def absorb(scores, lifts, pieces, old):
    block = pieces[0].shape[0] // 2
    lanes = [slice(at, at + HEAD) for at in range(0, block, HEAD)]
    peak = None
    for score, lift in zip(scores, lifts):
        high = functools.reduce(jnp.maximum, [score[:, lane] for lane in lanes])
        if lift is not None:
            high = high - lift
        peak = high if peak is None else jnp.maximum(peak, high)
    top = jnp.max(peak, axis=1, keepdims=True)
    if old is None:
        top = jnp.broadcast_to(top, peak.shape)
        acc, total = None, None
    else:
        top = jnp.maximum(top, old[0])
        factor = jnp.exp2(old[0] - top)
        acc, total = factor * old[1], factor * old[2]
    ones = jnp.ones((block, HEAD), jnp.bfloat16)
    for score, lift, piece in zip(scores, lifts, pieces):
        base = top if lift is None else top + lift
        weight = jnp.exp2(score - jnp.concatenate([base] * len(lanes), 1)).astype(jnp.bfloat16)
        both = jnp.dot(
            weight, jnp.concatenate([piece[block:], ones], 1), preferred_element_type=jnp.float32
        )
        acc = both[:, :HEAD] if acc is None else acc + both[:, :HEAD]
        total = both[:, HEAD:] if total is None else total + both[:, HEAD:]
    return top, acc, total


def begin_kernel(
    kinds, rank_ref, place_ref, query_hbm, cos_hbm, sin_hbm, weight_hbm, piece_ref,
    rot_ref, top_ref, acc_ref, total_ref, mine_ref, query_ref, cos_ref, sin_ref, sems, weight_sems,
):
    heads, block, _ = query_ref.shape
    per_span = SPAN // block
    rank, place = rank_ref[0], place_ref[0]
    inner = rank % per_span
    places = [inner, jnp.where(inner == 0, per_span, per_span + 1), per_span + 1][:kinds]
    copies = [pltpu.make_async_copy(query_hbm, query_ref, sems.at[0])]
    for kind, at in enumerate(places):
        rows = pl.ds(pl.multiple_of(at * block, block), block)
        copies.append(pltpu.make_async_copy(cos_hbm.at[rows], cos_ref.at[kind], sems.at[1 + 2 * kind]))
        copies.append(pltpu.make_async_copy(sin_hbm.at[rows], sin_ref.at[kind], sems.at[2 + 2 * kind]))
    for copy in copies:
        copy.start()
    loads = column_copies(place, weight_hbm, mine_ref, weight_sems)
    for copy in loads:
        copy.start()
    for copy in copies:
        copy.wait()
    causal = lax.broadcasted_iota(jnp.int32, (block, block), 1) <= lax.broadcasted_iota(
        jnp.int32, (block, block), 0
    )
    for head in range(heads):
        for kind in range(kinds):
            rot_ref[kind, head] = (
                rotated(query_ref[head], cos_ref[kind], sin_ref[kind]) * SCALE
            ).astype(jnp.bfloat16)
    later = scores_of([rot_ref[0, 0]], [piece_ref])
    for head in range(heads):
        now = later
        if head + 1 < heads:
            later = scores_of([rot_ref[0, head + 1]], [piece_ref])
        now = [jnp.where(causal, now[0], NEG)]
        top_ref[head], acc_ref[head], total_ref[head] = absorb(now, [None], [piece_ref], None)
    for copy in loads:
        copy.wait()


def begin(kinds, rank, place, queries, tables, out_weight, piece):
    heads, block, _ = queries.shape
    depth = out_weight.shape[0]
    smem, hbm, vmem = (pl.BlockSpec(memory_space=space) for space in (pltpu.SMEM, HBM, VMEM))
    halves = jax.ShapeDtypeStruct((2, depth, depth), jnp.bfloat16)
    return pl.pallas_call(
        functools.partial(begin_kernel, kinds),
        in_specs=[smem, smem, hbm, hbm, hbm, hbm, vmem],
        out_specs=[vmem] * 5,
        out_shape=[
            jax.ShapeDtypeStruct((kinds, heads, block, HEAD), jnp.bfloat16),
            *[jax.ShapeDtypeStruct((heads, block, HEAD), jnp.float32)] * 3,
            halves,
        ],
        scratch_shapes=[
            pltpu.VMEM((heads, block, HEAD), jnp.bfloat16),
            pltpu.VMEM((kinds, block, HEAD), jnp.float32),
            pltpu.VMEM((kinds, block, HEAD), jnp.float32),
            pltpu.SemaphoreType.DMA((1 + 2 * kinds,)),
            pltpu.SemaphoreType.DMA((2,)),
        ],
        cost_estimate=pl.CostEstimate(flops=2 * 10**9, bytes_accessed=2**23, transcendentals=10**6),
        compiler_params=pltpu.CompilerParams(vmem_limit_bytes=LIMIT),
        name="attend_0",
    )(rank, place, *[in_hbm(x) for x in (queries, *tables, out_weight)], piece)


def column_copies(place, weight_hbm, into, sems):
    columns = into.shape[2]
    copies = []
    for flip in range(2):
        at = pl.ds(pl.multiple_of((place ^ (2 * flip)) * columns, columns), columns)
        copies.append(pltpu.make_async_copy(weight_hbm.at[:, at], into.at[flip], sems.at[flip]))
    return copies


def attend_kernel(offsets, kinds, last, start, rows, stages, rank_ref, rot_ref, *refs):
    pieces, refs = refs[: len(offsets)], refs[len(offsets) :]
    old, refs = refs[:3], refs[3:]
    loads = []
    if stages:
        place_ref, weight_hbm, *refs, staged_ref, sems = refs
        loads = column_copies(place_ref[0], weight_hbm, staged_ref, sems)
    for copy in loads:
        copy.start()
    block = pieces[0].shape[0] // 2
    per_span = SPAN // block
    rank = rank_ref[0]
    lifts = [jnp.where((rank ^ offset) <= rank, 0.0, -NEG).astype(jnp.float32) for offset in offsets]
    picked = []
    for offset in offsets:
        kind = min(offset // per_span, 1)
        if kind and kinds > 2:
            back = rank // per_span - (rank ^ offset) // per_span
            kind = jnp.clip(back, 1, kinds - 1)
        picked.append(kind)
    here = slice(start, start + rows)
    def scores_at(head):
        return scores_of([rot_ref[kind, head, here] for kind in picked], pieces)

    later = scores_at(0)
    for head in range(GROUP):
        now = later
        if head + 1 < GROUP:
            later = scores_at(head + 1)
        top, acc, total = absorb(now, lifts, pieces, [ref[head, here] for ref in old])
        if last:
            (out_ref,) = refs
            out_ref[:, head * HEAD : (head + 1) * HEAD] = (acc / total).astype(jnp.bfloat16)
        else:
            refs[0][head], refs[1][head], refs[2][head] = top, acc, total
    for copy in loads:
        copy.wait()


def attend(rank, offsets, rot, pieces, state, last, start, rows, stage=()):
    block = pieces[0].shape[0] // 2
    smem, vmem = (pl.BlockSpec(memory_space=space) for space in (pltpu.SMEM, VMEM))
    if last:
        out_specs = vmem
        out_shape = jax.ShapeDtypeStruct((rows, GROUP * HEAD), jnp.bfloat16)
    else:
        out_specs = [vmem] * 3
        out_shape = [jax.ShapeDtypeStruct((GROUP, rows, HEAD), jnp.float32)] * 3
    args, in_specs, scratch = [], [], []
    if stage:
        place, weight = stage
        depth = weight.shape[0]
        args = [place, in_hbm(weight)]
        in_specs = [smem, pl.BlockSpec(memory_space=HBM)]
        out_specs = [*out_specs, vmem]
        out_shape = [*out_shape, jax.ShapeDtypeStruct((2, depth, depth), jnp.bfloat16)]
        scratch = [pltpu.SemaphoreType.DMA((2,))]
    pairs = GROUP * rows * block * len(pieces)
    return pl.pallas_call(
        functools.partial(
            attend_kernel, tuple(offsets), rot.shape[0], last, start, rows, bool(stage)
        ),
        in_specs=[smem] + [vmem] * (4 + len(pieces)) + in_specs,
        scratch_shapes=scratch,
        out_specs=out_specs,
        out_shape=out_shape,
        cost_estimate=pl.CostEstimate(
            flops=8 * HEAD * pairs, bytes_accessed=2**21, transcendentals=pairs
        ),
        compiler_params=pltpu.CompilerParams(vmem_limit_bytes=LIMIT),
        name="attend_" + "_".join(map(str, offsets)),
    )(rank, rot, *pieces, *state, *args)


def project_kernel(flip, own_ref, twin_ref, own_weight, twin_weight, out_ref):
    out_ref[...] = (
        jnp.dot(own_ref[...], own_weight[flip], preferred_element_type=jnp.float32)
        + jnp.dot(twin_ref[...], twin_weight[flip], preferred_element_type=jnp.float32)
    ).astype(out_ref.dtype)


def project(flip, own, twin, own_weight, twin_weight, dtype):
    rows, depth = own.shape
    columns = own_weight.shape[2]
    vmem = pl.BlockSpec(memory_space=VMEM)
    return pl.pallas_call(
        functools.partial(project_kernel, flip),
        in_specs=[vmem] * 4,
        out_specs=vmem,
        out_shape=jax.ShapeDtypeStruct((rows, columns), dtype),
        cost_estimate=pl.CostEstimate(
            flops=4 * rows * depth * columns, bytes_accessed=2 * depth * columns, transcendentals=0
        ),
        compiler_params=pltpu.CompilerParams(vmem_limit_bytes=LIMIT),
        name="project_away" if flip else "project_home",
    )(own, twin, own_weight, twin_weight)


def close_kernel(starts, *refs):
    out_ref = refs[-1]
    for at, start in enumerate(starts):
        home, landed = refs[2 * at], refs[2 * at + 1]
        out_ref[start : start + home.shape[0]] = (
            home[...] + landed[...].astype(jnp.float32)
        ).astype(out_ref.dtype)


def close(parts):
    starts, rows = [], 0
    for home, _ in parts:
        starts.append(rows)
        rows += home.shape[0]
    vmem = pl.BlockSpec(memory_space=VMEM)
    return pl.pallas_call(
        functools.partial(close_kernel, tuple(starts)),
        in_specs=[vmem] * (2 * len(parts)),
        out_specs=vmem,
        out_shape=jax.ShapeDtypeStruct((rows, parts[0][0].shape[1]), jnp.bfloat16),
        compiler_params=pltpu.CompilerParams(vmem_limit_bytes=LIMIT),
        name="close",
    )(*[x for part in parts for x in part])


def swap(x, axis, size, bits):
    return lax.ppermute(x, axis, [(i, i ^ bits) for i in range(size)])


def after(x, *others):
    return lax.optimization_barrier((x, *others))[0]


def make_shards(seq, kv):
    def shards(queries, keys, values, out_weight):
        block = queries.shape[0]
        per_span = SPAN // block
        rank = lax.axis_index("seq").astype(jnp.int32).reshape(1)
        place = lax.axis_index("kv").astype(jnp.int32).reshape(1)
        kinds = min(3, max(2, seq // per_span))
        tables = rope_tables(block)
        by_head = jnp.transpose(queries, (1, 0, 2))
        pieces = {0: prepare(rank, keys[:, 0, :], values[:, 0, :], tables)}

        def fetch(offset, *others):
            if offset not in pieces:
                low = offset % per_span
                step = (low & -low) if low else offset & -offset
                if offset > per_span and low == 3:
                    step = 3
                source = fetch(offset - step)
                pieces[offset] = swap(after(source, *others) if others else source, "seq", seq, step)
            return pieces[offset]

        for offset in [step for step in (4, 8, 16, 32) if step < seq] + [2, 1]:
            fetch(offset)
        rot, *state, mine = begin(
            kinds, rank, place, by_head, tables, out_weight, pieces[0]
        )
        twin_weight = swap(out_weight, "kv", kv, 1)
        for offset in [3, 7, 6, 5] + list(range(seq)):
            fetch(offset, state[0])
        calls = [[1, 2, 3, 4]]
        while calls[-1][-1] < seq - 1:
            at = calls[-1][-1] + 1
            calls.append(list(range(at, min(at + per_span, seq))))
        for at, offsets in enumerate(calls[:-1]):
            stage = (place, twin_weight) if at == 0 else ()
            state = attend(
                rank, offsets, rot, [pieces[o] for o in offsets], state, False, 0, block, stage
            )
            if stage:
                *state, theirs = state
        parts = []
        offsets = calls[-1]
        rows = block // ROW_CHUNKS
        for chunk in range(ROW_CHUNKS):
            own = attend(
                rank, offsets, rot, [pieces[o] for o in offsets], state, True, chunk * rows, rows
            )
            twin = swap(own, "kv", kv, 1)
            away = project(1, own, twin, mine, theirs, jnp.bfloat16)
            landed = swap(away, "kv", kv, 2)
            home = project(0, own, twin, mine, theirs, jnp.float32)
            parts.append((home, landed))
        return close(parts)

    return shards


def solution(mesh):
    return jax.shard_map(
        make_shards(mesh.shape["seq"], mesh.shape["kv"]),
        mesh=mesh,
        in_specs=(P("seq", "kv", None), P("seq", "kv", None), P("seq", "kv", None), P("kv", None)),
        out_specs=P("seq", "kv"),
        check_vma=False,
    )
```

time: 58.1 us -> 40 us (0.69)
  Pallas kernels: 26.6 us -> 14.9 us
  local copies, waits for them, and re-layouts: 8.03 us -> 0 us
  waiting for transfers between devices: 7.62 us -> 10.3 us
  other arithmetic: 0.91 us -> 0 us
    pallas_call x9 -> x10, Pallas kernels: 26.6 us -> 14.9 us  [the longest x3 6.71 us: attend(): pl.pallas_call(functools.partial(attend_kernel, tuple(offsets), rot.shape...]
    unnamed x16 -> x0, local copies, waits for them, and re-layouts: 8.03 us -> none
    ppermute x12, waiting for transfers between devices: 7.62 us -> 10.3 us  [swap(): return lax.ppermute(x, axis, [(i, i ^ bits) for i in range(size)])]
    concatenate x1 -> x0, other arithmetic: 0.81 us -> none  [shards(): jnp.concatenate([(home + landed.astype(jnp.float32)).astype(jnp.bfloat16)...]
  transfers between devices with their start and end apart: 12 -> 12, of which waited for: 3 -> 5; matrix products, arithmetic and copies ran while one was open for 0% -> 0% of each run, Pallas kernels for 46% -> 32%
where the time goes in v2:
time: 40 us; the launch traced here: 39.9 us
  Pallas kernels  14.9 us (37%)
  starting transfers between devices  14.6 us (36%)
  waiting for transfers between devices  10.3 us (26%)
    ppermute x12, starting transfers between devices, swap(): return lax.ppermute(x, axis, [(i, i ^ bits) for i in range(size)])  14.6 us
    ppermute x12, waiting for transfers between devices, swap(): return lax.ppermute(x, axis, [(i, i ^ bits) for i in range(size)])  10.3 us
    pallas_call x3, Pallas kernels, attend(): pl.pallas_call(functools.partial(attend_kernel, tuple(offsets), rot.shape...  6.71 us
    pallas_call x1, Pallas kernels, begin(): pl.pallas_call(functools.partial(begin_kernel, kinds), in_specs=[smem, sm...  3.31 us
    pallas_call x4, Pallas kernels, project(): pl.pallas_call(functools.partial(project_kernel, flip), in_specs=[vmem] *...  2.91 us
    pallas_call x1, Pallas kernels, prepare(): pl.pallas_call(prepare_kernel, in_specs=[pl.BlockSpec(memory_space=pltpu....  1.13 us
    pallas_call x1, Pallas kernels, close(): pl.pallas_call(functools.partial(close_kernel, tuple(starts)), in_specs=[...  0.85 us
  transfers between devices with their start and end apart: 12, of which 5 were waited for; matrix products, arithmetic and copies ran while one was open for 0% of the time, Pallas kernels for 32%

profile of v2, /device:TPU:0, one launch (start us, length us, event | category | flops | bytes accessed | tf_op | source)
XLA Modules:
  0.0 39.9 jit_solution(12386275257149685157)
XLA Ops:
  0.0 0.5 %collective-permute-start.7 = (bf16[896,3584]{1,0:T(8,128)(2,1)}, bf16[896,3584]{1,0:T(8,128)(2,1)}, u32[]{:S(2)}, u32[]{:S(2)}) collective-permute-start(bf16[896,3584]{1,0:T(8,128)(2,1)} %weight_hbm.1), channel_id=1, source_target_pairs={{0,1},{1,0},{2,3},{3,2},{4,5},{5,4},{6,7},{7,6},{8,9},{9,8},{10,11... | collective-permute-start | bytes 19267592 | tf_op jit(solution)/shard_map/ppermute | solution.py:320
  0.5 1.1 %rotate_keys.1.piece_ref = bf16[512,128]{1,0:T(8,128)(2,1)S(1)} custom-call(s32[1]{0:T(128)} %bitcast.rank_ref, bf16[256,128]{1,0:T(8,128)(2,1)} %bitcast.6, bf16[256,128]{1,0:T(8,128)(2,1)} %bitcast.7, f32[1536,128]{1,0:T(8,128)} %constant.13.clone.cos_hbm, f32[1536,128]{1,0:T(8,128)} %constant.14.clone.sin_hbm), custom_call_target="tpu_custom_call" | custom-call | tf_op jit(solution)/shard_map/rotate_keys/pallas_call | solution.py:65
  1.6 2.6 %collective-permute-start.5 = (bf16[512,128]{1,0:T(8,128)(2,1)S(1)}, bf16[512,128]{1,0:T(8,128)(2,1)S(1)}, u32[]{:S(2)}, u32[]{:S(2)}) collective-permute-start(bf16[512,128]{1,0:T(8,128)(2,1)S(1)} %rotate_keys.1.piece_ref), channel_id=1, source_target_pairs={{0,8},{4,12},{8,0},{12,4},{16,24},{20,28},{24,16},{28,20},{1,9},{5... | collective-permute-start | bytes 393224 | tf_op jit(solution)/shard_map/ppermute | solution.py:320
  4.2 2.6 %collective-permute-start = (bf16[512,128]{1,0:T(8,128)(2,1)S(1)}, bf16[512,128]{1,0:T(8,128)(2,1)S(1)}, u32[]{:S(2)}, u32[]{:S(2)}) collective-permute-start(bf16[512,128]{1,0:T(8,128)(2,1)S(1)} %rotate_keys.1.piece_ref), channel_id=1, source_target_pairs={{0,16},{4,20},{8,24},{12,28},{16,0},{20,4},{24,8},{28,12},{1,17},{... | collective-permute-start | bytes 393224 | tf_op jit(solution)/shard_map/ppermute | solution.py:320
  6.8 1.5 %collective-permute-start.4 = (bf16[512,128]{1,0:T(8,128)(2,1)S(1)}, bf16[512,128]{1,0:T(8,128)(2,1)S(1)}, u32[]{:S(2)}, u32[]{:S(2)}) collective-permute-start(bf16[512,128]{1,0:T(8,128)(2,1)S(1)} %rotate_keys.1.piece_ref), channel_id=1, source_target_pairs={{0,4},{4,0},{8,12},{12,8},{16,20},{20,16},{24,28},{28,24},{1,5},{5... | collective-permute-start | bytes 393224 | tf_op jit(solution)/shard_map/ppermute | solution.py:320
  8.3 3.3 %attend_0.1 = (bf16[2,7,256,128]{3,2,1,0:T(8,128)(2,1)S(1)}, f32[7,256,128]{2,1,0:T(8,128)S(1)}, f32[7,256,128]{2,1,0:T(8,128)S(1)}, f32[7,256,128]{2,1,0:T(8,128)S(1)}, bf16[2,896,896]{2,1,0:T(8,128)(2,1)S(1)}) custom-call(s32[1]{0:T(128)} %bitcast.rank_ref, s32[1]{0:T(128)} %bitcast.1.place_ref.refs_7_, bf16[7,256,128]{2,1,0:T(8,128)(2,1)} %bitcast.5, ...), custom_call_target="tpu_custom_call" | custom-call | flops 2000000000 | bytes 8388608 | tf_op jit(solution)/shard_map/attend_0/pallas_call | solution.py:165
  11.7 1.1 %collective-permute-start.6 = (bf16[512,128]{1,0:T(8,128)(2,1)S(1)}, bf16[512,128]{1,0:T(8,128)(2,1)S(1)}, u32[]{:S(2)}, u32[]{:S(2)}) collective-permute-start(bf16[512,128]{1,0:T(8,128)(2,1)S(1)} %collective-permute-done.5.refs_1_), channel_id=1, source_target_pairs={{0,4},{4,0},{8,12},{12,8},{16,20},{20,16},{24,28},{28,24},{1,5},{5... | collective-permute-start | bytes 393224 | tf_op jit(solution)/shard_map/ppermute | solution.py:320
  12.8 0.8 %collective-permute-done.refs_3_ = bf16[512,128]{1,0:T(8,128)(2,1)S(1)} collective-permute-done((bf16[512,128]{1,0:T(8,128)(2,1)S(1)}, bf16[512,128]{1,0:T(8,128)(2,1)S(1)}, u32[]{:S(2)}, u32[]{:S(2)}) %collective-permute-start) | collective-permute-done | bytes 131104 | tf_op jit(solution)/shard_map/ppermute | solution.py:320
  13.6 1.5 %collective-permute-start.1 = (bf16[512,128]{1,0:T(8,128)(2,1)S(1)}, bf16[512,128]{1,0:T(8,128)(2,1)S(1)}, u32[]{:S(2)}, u32[]{:S(2)}) collective-permute-start(bf16[512,128]{1,0:T(8,128)(2,1)S(1)} %collective-permute-done.refs_3_), channel_id=1, source_target_pairs={{0,4},{4,0},{8,12},{12,8},{16,20},{20,16},{24,28},{28,24},{1,5},{5... | collective-permute-start | bytes 393224 | tf_op jit(solution)/shard_map/ppermute | solution.py:320
  15.6 1.5 %collective-permute-start.3 = (bf16[512,128]{1,0:T(8,128)(2,1)S(1)}, bf16[512,128]{1,0:T(8,128)(2,1)S(1)}, u32[]{:S(2)}, u32[]{:S(2)}) collective-permute-start(bf16[512,128]{1,0:T(8,128)(2,1)S(1)} %collective-permute-done.refs_3_), channel_id=1, source_target_pairs={{0,12},{4,8},{8,4},{12,0},{16,28},{20,24},{24,20},{28,16},{1,13},{... | collective-permute-start | bytes 393224 | tf_op jit(solution)/shard_map/ppermute | solution.py:320
  17.1 1.0 %collective-permute-done.6.refs_2_ = bf16[512,128]{1,0:T(8,128)(2,1)S(1)} collective-permute-done((bf16[512,128]{1,0:T(8,128)(2,1)S(1)}, bf16[512,128]{1,0:T(8,128)(2,1)S(1)}, u32[]{:S(2)}, u32[]{:S(2)}) %collective-permute-start.6) | collective-permute-done | bytes 131104 | tf_op jit(solution)/shard_map/ppermute | solution.py:320
  18.1 4.0 %attend_1_2_3_4.1 = (f32[7,256,128]{2,1,0:T(8,128)S(1)}, f32[7,256,128]{2,1,0:T(8,128)S(1)}, f32[7,256,128]{2,1,0:T(8,128)S(1)}, bf16[2,896,896]{2,1,0:T(8,128)(2,1)S(1)}) custom-call(s32[1]{0:T(128)} %bitcast.rank_ref, bf16[2,7,256,128]{3,2,1,0:T(8,128)(2,1)S(1)} %get-tuple-element.16.rot_ref, bf16[512,128]{1,0:T(8,128)(2,1)S(1)} %collective-permute-done.4.refs_0_, ...), custom_call_target="tpu_custom_call" | custom-call | flops 1879048192 | bytes 2097152 | tf_op jit(solution)/shard_map/attend_1_2_3_4/pallas_call | solution.py:254
  22.4 1.3 %attend_5_6_7.3.own_ref = bf16[128,896]{1,0:T(8,128)(2,1)S(1)} custom-call(s32[1]{0:T(128)} %bitcast.rank_ref, bf16[2,7,256,128]{3,2,1,0:T(8,128)(2,1)S(1)} %get-tuple-element.16.rot_ref, bf16[512,128]{1,0:T(8,128)(2,1)S(1)} %collective-permute-done.1.refs_0_, bf16[512,128]{1,0:T(8,128)(2,1)S(1)} %collective-permute-done.2.refs_1_, ...), custom_call_target="tpu_custom_call" | custom-call | flops 704643072 | bytes 2097152 | tf_op jit(solution)/shard_map/attend_5_6_7/pallas_call | solution.py:254
  23.9 1.3 %attend_5_6_7.2.own_ref = bf16[128,896]{1,0:T(8,128)(2,1)S(1)} custom-call(s32[1]{0:T(128)} %bitcast.rank_ref, bf16[2,7,256,128]{3,2,1,0:T(8,128)(2,1)S(1)} %get-tuple-element.16.rot_ref, bf16[512,128]{1,0:T(8,128)(2,1)S(1)} %collective-permute-done.1.refs_0_, bf16[512,128]{1,0:T(8,128)(2,1)S(1)} %collective-permute-done.2.refs_1_, ...), custom_call_target="tpu_custom_call" | custom-call | flops 704643072 | bytes 2097152 | tf_op jit(solution)/shard_map/attend_5_6_7/pallas_call | solution.py:254
  25.2 0.6 %collective-permute-start.8 = (bf16[128,896]{1,0:T(8,128)(2,1)S(1)}, bf16[128,896]{1,0:T(8,128)(2,1)S(1)}, u32[]{:S(2)}, u32[]{:S(2)}) collective-permute-start(bf16[128,896]{1,0:T(8,128)(2,1)S(1)} %attend_5_6_7.2.own_ref), channel_id=1, source_target_pairs={{0,1},{1,0},{2,3},{3,2},{4,5},{5,4},{6,7},{7,6},{8,9},{9,8},{10,11... | collective-permute-start | bytes 688136 | tf_op jit(solution)/shard_map/ppermute | solution.py:320
  25.8 0.7 %project_away.3 = bf16[128,896]{1,0:T(8,128)(2,1)S(1)} custom-call(bf16[128,896]{1,0:T(8,128)(2,1)S(1)} %attend_5_6_7.3.own_ref, bf16[128,896]{1,0:T(8,128)(2,1)S(1)} %collective-permute-done.10.twin_ref, bf16[2,896,896]{2,1,0:T(8,128)(2,1)S(1)} %get-tuple-element.25.own_weight, bf16[2,896,896]{2,1,0:T(8,128)(2,1)S(1)} %get-tuple-element.26.twin_weight), custom_call_target="tpu_custom_call" | custom-call | flops 411041792 | bytes 1605632 | tf_op jit(solution)/shard_map/project_away/pallas_call | solution.py:281
  26.5 1.6 %collective-permute-start.11 = (bf16[128,896]{1,0:T(8,128)(2,1)S(1)}, bf16[128,896]{1,0:T(8,128)(2,1)S(1)}, u32[]{:S(2)}, u32[]{:S(2)}) collective-permute-start(bf16[128,896]{1,0:T(8,128)(2,1)S(1)} %project_away.3), channel_id=1, source_target_pairs={{0,2},{1,3},{2,0},{3,1},{4,6},{5,7},{6,4},{7,5},{8,10},{9,11},{10,... | collective-permute-start | bytes 688136 | tf_op jit(solution)/shard_map/ppermute | solution.py:320
  28.1 0.7 %project_away.2 = bf16[128,896]{1,0:T(8,128)(2,1)S(1)} custom-call(bf16[128,896]{1,0:T(8,128)(2,1)S(1)} %attend_5_6_7.2.own_ref, bf16[128,896]{1,0:T(8,128)(2,1)S(1)} %collective-permute-done.8.twin_ref, bf16[2,896,896]{2,1,0:T(8,128)(2,1)S(1)} %get-tuple-element.25.own_weight, bf16[2,896,896]{2,1,0:T(8,128)(2,1)S(1)} %get-tuple-element.26.twin_weight), custom_call_target="tpu_custom_call" | custom-call | flops 411041792 | bytes 1605632 | tf_op jit(solution)/shard_map/project_away/pallas_call | solution.py:281
  28.8 0.6 %collective-permute-start.9 = (bf16[128,896]{1,0:T(8,128)(2,1)S(1)}, bf16[128,896]{1,0:T(8,128)(2,1)S(1)}, u32[]{:S(2)}, u32[]{:S(2)}) collective-permute-start(bf16[128,896]{1,0:T(8,128)(2,1)S(1)} %project_away.2), channel_id=1, source_target_pairs={{0,2},{1,3},{2,0},{3,1},{4,6},{5,7},{6,4},{7,5},{8,10},{9,11},{10,... | collective-permute-start | bytes 688136 | tf_op jit(solution)/shard_map/ppermute | solution.py:320
  29.4 0.7 %project_home.3.refs_2_ = f32[128,896]{1,0:T(8,128)S(1)} custom-call(bf16[128,896]{1,0:T(8,128)(2,1)S(1)} %attend_5_6_7.3.own_ref, bf16[128,896]{1,0:T(8,128)(2,1)S(1)} %collective-permute-done.10.twin_ref, bf16[2,896,896]{2,1,0:T(8,128)(2,1)S(1)} %get-tuple-element.25.own_weight, bf16[2,896,896]{2,1,0:T(8,128)(2,1)S(1)} %get-tuple-element.26.twin_weight), custom_call_target="tpu_custom_call" | custom-call | flops 411041792 | bytes 1605632 | tf_op jit(solution)/shard_map/project_home/pallas_call | solution.py:281
  30.1 0.7 %project_home.2.refs_0_ = f32[128,896]{1,0:T(8,128)S(1)} custom-call(bf16[128,896]{1,0:T(8,128)(2,1)S(1)} %attend_5_6_7.2.own_ref, bf16[128,896]{1,0:T(8,128)(2,1)S(1)} %collective-permute-done.8.twin_ref, bf16[2,896,896]{2,1,0:T(8,128)(2,1)S(1)} %get-tuple-element.25.own_weight, bf16[2,896,896]{2,1,0:T(8,128)(2,1)S(1)} %get-tuple-element.26.twin_weight), custom_call_target="tpu_custom_call" | custom-call | flops 411041792 | bytes 1605632 | tf_op jit(solution)/shard_map/project_home/pallas_call | solution.py:281
  30.9 4.2 %collective-permute-done.11.refs_3_ = bf16[128,896]{1,0:T(8,128)(2,1)S(1)} collective-permute-done((bf16[128,896]{1,0:T(8,128)(2,1)S(1)}, bf16[128,896]{1,0:T(8,128)(2,1)S(1)}, u32[]{:S(2)}, u32[]{:S(2)}) %collective-permute-start.11) | collective-permute-done | bytes 229408 | tf_op jit(solution)/shard_map/ppermute | solution.py:320
  35.0 4.0 %collective-permute-done.9.refs_1_ = bf16[128,896]{1,0:T(8,128)(2,1)S(1)} collective-permute-done((bf16[128,896]{1,0:T(8,128)(2,1)S(1)}, bf16[128,896]{1,0:T(8,128)(2,1)S(1)}, u32[]{:S(2)}, u32[]{:S(2)}) %collective-permute-start.9) | collective-permute-done | bytes 229408 | tf_op jit(solution)/shard_map/ppermute | solution.py:320
  39.0 0.8 %close.1 = bf16[256,896]{1,0:T(8,128)(2,1)} custom-call(f32[128,896]{1,0:T(8,128)S(1)} %project_home.2.refs_0_, bf16[128,896]{1,0:T(8,128)(2,1)S(1)} %collective-permute-done.9.refs_1_, f32[128,896]{1,0:T(8,128)S(1)} %project_home.3.refs_2_, bf16[128,896]{1,0:T(8,128)(2,1)S(1)} %collective-permute-done.11.refs_3_), custom_call_target="tpu_custom_call" | custom-call | tf_op jit(solution)/shard_map/close/pallas_call | solution.py:309
  (10 shorter events, 0.8 us)
Async XLA Ops:
  0.0 18.1 %collective-permute-start.7 = (bf16[896,3584]{1,0:T(8,128)(2,1)}, bf16[896,3584]{1,0:T(8,128)(2,1)}, u32[]{:S(2)}, u32[]{:S(2)}) collective-permute-start(bf16[896,3584]{1,0:T(8,128)(2,1)} %weight_hbm.1), channel_id=1, source_target_pairs={{0,1},{1,0},{2,3},{3,2},{4,5},{5,4},{6,7},{7,6},{8,9},{9,8},{10,11... | collective-permute-start | bytes 19267592 | tf_op jit(solution)/shard_map/ppermute | solution.py:320
  1.6 10.1 %collective-permute-start.5 = (bf16[512,128]{1,0:T(8,128)(2,1)S(1)}, bf16[512,128]{1,0:T(8,128)(2,1)S(1)}, u32[]{:S(2)}, u32[]{:S(2)}) collective-permute-start(bf16[512,128]{1,0:T(8,128)(2,1)S(1)} %rotate_keys.1.piece_ref), channel_id=1, source_target_pairs={{0,8},{4,12},{8,0},{12,4},{16,24},{20,28},{24,16},{28,20},{1,9},{5... | collective-permute-start | bytes 393224 | tf_op jit(solution)/shard_map/ppermute | solution.py:320
  4.2 9.4 %collective-permute-start = (bf16[512,128]{1,0:T(8,128)(2,1)S(1)}, bf16[512,128]{1,0:T(8,128)(2,1)S(1)}, u32[]{:S(2)}, u32[]{:S(2)}) collective-permute-start(bf16[512,128]{1,0:T(8,128)(2,1)S(1)} %rotate_keys.1.piece_ref), channel_id=1, source_target_pairs={{0,16},{4,20},{8,24},{12,28},{16,0},{20,4},{24,8},{28,12},{1,17},{... | collective-permute-start | bytes 393224 | tf_op jit(solution)/shard_map/ppermute | solution.py:320
  6.8 8.8 %collective-permute-start.4 = (bf16[512,128]{1,0:T(8,128)(2,1)S(1)}, bf16[512,128]{1,0:T(8,128)(2,1)S(1)}, u32[]{:S(2)}, u32[]{:S(2)}) collective-permute-start(bf16[512,128]{1,0:T(8,128)(2,1)S(1)} %rotate_keys.1.piece_ref), channel_id=1, source_target_pairs={{0,4},{4,0},{8,12},{12,8},{16,20},{20,16},{24,28},{28,24},{1,5},{5... | collective-permute-start | bytes 393224 | tf_op jit(solution)/shard_map/ppermute | solution.py:320
  11.7 6.5 %collective-permute-start.6 = (bf16[512,128]{1,0:T(8,128)(2,1)S(1)}, bf16[512,128]{1,0:T(8,128)(2,1)S(1)}, u32[]{:S(2)}, u32[]{:S(2)}) collective-permute-start(bf16[512,128]{1,0:T(8,128)(2,1)S(1)} %collective-permute-done.5.refs_1_), channel_id=1, source_target_pairs={{0,4},{4,0},{8,12},{12,8},{16,20},{20,16},{24,28},{28,24},{1,5},{5... | collective-permute-start | bytes 393224 | tf_op jit(solution)/shard_map/ppermute | solution.py:320
  13.6 8.5 %collective-permute-start.1 = (bf16[512,128]{1,0:T(8,128)(2,1)S(1)}, bf16[512,128]{1,0:T(8,128)(2,1)S(1)}, u32[]{:S(2)}, u32[]{:S(2)}) collective-permute-start(bf16[512,128]{1,0:T(8,128)(2,1)S(1)} %collective-permute-done.refs_3_), channel_id=1, source_target_pairs={{0,4},{4,0},{8,12},{12,8},{16,20},{20,16},{24,28},{28,24},{1,5},{5... | collective-permute-start | bytes 393224 | tf_op jit(solution)/shard_map/ppermute | solution.py:320
  15.1 7.0 %collective-permute-start.2 = (bf16[512,128]{1,0:T(8,128)(2,1)S(1)}, bf16[512,128]{1,0:T(8,128)(2,1)S(1)}, u32[]{:S(2)}, u32[]{:S(2)}) collective-permute-start(bf16[512,128]{1,0:T(8,128)(2,1)S(1)} %collective-permute-done.refs_3_), channel_id=1, source_target_pairs={{0,8},{4,12},{8,0},{12,4},{16,24},{20,28},{24,16},{28,20},{1,9},{5... | collective-permute-start | bytes 393224 | tf_op jit(solution)/shard_map/ppermute | solution.py:320
  15.6 6.8 %collective-permute-start.3 = (bf16[512,128]{1,0:T(8,128)(2,1)S(1)}, bf16[512,128]{1,0:T(8,128)(2,1)S(1)}, u32[]{:S(2)}, u32[]{:S(2)}) collective-permute-start(bf16[512,128]{1,0:T(8,128)(2,1)S(1)} %collective-permute-done.refs_3_), channel_id=1, source_target_pairs={{0,12},{4,8},{8,4},{12,0},{16,28},{20,24},{24,20},{28,16},{1,13},{... | collective-permute-start | bytes 393224 | tf_op jit(solution)/shard_map/ppermute | solution.py:320
  23.8 2.0 %collective-permute-start.10 = (bf16[128,896]{1,0:T(8,128)(2,1)S(1)}, bf16[128,896]{1,0:T(8,128)(2,1)S(1)}, u32[]{:S(2)}, u32[]{:S(2)}) collective-permute-start(bf16[128,896]{1,0:T(8,128)(2,1)S(1)} %attend_5_6_7.3.own_ref), channel_id=1, source_target_pairs={{0,1},{1,0},{2,3},{3,2},{4,5},{5,4},{6,7},{7,6},{8,9},{9,8},{10,11... | collective-permute-start | bytes 688136 | tf_op jit(solution)/shard_map/ppermute | solution.py:320
  25.2 2.9 %collective-permute-start.8 = (bf16[128,896]{1,0:T(8,128)(2,1)S(1)}, bf16[128,896]{1,0:T(8,128)(2,1)S(1)}, u32[]{:S(2)}, u32[]{:S(2)}) collective-permute-start(bf16[128,896]{1,0:T(8,128)(2,1)S(1)} %attend_5_6_7.2.own_ref), channel_id=1, source_target_pairs={{0,1},{1,0},{2,3},{3,2},{4,5},{5,4},{6,7},{7,6},{8,9},{9,8},{10,11... | collective-permute-start | bytes 688136 | tf_op jit(solution)/shard_map/ppermute | solution.py:320
  26.5 8.5 %collective-permute-start.11 = (bf16[128,896]{1,0:T(8,128)(2,1)S(1)}, bf16[128,896]{1,0:T(8,128)(2,1)S(1)}, u32[]{:S(2)}, u32[]{:S(2)}) collective-permute-start(bf16[128,896]{1,0:T(8,128)(2,1)S(1)} %project_away.3), channel_id=1, source_target_pairs={{0,2},{1,3},{2,0},{3,1},{4,6},{5,7},{6,4},{7,5},{8,10},{9,11},{10,... | collective-permute-start | bytes 688136 | tf_op jit(solution)/shard_map/ppermute | solution.py:320
  28.8 10.2 %collective-permute-start.9 = (bf16[128,896]{1,0:T(8,128)(2,1)S(1)}, bf16[128,896]{1,0:T(8,128)(2,1)S(1)}, u32[]{:S(2)}, u32[]{:S(2)}) collective-permute-start(bf16[128,896]{1,0:T(8,128)(2,1)S(1)} %project_away.2), channel_id=1, source_target_pairs={{0,2},{1,3},{2,0},{3,1},{4,6},{5,7},{6,4},{7,5},{8,10},{9,11},{10,... | collective-permute-start | bytes 688136 | tf_op jit(solution)/shard_map/ppermute | solution.py:320

commit v3 on v2

--- a/solution.py
+++ b/solution.py
@@ -16,10 +16,16 @@
 THETA = 10000000.0
 NEG = -1e30
 SCALE = math.log2(math.e) / math.sqrt(HEAD)
-ROW_CHUNKS = 2
+ROW_CHUNKS = (128, 128)
+FIRST = [4, 1, 2, 3]
+CALLS = [[1, 2], [3, 4], [7], [5, 6]]
+LATER = [7, 6, 5]
+EARLY = 0
+STAGE = 1
 VMEM = pltpu.MemorySpace.VMEM
 HBM = pltpu.MemorySpace.HBM
 LIMIT = 24 * 2**20
+LIGHT = pl.CostEstimate(flops=1, bytes_accessed=1, transcendentals=0)
 
 
 def rope_tables(block):
@@ -117,10 +123,20 @@
     return top, acc, total
 
 
+def column_copies(place, weight_hbm, into, sems):
+    columns = into[0].shape[1]
+    copies = []
+    for flip, ref in enumerate(into):
+        at = pl.ds(pl.multiple_of((place ^ (2 * flip)) * columns, columns), columns)
+        copies.append(pltpu.make_async_copy(weight_hbm.at[:, at], ref, sems.at[flip]))
+    return copies
+
+
 def begin_kernel(
     kinds, rank_ref, place_ref, query_hbm, cos_hbm, sin_hbm, weight_hbm, piece_ref,
-    rot_ref, top_ref, acc_ref, total_ref, mine_ref, query_ref, cos_ref, sin_ref, sems, weight_sems,
+    rot_ref, top_ref, acc_ref, total_ref, *refs,
 ):
+    *mine, query_ref, cos_ref, sin_ref, sems, weight_sems = refs
     heads, block, _ = query_ref.shape
     per_span = SPAN // block
     rank, place = rank_ref[0], place_ref[0]
@@ -133,7 +149,7 @@
         copies.append(pltpu.make_async_copy(sin_hbm.at[rows], sin_ref.at[kind], sems.at[2 + 2 * kind]))
     for copy in copies:
         copy.start()
-    loads = column_copies(place, weight_hbm, mine_ref, weight_sems)
+    loads = column_copies(place, weight_hbm, mine, weight_sems)
     for copy in loads:
         copy.start()
     for copy in copies:
@@ -161,36 +177,27 @@
     heads, block, _ = queries.shape
     depth = out_weight.shape[0]
     smem, hbm, vmem = (pl.BlockSpec(memory_space=space) for space in (pltpu.SMEM, HBM, VMEM))
-    halves = jax.ShapeDtypeStruct((2, depth, depth), jnp.bfloat16)
+    parts = 2
     return pl.pallas_call(
         functools.partial(begin_kernel, kinds),
         in_specs=[smem, smem, hbm, hbm, hbm, hbm, vmem],
-        out_specs=[vmem] * 5,
+        out_specs=[vmem] * (4 + parts),
         out_shape=[
             jax.ShapeDtypeStruct((kinds, heads, block, HEAD), jnp.bfloat16),
             *[jax.ShapeDtypeStruct((heads, block, HEAD), jnp.float32)] * 3,
-            halves,
+            *[jax.ShapeDtypeStruct((depth, depth), jnp.bfloat16)] * parts,
         ],
         scratch_shapes=[
             pltpu.VMEM((heads, block, HEAD), jnp.bfloat16),
             pltpu.VMEM((kinds, block, HEAD), jnp.float32),
             pltpu.VMEM((kinds, block, HEAD), jnp.float32),
             pltpu.SemaphoreType.DMA((1 + 2 * kinds,)),
-            pltpu.SemaphoreType.DMA((2,)),
+            pltpu.SemaphoreType.DMA((parts,)),
         ],
-        cost_estimate=pl.CostEstimate(flops=2 * 10**9, bytes_accessed=2**23, transcendentals=10**6),
+        cost_estimate=LIGHT,
         compiler_params=pltpu.CompilerParams(vmem_limit_bytes=LIMIT),
         name="attend_0",
     )(rank, place, *[in_hbm(x) for x in (queries, *tables, out_weight)], piece)
-
-
-def column_copies(place, weight_hbm, into, sems):
-    columns = into.shape[2]
-    copies = []
-    for flip in range(2):
-        at = pl.ds(pl.multiple_of((place ^ (2 * flip)) * columns, columns), columns)
-        copies.append(pltpu.make_async_copy(weight_hbm.at[:, at], into.at[flip], sems.at[flip]))
-    return copies
 
 
 def attend_kernel(offsets, kinds, last, start, rows, stages, rank_ref, rot_ref, *refs):
@@ -198,8 +205,8 @@
     old, refs = refs[:3], refs[3:]
     loads = []
     if stages:
-        place_ref, weight_hbm, *refs, staged_ref, sems = refs
-        loads = column_copies(place_ref[0], weight_hbm, staged_ref, sems)
+        place_ref, weight_hbm, *refs, away_ref, sems = refs
+        loads = column_copies(place_ref[0] ^ 2, weight_hbm, [away_ref], sems)
     for copy in loads:
         copy.start()
     block = pieces[0].shape[0] // 2
@@ -248,9 +255,8 @@
         args = [place, in_hbm(weight)]
         in_specs = [smem, pl.BlockSpec(memory_space=HBM)]
         out_specs = [*out_specs, vmem]
-        out_shape = [*out_shape, jax.ShapeDtypeStruct((2, depth, depth), jnp.bfloat16)]
-        scratch = [pltpu.SemaphoreType.DMA((2,))]
-    pairs = GROUP * rows * block * len(pieces)
+        out_shape = [*out_shape, jax.ShapeDtypeStruct((depth, depth), jnp.bfloat16)]
+        scratch = [pltpu.SemaphoreType.DMA((1,))]
     return pl.pallas_call(
         functools.partial(
             attend_kernel, tuple(offsets), rot.shape[0], last, start, rows, bool(stage)
@@ -259,61 +265,96 @@
         scratch_shapes=scratch,
         out_specs=out_specs,
         out_shape=out_shape,
-        cost_estimate=pl.CostEstimate(
-            flops=8 * HEAD * pairs, bytes_accessed=2**21, transcendentals=pairs
-        ),
+        cost_estimate=LIGHT,
         compiler_params=pltpu.CompilerParams(vmem_limit_bytes=LIMIT),
         name="attend_" + "_".join(map(str, offsets)),
     )(rank, rot, *pieces, *state, *args)
 
 
-def project_kernel(flip, own_ref, twin_ref, own_weight, twin_weight, out_ref):
+def project_kernel(own_ref, twin_ref, own_weight, twin_weight, out_ref):
     out_ref[...] = (
-        jnp.dot(own_ref[...], own_weight[flip], preferred_element_type=jnp.float32)
-        + jnp.dot(twin_ref[...], twin_weight[flip], preferred_element_type=jnp.float32)
+        jnp.dot(own_ref[...], own_weight[...], preferred_element_type=jnp.float32)
+        + jnp.dot(twin_ref[...], twin_weight[...], preferred_element_type=jnp.float32)
     ).astype(out_ref.dtype)
 
 
-def project(flip, own, twin, own_weight, twin_weight, dtype):
-    rows, depth = own.shape
-    columns = own_weight.shape[2]
+def project(own, twin, own_weight, twin_weight, dtype, name):
     vmem = pl.BlockSpec(memory_space=VMEM)
     return pl.pallas_call(
-        functools.partial(project_kernel, flip),
+        project_kernel,
         in_specs=[vmem] * 4,
         out_specs=vmem,
-        out_shape=jax.ShapeDtypeStruct((rows, columns), dtype),
-        cost_estimate=pl.CostEstimate(
-            flops=4 * rows * depth * columns, bytes_accessed=2 * depth * columns, transcendentals=0
-        ),
-        compiler_params=pltpu.CompilerParams(vmem_limit_bytes=LIMIT),
-        name="project_away" if flip else "project_home",
+        out_shape=jax.ShapeDtypeStruct((own.shape[0], own_weight.shape[1]), dtype),
+        cost_estimate=LIGHT,
+        compiler_params=pltpu.CompilerParams(vmem_limit_bytes=LIMIT),
+        name=name,
     )(own, twin, own_weight, twin_weight)
 
 
-def close_kernel(starts, *refs):
-    out_ref = refs[-1]
-    for at, start in enumerate(starts):
-        home, landed = refs[2 * at], refs[2 * at + 1]
-        out_ref[start : start + home.shape[0]] = (
-            home[...] + landed[...].astype(jnp.float32)
-        ).astype(out_ref.dtype)
-
-
-def close(parts):
-    starts, rows = [], 0
-    for home, _ in parts:
-        starts.append(rows)
-        rows += home.shape[0]
-    vmem = pl.BlockSpec(memory_space=VMEM)
-    return pl.pallas_call(
-        functools.partial(close_kernel, tuple(starts)),
-        in_specs=[vmem] * (2 * len(parts)),
+def home_kernel(count, place_ref, twin_hbm, own_weight, *refs):
+    own_refs, twin_refs, refs = refs[:count], refs[count : 2 * count], refs[2 * count :]
+    out_ref, twin_weight, sems = refs
+    (load,) = column_copies(place_ref[0], twin_hbm, [twin_weight], sems)
+    load.start()
+    start = 0
+    for own in own_refs:
+        rows = pl.ds(start, own.shape[0])
+        out_ref[rows] = jnp.dot(own[...], own_weight[...], preferred_element_type=jnp.float32)
+        start += own.shape[0]
+    load.wait()
+    start = 0
+    for twin in twin_refs:
+        rows = pl.ds(start, twin.shape[0])
+        out_ref[rows] += jnp.dot(twin[...], twin_weight[...], preferred_element_type=jnp.float32)
+        start += twin.shape[0]
+
+
+def project_home(place, own, twin, own_weight, twin_weight):
+    smem, hbm, vmem = (pl.BlockSpec(memory_space=space) for space in (pltpu.SMEM, HBM, VMEM))
+    rows = sum(x.shape[0] for x in own)
+    return pl.pallas_call(
+        functools.partial(home_kernel, len(own)),
+        in_specs=[smem, hbm] + [vmem] * (2 * len(own) + 1),
         out_specs=vmem,
-        out_shape=jax.ShapeDtypeStruct((rows, parts[0][0].shape[1]), jnp.bfloat16),
+        out_shape=jax.ShapeDtypeStruct((rows, own_weight.shape[1]), jnp.float32),
+        scratch_shapes=[
+            pltpu.VMEM(own_weight.shape, jnp.bfloat16),
+            pltpu.SemaphoreType.DMA((1,)),
+        ],
+        cost_estimate=LIGHT,
+        compiler_params=pltpu.CompilerParams(vmem_limit_bytes=LIMIT),
+        name="home",
+    )(place, in_hbm(twin_weight), own_weight, *own, *twin)
+
+
+def close_kernel(home_ref, *refs):
+    *landed_refs, out_hbm, sum_ref, sems = refs
+    copies, start = [], 0
+    for at, landed in enumerate(landed_refs):
+        rows = pl.ds(start, landed.shape[0])
+        sum_ref[rows] = (home_ref[rows] + landed[...].astype(jnp.float32)).astype(sum_ref.dtype)
+        copies.append(pltpu.make_async_copy(sum_ref.at[rows], out_hbm.at[rows], sems.at[at]))
+        copies[-1].start()
+        start += landed.shape[0]
+    for copy in copies:
+        copy.wait()
+
+
+def close(home, landed):
+    vmem, hbm = (pl.BlockSpec(memory_space=space) for space in (VMEM, HBM))
+    return pl.pallas_call(
+        close_kernel,
+        in_specs=[vmem] * (1 + len(landed)),
+        out_specs=hbm,
+        out_shape=jax.ShapeDtypeStruct(home.shape, jnp.bfloat16),
+        scratch_shapes=[
+            pltpu.VMEM(home.shape, jnp.bfloat16),
+            pltpu.SemaphoreType.DMA((len(landed),)),
+        ],
+        cost_estimate=LIGHT,
         compiler_params=pltpu.CompilerParams(vmem_limit_bytes=LIMIT),
         name="close",
-    )(*[x for part in parts for x in part])
+    )(home, *landed)
 
 
 def swap(x, axis, size, bits):
@@ -335,48 +376,45 @@
         by_head = jnp.transpose(queries, (1, 0, 2))
         pieces = {0: prepare(rank, keys[:, 0, :], values[:, 0, :], tables)}
 
-        def fetch(offset, *others):
-            if offset not in pieces:
-                low = offset % per_span
-                step = (low & -low) if low else offset & -offset
-                if offset > per_span and low == 3:
-                    step = 3
-                source = fetch(offset - step)
-                pieces[offset] = swap(after(source, *others) if others else source, "seq", seq, step)
-            return pieces[offset]
-
-        for offset in [step for step in (4, 8, 16, 32) if step < seq] + [2, 1]:
-            fetch(offset)
-        rot, *state, mine = begin(
+        def send(offset, step, *others):
+            pieces[offset] = swap(after(pieces[offset ^ step], *others), "seq", seq, step)
+
+        twin_weight = swap(out_weight, "kv", kv, 1)
+        for offset in FIRST:
+            send(offset, offset)
+        rot, *state = begin(
             kinds, rank, place, by_head, tables, out_weight, pieces[0]
         )
-        twin_weight = swap(out_weight, "kv", kv, 1)
-        for offset in [3, 7, 6, 5] + list(range(seq)):
-            fetch(offset, state[0])
-        calls = [[1, 2, 3, 4]]
-        while calls[-1][-1] < seq - 1:
-            at = calls[-1][-1] + 1
-            calls.append(list(range(at, min(at + per_span, seq))))
+        state, mine = state[:3], state[3:]
+        for offset in range(2 * per_span, seq, per_span):
+            send(offset, offset & -offset)
+            for low in range(1, per_span):
+                send(offset + low, low)
+        calls = CALLS + [list(range(at, at + per_span)) for at in range(2 * per_span, seq, per_span)]
+
+        def blocks(offsets, state, *how):
+            return attend(rank, offsets, rot, [pieces[o] for o in offsets], state, *how)
+
         for at, offsets in enumerate(calls[:-1]):
-            stage = (place, twin_weight) if at == 0 else ()
-            state = attend(
-                rank, offsets, rot, [pieces[o] for o in offsets], state, False, 0, block, stage
+            if at == EARLY:
+                for offset in LATER:
+                    send(offset, offset % per_span, state[0])
+            state = blocks(offsets, state, False, 0, block, (place, twin_weight) if at == STAGE else ())
+            if at == STAGE:
+                state, theirs = state[:3], state[3]
+        own, twin, start = [], [], 0
+        for rows in ROW_CHUNKS:
+            own.append(blocks(calls[-1], state, True, start, rows))
+            twin.append(swap(own[-1], "kv", kv, 1))
+            start += rows
+        landed = []
+        for rows in zip(own, twin):
+            away = project(
+                *rows, mine[1], theirs, jnp.bfloat16, "away"
             )
-            if stage:
-                *state, theirs = state
-        parts = []
-        offsets = calls[-1]
-        rows = block // ROW_CHUNKS
-        for chunk in range(ROW_CHUNKS):
-            own = attend(
-                rank, offsets, rot, [pieces[o] for o in offsets], state, True, chunk * rows, rows
-            )
-            twin = swap(own, "kv", kv, 1)
-            away = project(1, own, twin, mine, theirs, jnp.bfloat16)
-            landed = swap(away, "kv", kv, 2)
-            home = project(0, own, twin, mine, theirs, jnp.float32)
-            parts.append((home, landed))
-        return close(parts)
+            landed.append(swap(away, "kv", kv, 2))
+        home = project_home(place, own, twin, mine[0], twin_weight)
+        return close(home, landed)
 
     return shards
 

time: 40 us -> 38.9 us (0.972)
  waiting for transfers between devices: 10.3 us -> 8.31 us
  Pallas kernels: 14.9 us -> 16.3 us
  starting transfers between devices: 14.6 us -> 14 us
    ppermute x12, waiting for transfers between devices: 10.3 us -> 8.31 us  [swap(): return lax.ppermute(x, axis, [(i, i ^ bits) for i in range(size)])]
    pallas_call x5 -> x4, Pallas kernels: 3.76 us -> 4.5 us  [the longest x1 2.21 us: project_home(): pl.pallas_call(functools.partial(home_kernel, len(own)), in_specs=[smem,...]
    pallas_call x3 -> x5, Pallas kernels: 6.71 us -> 7.37 us  [attend(): pl.pallas_call(functools.partial(attend_kernel, tuple(offsets), rot.shape...]
    ppermute x12, starting transfers between devices: 14.6 us -> 14 us  [swap(): return lax.ppermute(x, axis, [(i, i ^ bits) for i in range(size)])]
  transfers between devices with their start and end apart: 12 -> 12, of which waited for: 5 -> 4; matrix products, arithmetic and copies ran while one was open for 0% -> 0% of each run, Pallas kernels for 32% -> 37%
where the time goes in v3:
time: 38.9 us; the launch traced here: 38.7 us
  Pallas kernels  16.3 us (42%)
  starting transfers between devices  14 us (36%)
  waiting for transfers between devices  8.31 us (21%)
    ppermute x12, starting transfers between devices, swap(): return lax.ppermute(x, axis, [(i, i ^ bits) for i in range(size)])  14 us
    ppermute x12, waiting for transfers between devices, swap(): return lax.ppermute(x, axis, [(i, i ^ bits) for i in range(size)])  8.31 us
    pallas_call x5, Pallas kernels, attend(): pl.pallas_call(functools.partial(attend_kernel, tuple(offsets), rot.shape...  7.37 us
    pallas_call x1, Pallas kernels, begin(): pl.pallas_call(functools.partial(begin_kernel, kinds), in_specs=[smem, sm...  3.3 us
    pallas_call x1, Pallas kernels, project_home(): pl.pallas_call(functools.partial(home_kernel, len(own)), in_specs=[smem,...  2.21 us
    pallas_call x2, Pallas kernels, project(): pl.pallas_call(project_kernel, in_specs=[vmem] * 4, out_specs=vmem, out_s...  1.47 us
    pallas_call x1, Pallas kernels, prepare(): pl.pallas_call(prepare_kernel, in_specs=[pl.BlockSpec(memory_space=pltpu....  1.13 us
    pallas_call x1, Pallas kernels, close(): pl.pallas_call(close_kernel, in_specs=[vmem] * (1 + len(landed)), out_spe...  0.82 us
  transfers between devices with their start and end apart: 12, of which 4 were waited for; matrix products, arithmetic and copies ran while one was open for 0% of the time, Pallas kernels for 37%

profile of v3, /device:TPU:0, one launch (start us, length us, event | category | flops | bytes accessed | tf_op | source)
XLA Modules:
  0.0 38.7 jit_solution(10893910450206398985)
XLA Ops:
  0.0 0.5 %collective-permute-start = (bf16[896,3584]{1,0:T(8,128)(2,1)}, bf16[896,3584]{1,0:T(8,128)(2,1)}, u32[]{:S(2)}, u32[]{:S(2)}) collective-permute-start(bf16[896,3584]{1,0:T(8,128)(2,1)} %weight_hbm.1), channel_id=1, source_target_pairs={{0,1},{1,0},{2,3},{3,2},{4,5},{5,4},{6,7},{7,6},{8,9},{9,8},{10,11... | collective-permute-start | bytes 19267592 | tf_op jit(solution)/shard_map/ppermute | solution.py:361
  0.5 1.1 %rotate_keys.1.piece_ref = bf16[512,128]{1,0:T(8,128)(2,1)S(1)} custom-call(s32[1]{0:T(128)} %bitcast.1.rank_ref, bf16[256,128]{1,0:T(8,128)(2,1)} %bitcast.6, bf16[256,128]{1,0:T(8,128)(2,1)} %bitcast.7, f32[1536,128]{1,0:T(8,128)} %constant.13.clone.cos_hbm, f32[1536,128]{1,0:T(8,128)} %constant.14.clone.sin_hbm), custom_call_target="tpu_custom_call" | custom-call | tf_op jit(solution)/shard_map/rotate_keys/pallas_call | solution.py:71
  1.6 3.7 %collective-permute-start.1 = (bf16[512,128]{1,0:T(8,128)(2,1)S(1)}, bf16[512,128]{1,0:T(8,128)(2,1)S(1)}, u32[]{:S(2)}, u32[]{:S(2)}) collective-permute-start(bf16[512,128]{1,0:T(8,128)(2,1)S(1)} %rotate_keys.1.piece_ref), channel_id=1, source_target_pairs={{0,16},{4,20},{8,24},{12,28},{16,0},{20,4},{24,8},{28,12},{1,17},{... | collective-permute-start | bytes 393224 | tf_op jit(solution)/shard_map/ppermute | solution.py:361
  5.2 1.6 %collective-permute-start.7 = (bf16[512,128]{1,0:T(8,128)(2,1)S(1)}, bf16[512,128]{1,0:T(8,128)(2,1)S(1)}, u32[]{:S(2)}, u32[]{:S(2)}) collective-permute-start(bf16[512,128]{1,0:T(8,128)(2,1)S(1)} %rotate_keys.1.piece_ref), channel_id=1, source_target_pairs={{0,8},{4,12},{8,0},{12,4},{16,24},{20,28},{24,16},{28,20},{1,9},{5... | collective-permute-start | bytes 393224 | tf_op jit(solution)/shard_map/ppermute | solution.py:361
  6.8 1.5 %collective-permute-start.6 = (bf16[512,128]{1,0:T(8,128)(2,1)S(1)}, bf16[512,128]{1,0:T(8,128)(2,1)S(1)}, u32[]{:S(2)}, u32[]{:S(2)}) collective-permute-start(bf16[512,128]{1,0:T(8,128)(2,1)S(1)} %rotate_keys.1.piece_ref), channel_id=1, source_target_pairs={{0,4},{4,0},{8,12},{12,8},{16,20},{20,16},{24,28},{28,24},{1,5},{5... | collective-permute-start | bytes 393224 | tf_op jit(solution)/shard_map/ppermute | solution.py:361
  8.7 3.3 %attend_0.1 = (bf16[2,7,256,128]{3,2,1,0:T(8,128)(2,1)S(1)}, f32[7,256,128]{2,1,0:T(8,128)S(1)}, f32[7,256,128]{2,1,0:T(8,128)S(1)}, f32[7,256,128]{2,1,0:T(8,12...) custom-call(s32[1]{0:T(128)} %bitcast.1.rank_ref, s32[1]{0:T(128)} %bitcast.place_ref.refs_5_, ...), custom_call_target="tpu_custom_call" | custom-call | flops 1 | bytes 1 | tf_op jit(solution)/shard_map/attend_0/pallas_call | solution.py:181
  12.3 2.3 %collective-permute-start.4 = (bf16[512,128]{1,0:T(8,128)(2,1)S(1)}, bf16[512,128]{1,0:T(8,128)(2,1)S(1)}, u32[]{:S(2)}, u32[]{:S(2)}) collective-permute-start(bf16[512,128]{1,0:T(8,128)(2,1)S(1)} %collective-permute-done.1.refs_1_), channel_id=1, source_target_pairs={{0,12},{4,8},{8,4},{12,0},{16,28},{20,24},{24,20},{28,16},{1,13},{... | collective-permute-start | bytes 393224 | tf_op jit(solution)/shard_map/ppermute | solution.py:361
  14.7 0.7 %collective-permute-start.3 = (bf16[512,128]{1,0:T(8,128)(2,1)S(1)}, bf16[512,128]{1,0:T(8,128)(2,1)S(1)}, u32[]{:S(2)}, u32[]{:S(2)}) collective-permute-start(bf16[512,128]{1,0:T(8,128)(2,1)S(1)} %collective-permute-done.1.refs_1_), channel_id=1, source_target_pairs={{0,8},{4,12},{8,0},{12,4},{16,24},{20,28},{24,16},{28,20},{1,9},{5... | collective-permute-start | bytes 393224 | tf_op jit(solution)/shard_map/ppermute | solution.py:361
  15.4 0.6 %collective-permute-start.2 = (bf16[512,128]{1,0:T(8,128)(2,1)S(1)}, bf16[512,128]{1,0:T(8,128)(2,1)S(1)}, u32[]{:S(2)}, u32[]{:S(2)}) collective-permute-start(bf16[512,128]{1,0:T(8,128)(2,1)S(1)} %collective-permute-done.1.refs_1_), channel_id=1, source_target_pairs={{0,4},{4,0},{8,12},{12,8},{16,20},{20,16},{24,28},{28,24},{1,5},{5... | collective-permute-start | bytes 393224 | tf_op jit(solution)/shard_map/ppermute | solution.py:361
  15.9 1.6 %attend_1_2.1 = (f32[7,256,128]{2,1,0:T(8,128)S(1)}, f32[7,256,128]{2,1,0:T(8,128)S(1)}, f32[7,256,128]{2,1,0:T(8,128)S(1)}) custom-call(s32[1]{0:T(128)} %bitcast.1.rank_ref, bf16[2,7,256,128]{3,2,1,0:T(8,128)(2,1)S(1)} %get-tuple-element.23.rot_ref, bf16[512,128]{1,0:T(8,128)(2,1)S(1)} %collective-permute-done.6.refs_0_, ...), custom_call_target="tpu_custom_call" | custom-call | flops 1 | bytes 1 | tf_op jit(solution)/shard_map/attend_1_2/pallas_call | solution.py:260
  17.6 2.8 %attend_3_4.1 = (f32[7,256,128]{2,1,0:T(8,128)S(1)}, f32[7,256,128]{2,1,0:T(8,128)S(1)}, f32[7,256,128]{2,1,0:T(8,128)S(1)}, bf16[896,896]{1,0:T(8,128)(2,1)S(1)}) custom-call(s32[1]{0:T(128)} %bitcast.1.rank_ref, bf16[2,7,256,128]{3,2,1,0:T(8,128)(2,1)S(1)} %get-tuple-element.23.rot_ref, bf16[512,128]{1,0:T(8,128)(2,1)S(1)} %collective-permute-done.5.refs_0_, ...), custom_call_target="tpu_custom_call" | custom-call | flops 1 | bytes 1 | tf_op jit(solution)/shard_map/attend_3_4/pallas_call | solution.py:260
  20.4 1.0 %attend_7.1 = (f32[7,256,128]{2,1,0:T(8,128)S(1)}, f32[7,256,128]{2,1,0:T(8,128)S(1)}, f32[7,256,128]{2,1,0:T(8,128)S(1)}) custom-call(s32[1]{0:T(128)} %bitcast.1.rank_ref, bf16[2,7,256,128]{3,2,1,0:T(8,128)(2,1)S(1)} %get-tuple-element.23.rot_ref, bf16[512,128]{1,0:T(8,128)(2,1)S(1)} %collective-permute-done.4.refs_0_, ...), custom_call_target="tpu_custom_call" | custom-call | flops 1 | bytes 1 | tf_op jit(solution)/shard_map/attend_7/pallas_call | solution.py:260
  21.4 0.6 %collective-permute-done.2.refs_0_ = bf16[512,128]{1,0:T(8,128)(2,1)S(1)} collective-permute-done((bf16[512,128]{1,0:T(8,128)(2,1)S(1)}, bf16[512,128]{1,0:T(8,128)(2,1)S(1)}, u32[]{:S(2)}, u32[]{:S(2)}) %collective-permute-start.2) | collective-permute-done | bytes 131104 | tf_op jit(solution)/shard_map/ppermute | solution.py:361
  22.0 1.0 %attend_5_6.2.refs_0_.own_ref = bf16[128,896]{1,0:T(8,128)(2,1)S(1)} custom-call(s32[1]{0:T(128)} %bitcast.1.rank_ref, bf16[2,7,256,128]{3,2,1,0:T(8,128)(2,1)S(1)} %get-tuple-element.23.rot_ref, bf16[512,128]{1,0:T(8,128)(2,1)S(1)} %collective-permute-done.2.refs_0_, bf16[512,128]{1,0:T(8,128)(2,1)S(1)} %collective-permute-done.3.refs_1_, ...), custom_call_target="tpu_custom_call" | custom-call | flops 1 | bytes 1 | tf_op jit(solution)/shard_map/attend_5_6/pallas_call | solution.py:260
  23.0 1.0 %attend_5_6.3.refs_1_.own_ref = bf16[128,896]{1,0:T(8,128)(2,1)S(1)} custom-call(s32[1]{0:T(128)} %bitcast.1.rank_ref, bf16[2,7,256,128]{3,2,1,0:T(8,128)(2,1)S(1)} %get-tuple-element.23.rot_ref, bf16[512,128]{1,0:T(8,128)(2,1)S(1)} %collective-permute-done.2.refs_0_, bf16[512,128]{1,0:T(8,128)(2,1)S(1)} %collective-permute-done.3.refs_1_, ...), custom_call_target="tpu_custom_call" | custom-call | flops 1 | bytes 1 | tf_op jit(solution)/shard_map/attend_5_6/pallas_call | solution.py:260
  24.0 0.6 %collective-permute-start.9 = (bf16[128,896]{1,0:T(8,128)(2,1)S(1)}, bf16[128,896]{1,0:T(8,128)(2,1)S(1)}, u32[]{:S(2)}, u32[]{:S(2)}) collective-permute-start(bf16[128,896]{1,0:T(8,128)(2,1)S(1)} %attend_5_6.3.refs_1_.own_ref), channel_id=1, source_target_pairs={{0,1},{1,0},{2,3},{3,2},{4,5},{5,4},{6,7},{7,6},{8,9},{9,8},{10,11... | collective-permute-start | bytes 688136 | tf_op jit(solution)/shard_map/ppermute | solution.py:361
  24.6 0.7 %away.2 = bf16[128,896]{1,0:T(8,128)(2,1)S(1)} custom-call(bf16[128,896]{1,0:T(8,128)(2,1)S(1)} %attend_5_6.2.refs_0_.own_ref, bf16[128,896]{1,0:T(8,128)(2,1)S(1)} %collective-permute-done.8.refs_2_.twin_ref, bf16[896,896]{1,0:T(8,128)(2,1)S(1)} %get-tuple-element.37.own_weight, bf16[896,896]{1,0:T(8,128)(2,1)S(1)} %get-tuple-element.38.twin_weight), custom_call_target="tpu_custom_call" | custom-call | flops 1 | bytes 1 | tf_op jit(solution)/shard_map/away/pallas_call | solution.py:283
  25.3 1.6 %collective-permute-start.10 = (bf16[128,896]{1,0:T(8,128)(2,1)S(1)}, bf16[128,896]{1,0:T(8,128)(2,1)S(1)}, u32[]{:S(2)}, u32[]{:S(2)}) collective-permute-start(bf16[128,896]{1,0:T(8,128)(2,1)S(1)} %away.2), channel_id=1, source_target_pairs={{0,2},{1,3},{2,0},{3,1},{4,6},{5,7},{6,4},{7,5},{8,10},{9,11},{10,... | collective-permute-start | bytes 688136 | tf_op jit(solution)/shard_map/ppermute | solution.py:361
  26.9 0.7 %away.3 = bf16[128,896]{1,0:T(8,128)(2,1)S(1)} custom-call(bf16[128,896]{1,0:T(8,128)(2,1)S(1)} %attend_5_6.3.refs_1_.own_ref, bf16[128,896]{1,0:T(8,128)(2,1)S(1)} %collective-permute-done.9.refs_3_.twin_ref, bf16[896,896]{1,0:T(8,128)(2,1)S(1)} %get-tuple-element.37.own_weight, bf16[896,896]{1,0:T(8,128)(2,1)S(1)} %get-tuple-element.38.twin_weight), custom_call_target="tpu_custom_call" | custom-call | flops 1 | bytes 1 | tf_op jit(solution)/shard_map/away/pallas_call | solution.py:283
  27.6 0.6 %collective-permute-start.11 = (bf16[128,896]{1,0:T(8,128)(2,1)S(1)}, bf16[128,896]{1,0:T(8,128)(2,1)S(1)}, u32[]{:S(2)}, u32[]{:S(2)}) collective-permute-start(bf16[128,896]{1,0:T(8,128)(2,1)S(1)} %away.3), channel_id=1, source_target_pairs={{0,2},{1,3},{2,0},{3,1},{4,6},{5,7},{6,4},{7,5},{8,10},{9,11},{10,... | collective-permute-start | bytes 688136 | tf_op jit(solution)/shard_map/ppermute | solution.py:361
  28.2 2.2 %home.1.home_ref = f32[256,896]{1,0:T(8,128)S(1)} custom-call(s32[1]{0:T(128)} %bitcast.place_ref.refs_5_, bf16[896,3584]{1,0:T(8,128)(2,1)} %collective-permute-done.refs_6_.twin_hbm, bf16[896,896]{1,0:T(8,128)(2,1)S(1)} %get-tuple-element.22.own_weight, bf16[128,896]{1,0:T(8,128)(2,1)S(1)} %attend_5_6.2.refs_0_.own_ref, ...), custom_call_target="tpu_custom_call" | custom-call | flops 1 | bytes 1 | tf_op jit(solution)/shard_map/home/pallas_call | solution.py:315
  30.5 3.4 %collective-permute-done.10.refs_0_ = bf16[128,896]{1,0:T(8,128)(2,1)S(1)} collective-permute-done((bf16[128,896]{1,0:T(8,128)(2,1)S(1)}, bf16[128,896]{1,0:T(8,128)(2,1)S(1)}, u32[]{:S(2)}, u32[]{:S(2)}) %collective-permute-start.10) | collective-permute-done | bytes 229408 | tf_op jit(solution)/shard_map/ppermute | solution.py:361
  33.9 4.0 %collective-permute-done.11.refs_1_ = bf16[128,896]{1,0:T(8,128)(2,1)S(1)} collective-permute-done((bf16[128,896]{1,0:T(8,128)(2,1)S(1)}, bf16[128,896]{1,0:T(8,128)(2,1)S(1)}, u32[]{:S(2)}, u32[]{:S(2)}) %collective-permute-start.11) | collective-permute-done | bytes 229408 | tf_op jit(solution)/shard_map/ppermute | solution.py:361
  37.9 0.8 %close.1 = bf16[256,896]{1,0:T(8,128)(2,1)} custom-call(f32[256,896]{1,0:T(8,128)S(1)} %home.1.home_ref, bf16[128,896]{1,0:T(8,128)(2,1)S(1)} %collective-permute-done.10.refs_0_, bf16[128,896]{1,0:T(8,128)(2,1)S(1)} %collective-permute-done.11.refs_1_), custom_call_target="tpu_custom_call" | custom-call | flops 1 | bytes 1 | tf_op jit(solution)/shard_map/close/pallas_call | solution.py:345
  (11 shorter events, 0.8 us)
Async XLA Ops:
  0.0 17.5 %collective-permute-start = (bf16[896,3584]{1,0:T(8,128)(2,1)}, bf16[896,3584]{1,0:T(8,128)(2,1)}, u32[]{:S(2)}, u32[]{:S(2)}) collective-permute-start(bf16[896,3584]{1,0:T(8,128)(2,1)} %weight_hbm.1), channel_id=1, source_target_pairs={{0,1},{1,0},{2,3},{3,2},{4,5},{5,4},{6,7},{7,6},{8,9},{9,8},{10,11... | collective-permute-start | bytes 19267592 | tf_op jit(solution)/shard_map/ppermute | solution.py:361
  1.6 10.7 %collective-permute-start.1 = (bf16[512,128]{1,0:T(8,128)(2,1)S(1)}, bf16[512,128]{1,0:T(8,128)(2,1)S(1)}, u32[]{:S(2)}, u32[]{:S(2)}) collective-permute-start(bf16[512,128]{1,0:T(8,128)(2,1)S(1)} %rotate_keys.1.piece_ref), channel_id=1, source_target_pairs={{0,16},{4,20},{8,24},{12,28},{16,0},{20,4},{24,8},{28,12},{1,17},{... | collective-permute-start | bytes 393224 | tf_op jit(solution)/shard_map/ppermute | solution.py:361
  5.2 9.4 %collective-permute-start.7 = (bf16[512,128]{1,0:T(8,128)(2,1)S(1)}, bf16[512,128]{1,0:T(8,128)(2,1)S(1)}, u32[]{:S(2)}, u32[]{:S(2)}) collective-permute-start(bf16[512,128]{1,0:T(8,128)(2,1)S(1)} %rotate_keys.1.piece_ref), channel_id=1, source_target_pairs={{0,8},{4,12},{8,0},{12,4},{16,24},{20,28},{24,16},{28,20},{1,9},{5... | collective-permute-start | bytes 393224 | tf_op jit(solution)/shard_map/ppermute | solution.py:361
  6.8 8.5 %collective-permute-start.6 = (bf16[512,128]{1,0:T(8,128)(2,1)S(1)}, bf16[512,128]{1,0:T(8,128)(2,1)S(1)}, u32[]{:S(2)}, u32[]{:S(2)}) collective-permute-start(bf16[512,128]{1,0:T(8,128)(2,1)S(1)} %rotate_keys.1.piece_ref), channel_id=1, source_target_pairs={{0,4},{4,0},{8,12},{12,8},{16,20},{20,16},{24,28},{28,24},{1,5},{5... | collective-permute-start | bytes 393224 | tf_op jit(solution)/shard_map/ppermute | solution.py:361
  8.3 9.2 %collective-permute-start.5 = (bf16[512,128]{1,0:T(8,128)(2,1)S(1)}, bf16[512,128]{1,0:T(8,128)(2,1)S(1)}, u32[]{:S(2)}, u32[]{:S(2)}) collective-permute-start(bf16[512,128]{1,0:T(8,128)(2,1)S(1)} %rotate_keys.1.piece_ref), channel_id=1, source_target_pairs={{0,12},{4,8},{8,4},{12,0},{16,28},{20,24},{24,20},{28,16},{1,13},{... | collective-permute-start | bytes 393224 | tf_op jit(solution)/shard_map/ppermute | solution.py:361
  12.3 8.0 %collective-permute-start.4 = (bf16[512,128]{1,0:T(8,128)(2,1)S(1)}, bf16[512,128]{1,0:T(8,128)(2,1)S(1)}, u32[]{:S(2)}, u32[]{:S(2)}) collective-permute-start(bf16[512,128]{1,0:T(8,128)(2,1)S(1)} %collective-permute-done.1.refs_1_), channel_id=1, source_target_pairs={{0,12},{4,8},{8,4},{12,0},{16,28},{20,24},{24,20},{28,16},{1,13},{... | collective-permute-start | bytes 393224 | tf_op jit(solution)/shard_map/ppermute | solution.py:361
  14.7 6.7 %collective-permute-start.3 = (bf16[512,128]{1,0:T(8,128)(2,1)S(1)}, bf16[512,128]{1,0:T(8,128)(2,1)S(1)}, u32[]{:S(2)}, u32[]{:S(2)}) collective-permute-start(bf16[512,128]{1,0:T(8,128)(2,1)S(1)} %collective-permute-done.1.refs_1_), channel_id=1, source_target_pairs={{0,8},{4,12},{8,0},{12,4},{16,24},{20,28},{24,16},{28,20},{1,9},{5... | collective-permute-start | bytes 393224 | tf_op jit(solution)/shard_map/ppermute | solution.py:361
  15.4 6.6 %collective-permute-start.2 = (bf16[512,128]{1,0:T(8,128)(2,1)S(1)}, bf16[512,128]{1,0:T(8,128)(2,1)S(1)}, u32[]{:S(2)}, u32[]{:S(2)}) collective-permute-start(bf16[512,128]{1,0:T(8,128)(2,1)S(1)} %collective-permute-done.1.refs_1_), channel_id=1, source_target_pairs={{0,4},{4,0},{8,12},{12,8},{16,20},{20,16},{24,28},{28,24},{1,5},{5... | collective-permute-start | bytes 393224 | tf_op jit(solution)/shard_map/ppermute | solution.py:361
  22.9 1.6 %collective-permute-start.8 = (bf16[128,896]{1,0:T(8,128)(2,1)S(1)}, bf16[128,896]{1,0:T(8,128)(2,1)S(1)}, u32[]{:S(2)}, u32[]{:S(2)}) collective-permute-start(bf16[128,896]{1,0:T(8,128)(2,1)S(1)} %attend_5_6.2.refs_0_.own_ref), channel_id=1, source_target_pairs={{0,1},{1,0},{2,3},{3,2},{4,5},{5,4},{6,7},{7,6},{8,9},{9,8},{10,11... | collective-permute-start | bytes 688136 | tf_op jit(solution)/shard_map/ppermute | solution.py:361
  24.0 2.9 %collective-permute-start.9 = (bf16[128,896]{1,0:T(8,128)(2,1)S(1)}, bf16[128,896]{1,0:T(8,128)(2,1)S(1)}, u32[]{:S(2)}, u32[]{:S(2)}) collective-permute-start(bf16[128,896]{1,0:T(8,128)(2,1)S(1)} %attend_5_6.3.refs_1_.own_ref), channel_id=1, source_target_pairs={{0,1},{1,0},{2,3},{3,2},{4,5},{5,4},{6,7},{7,6},{8,9},{9,8},{10,11... | collective-permute-start | bytes 688136 | tf_op jit(solution)/shard_map/ppermute | solution.py:361
  25.3 8.5 %collective-permute-start.10 = (bf16[128,896]{1,0:T(8,128)(2,1)S(1)}, bf16[128,896]{1,0:T(8,128)(2,1)S(1)}, u32[]{:S(2)}, u32[]{:S(2)}) collective-permute-start(bf16[128,896]{1,0:T(8,128)(2,1)S(1)} %away.2), channel_id=1, source_target_pairs={{0,2},{1,3},{2,0},{3,1},{4,6},{5,7},{6,4},{7,5},{8,10},{9,11},{10,... | collective-permute-start | bytes 688136 | tf_op jit(solution)/shard_map/ppermute | solution.py:361
  27.6 10.2 %collective-permute-start.11 = (bf16[128,896]{1,0:T(8,128)(2,1)S(1)}, bf16[128,896]{1,0:T(8,128)(2,1)S(1)}, u32[]{:S(2)}, u32[]{:S(2)}) collective-permute-start(bf16[128,896]{1,0:T(8,128)(2,1)S(1)} %away.3), channel_id=1, source_target_pairs={{0,2},{1,3},{2,0},{3,1},{4,6},{5,7},{6,4},{7,5},{8,10},{9,11},{10,... | collective-permute-start | bytes 688136 | tf_op jit(solution)/shard_map/ppermute | solution.py:361

commit v4 on v3

--- a/solution.py
+++ b/solution.py
@@ -17,11 +17,11 @@
 NEG = -1e30
 SCALE = math.log2(math.e) / math.sqrt(HEAD)
 ROW_CHUNKS = (128, 128)
+TURN = 4
 FIRST = [4, 1, 2, 3]
-CALLS = [[1, 2], [3, 4], [7], [5, 6]]
+CALLS = [[0, 1], [2, 3], [4, 7], [5, 6]]
 LATER = [7, 6, 5]
-EARLY = 0
-STAGE = 1
+STAGES = [[0], [1]]
 VMEM = pltpu.MemorySpace.VMEM
 HBM = pltpu.MemorySpace.HBM
 LIMIT = 24 * 2**20
@@ -132,15 +132,10 @@
     return copies
 
 
-def begin_kernel(
-    kinds, rank_ref, place_ref, query_hbm, cos_hbm, sin_hbm, weight_hbm, piece_ref,
-    rot_ref, top_ref, acc_ref, total_ref, *refs,
-):
-    *mine, query_ref, cos_ref, sin_ref, sems, weight_sems = refs
+def turn_kernel(kinds, rank_ref, query_hbm, cos_hbm, sin_hbm, rot_ref, query_ref, cos_ref, sin_ref, sems):
     heads, block, _ = query_ref.shape
     per_span = SPAN // block
-    rank, place = rank_ref[0], place_ref[0]
-    inner = rank % per_span
+    inner = rank_ref[0] % per_span
     places = [inner, jnp.where(inner == 0, per_span, per_span + 1), per_span + 1][:kinds]
     copies = [pltpu.make_async_copy(query_hbm, query_ref, sems.at[0])]
     for kind, at in enumerate(places):
@@ -149,70 +144,58 @@
         copies.append(pltpu.make_async_copy(sin_hbm.at[rows], sin_ref.at[kind], sems.at[2 + 2 * kind]))
     for copy in copies:
         copy.start()
-    loads = column_copies(place, weight_hbm, mine, weight_sems)
-    for copy in loads:
-        copy.start()
     for copy in copies:
         copy.wait()
-    causal = lax.broadcasted_iota(jnp.int32, (block, block), 1) <= lax.broadcasted_iota(
-        jnp.int32, (block, block), 0
-    )
-    for head in range(heads):
-        for kind in range(kinds):
+
+    def turned(kind):
+        for head in range(heads):
             rot_ref[kind, head] = (
                 rotated(query_ref[head], cos_ref[kind], sin_ref[kind]) * SCALE
             ).astype(jnp.bfloat16)
-    later = scores_of([rot_ref[0, 0]], [piece_ref])
-    for head in range(heads):
-        now = later
-        if head + 1 < heads:
-            later = scores_of([rot_ref[0, head + 1]], [piece_ref])
-        now = [jnp.where(causal, now[0], NEG)]
-        top_ref[head], acc_ref[head], total_ref[head] = absorb(now, [None], [piece_ref], None)
-    for copy in loads:
-        copy.wait()
-
-
-def begin(kinds, rank, place, queries, tables, out_weight, piece):
+
+    turned(0)
+    for kind in range(1, kinds):
+        pl.when(rank_ref[0] >= kind * per_span)(functools.partial(turned, kind))
+
+
+def turn(kinds, rank, queries, tables):
     heads, block, _ = queries.shape
-    depth = out_weight.shape[0]
     smem, hbm, vmem = (pl.BlockSpec(memory_space=space) for space in (pltpu.SMEM, HBM, VMEM))
-    parts = 2
-    return pl.pallas_call(
-        functools.partial(begin_kernel, kinds),
-        in_specs=[smem, smem, hbm, hbm, hbm, hbm, vmem],
-        out_specs=[vmem] * (4 + parts),
-        out_shape=[
-            jax.ShapeDtypeStruct((kinds, heads, block, HEAD), jnp.bfloat16),
-            *[jax.ShapeDtypeStruct((heads, block, HEAD), jnp.float32)] * 3,
-            *[jax.ShapeDtypeStruct((depth, depth), jnp.bfloat16)] * parts,
-        ],
+    return pl.pallas_call(
+        functools.partial(turn_kernel, kinds),
+        in_specs=[smem, hbm, hbm, hbm],
+        out_specs=vmem,
+        out_shape=jax.ShapeDtypeStruct((kinds, heads, block, HEAD), jnp.bfloat16),
         scratch_shapes=[
             pltpu.VMEM((heads, block, HEAD), jnp.bfloat16),
             pltpu.VMEM((kinds, block, HEAD), jnp.float32),
             pltpu.VMEM((kinds, block, HEAD), jnp.float32),
             pltpu.SemaphoreType.DMA((1 + 2 * kinds,)),
-            pltpu.SemaphoreType.DMA((parts,)),
         ],
         cost_estimate=LIGHT,
         compiler_params=pltpu.CompilerParams(vmem_limit_bytes=LIMIT),
-        name="attend_0",
-    )(rank, place, *[in_hbm(x) for x in (queries, *tables, out_weight)], piece)
-
-
-def attend_kernel(offsets, kinds, last, start, rows, stages, rank_ref, rot_ref, *refs):
+        name="rotate_queries",
+    )(rank, *[in_hbm(x) for x in (queries, *tables)])
+
+
+def attend_kernel(offsets, kinds, first, last, start, rows, stages, rank_ref, rot_ref, *refs):
     pieces, refs = refs[: len(offsets)], refs[len(offsets) :]
-    old, refs = refs[:3], refs[3:]
+    old, refs = ([], refs) if first else (refs[:3], refs[3:])
     loads = []
     if stages:
-        place_ref, weight_hbm, *refs, away_ref, sems = refs
-        loads = column_copies(place_ref[0] ^ 2, weight_hbm, [away_ref], sems)
+        place_ref, *refs, sems = refs
+        weights, refs, staged = refs[:stages], refs[stages:-stages], refs[-stages:]
+        for at, (weight_hbm, ref) in enumerate(zip(weights, staged)):
+            loads += column_copies(place_ref[0] ^ 2, weight_hbm, [ref], sems.at[pl.ds(at, 1)])
     for copy in loads:
         copy.start()
     block = pieces[0].shape[0] // 2
     per_span = SPAN // block
     rank = rank_ref[0]
-    lifts = [jnp.where((rank ^ offset) <= rank, 0.0, -NEG).astype(jnp.float32) for offset in offsets]
+    lifts = [
+        jnp.where((rank ^ offset) <= rank, 0.0, -NEG).astype(jnp.float32) if offset else None
+        for offset in offsets
+    ]
     picked = []
     for offset in offsets:
         kind = min(offset // per_span, 1)
@@ -221,20 +204,45 @@
             kind = jnp.clip(back, 1, kinds - 1)
         picked.append(kind)
     here = slice(start, start + rows)
+    if 0 in offsets:
+        causal = lax.broadcasted_iota(jnp.int32, (rows, block), 1) <= start + lax.broadcasted_iota(
+            jnp.int32, (rows, block), 0
+        )
+
     def scores_at(head):
-        return scores_of([rot_ref[kind, head, here] for kind in picked], pieces)
-
-    later = scores_at(0)
-    for head in range(GROUP):
-        now = later
-        if head + 1 < GROUP:
-            later = scores_at(head + 1)
-        top, acc, total = absorb(now, lifts, pieces, [ref[head, here] for ref in old])
+        scores = scores_of([rot_ref[kind, head, here] for kind in picked], pieces)
+        return [
+            score if offset else jnp.where(causal, score, NEG)
+            for offset, score in zip(offsets, scores)
+        ]
+
+    def put(head, top, acc, total):
         if last:
-            (out_ref,) = refs
-            out_ref[:, head * HEAD : (head + 1) * HEAD] = (acc / total).astype(jnp.bfloat16)
+            refs[0][:, head * HEAD : (head + 1) * HEAD] = (acc / total).astype(jnp.bfloat16)
         else:
             refs[0][head], refs[1][head], refs[2][head] = top, acc, total
+
+    def meet():
+        later = scores_at(0)
+        for head in range(GROUP):
+            now = later
+            if head + 1 < GROUP:
+                later = scores_at(head + 1)
+            put(
+                head,
+                *absorb(now, lifts, pieces, [ref[head, here] for ref in old] or None),
+            )
+
+    def keep():
+        for head in range(GROUP):
+            put(head, *[ref[head, here] for ref in old])
+
+    if first:
+        meet()
+    else:
+        seen = functools.reduce(jnp.logical_or, [(rank ^ offset) <= rank for offset in offsets])
+        pl.when(seen)(meet)
+        pl.when(jnp.logical_not(seen))(keep)
     for copy in loads:
         copy.wait()
 
@@ -250,18 +258,28 @@
         out_shape = [jax.ShapeDtypeStruct((GROUP, rows, HEAD), jnp.float32)] * 3
     args, in_specs, scratch = [], [], []
     if stage:
-        place, weight = stage
-        depth = weight.shape[0]
-        args = [place, in_hbm(weight)]
-        in_specs = [smem, pl.BlockSpec(memory_space=HBM)]
-        out_specs = [*out_specs, vmem]
-        out_shape = [*out_shape, jax.ShapeDtypeStruct((depth, depth), jnp.bfloat16)]
-        scratch = [pltpu.SemaphoreType.DMA((1,))]
+        place, *weights = stage
+        depth = weights[0].shape[0]
+        args = [place, *[in_hbm(weight) for weight in weights]]
+        in_specs = [smem] + [pl.BlockSpec(memory_space=HBM)] * len(weights)
+        out_specs = [*out_specs, *[vmem] * len(weights)]
+        out_shape = [
+            *out_shape,
+            *[jax.ShapeDtypeStruct((depth, depth), jnp.bfloat16)] * len(weights),
+        ]
+        scratch = [pltpu.SemaphoreType.DMA((len(weights),))]
     return pl.pallas_call(
         functools.partial(
-            attend_kernel, tuple(offsets), rot.shape[0], last, start, rows, bool(stage)
+            attend_kernel,
+            tuple(offsets),
+            rot.shape[0],
+            not state,
+            last,
+            start,
+            rows,
+            len(stage[1:]),
         ),
-        in_specs=[smem] + [vmem] * (4 + len(pieces)) + in_specs,
+        in_specs=[smem] + [vmem] * (1 + len(pieces) + len(state)) + in_specs,
         scratch_shapes=scratch,
         out_specs=out_specs,
         out_shape=out_shape,
@@ -291,40 +309,43 @@
     )(own, twin, own_weight, twin_weight)
 
 
-def home_kernel(count, place_ref, twin_hbm, own_weight, *refs):
+def home_kernel(count, place_ref, own_hbm, twin_hbm, *refs):
     own_refs, twin_refs, refs = refs[:count], refs[count : 2 * count], refs[2 * count :]
-    out_ref, twin_weight, sems = refs
-    (load,) = column_copies(place_ref[0], twin_hbm, [twin_weight], sems)
-    load.start()
+    out_ref, own_weight, twin_weight, sems = refs
+    loads = []
+    for at, (hbm, ref) in enumerate(((own_hbm, own_weight), (twin_hbm, twin_weight))):
+        loads += column_copies(place_ref[0], hbm, [ref], sems.at[pl.ds(at, 1)])
+    for load in loads:
+        load.start()
+    for load in loads:
+        load.wait()
     start = 0
-    for own in own_refs:
+    for own, twin in zip(own_refs, twin_refs):
         rows = pl.ds(start, own.shape[0])
-        out_ref[rows] = jnp.dot(own[...], own_weight[...], preferred_element_type=jnp.float32)
+        out_ref[rows] = jnp.dot(
+            own[...], own_weight[...], preferred_element_type=jnp.float32
+        ) + jnp.dot(twin[...], twin_weight[...], preferred_element_type=jnp.float32)
         start += own.shape[0]
-    load.wait()
-    start = 0
-    for twin in twin_refs:
-        rows = pl.ds(start, twin.shape[0])
-        out_ref[rows] += jnp.dot(twin[...], twin_weight[...], preferred_element_type=jnp.float32)
-        start += twin.shape[0]
 
 
 def project_home(place, own, twin, own_weight, twin_weight):
     smem, hbm, vmem = (pl.BlockSpec(memory_space=space) for space in (pltpu.SMEM, HBM, VMEM))
     rows = sum(x.shape[0] for x in own)
+    depth = own_weight.shape[0]
     return pl.pallas_call(
         functools.partial(home_kernel, len(own)),
-        in_specs=[smem, hbm] + [vmem] * (2 * len(own) + 1),
+        in_specs=[smem, hbm, hbm] + [vmem] * (2 * len(own)),
         out_specs=vmem,
-        out_shape=jax.ShapeDtypeStruct((rows, own_weight.shape[1]), jnp.float32),
+        out_shape=jax.ShapeDtypeStruct((rows, depth), jnp.float32),
         scratch_shapes=[
-            pltpu.VMEM(own_weight.shape, jnp.bfloat16),
-            pltpu.SemaphoreType.DMA((1,)),
+            pltpu.VMEM((depth, depth), jnp.bfloat16),
+            pltpu.VMEM((depth, depth), jnp.bfloat16),
+            pltpu.SemaphoreType.DMA((2,)),
         ],
         cost_estimate=LIGHT,
         compiler_params=pltpu.CompilerParams(vmem_limit_bytes=LIMIT),
         name="home",
-    )(place, in_hbm(twin_weight), own_weight, *own, *twin)
+    )(place, in_hbm(own_weight), in_hbm(twin_weight), *own, *twin)
 
 
 def close_kernel(home_ref, *refs):
@@ -382,10 +403,7 @@
         twin_weight = swap(out_weight, "kv", kv, 1)
         for offset in FIRST:
             send(offset, offset)
-        rot, *state = begin(
-            kinds, rank, place, by_head, tables, out_weight, pieces[0]
-        )
-        state, mine = state[:3], state[3:]
+        rot = turn(kinds, rank, by_head, tables)
         for offset in range(2 * per_span, seq, per_span):
             send(offset, offset & -offset)
             for low in range(1, per_span):
@@ -395,13 +413,13 @@
         def blocks(offsets, state, *how):
             return attend(rank, offsets, rot, [pieces[o] for o in offsets], state, *how)
 
-        for at, offsets in enumerate(calls[:-1]):
-            if at == EARLY:
-                for offset in LATER:
-                    send(offset, offset % per_span, state[0])
-            state = blocks(offsets, state, False, 0, block, (place, twin_weight) if at == STAGE else ())
-            if at == STAGE:
-                state, theirs = state[:3], state[3]
+        for offset in LATER:
+            send(offset, offset ^ TURN, rot)
+        state, staged = [], []
+        for offsets, weights in zip(calls[:-1], STAGES + [[]] * len(calls)):
+            stage = (place, *[(out_weight, twin_weight)[at] for at in weights]) if weights else ()
+            state = blocks(offsets, state, False, 0, block, stage)
+            state, staged = state[:3], staged + list(state[3:])
         own, twin, start = [], [], 0
         for rows in ROW_CHUNKS:
             own.append(blocks(calls[-1], state, True, start, rows))
@@ -410,10 +428,10 @@
         landed = []
         for rows in zip(own, twin):
             away = project(
-                *rows, mine[1], theirs, jnp.bfloat16, "away"
+                *rows, *staged, jnp.bfloat16, "away"
             )
             landed.append(swap(away, "kv", kv, 2))
-        home = project_home(place, own, twin, mine[0], twin_weight)
+        home = project_home(place, own, twin, out_weight, twin_weight)
         return close(home, landed)
 
     return shards

time: 38.9 us -> 38.3 us (0.985)
  Pallas kernels: 16.3 us -> 12.5 us
  waiting for transfers between devices: 8.31 us -> 11.9 us
  starting transfers between devices: 14 us -> 13.6 us
    ppermute x12, waiting for transfers between devices: 8.31 us -> 11.9 us  [swap(): return lax.ppermute(x, axis, [(i, i ^ bits) for i in range(size)])]
    pallas_call x5, Pallas kernels: 7.37 us -> 4.28 us  [attend(): pl.pallas_call(functools.partial(attend_kernel, tuple(offsets), rot.shape...]
    pallas_call x1, Pallas kernels: 3.3 us -> 1.47 us  [turn(): pl.pallas_call(functools.partial(turn_kernel, kinds), in_specs=[smem, hbm...]
    pallas_call x1, Pallas kernels: 2.21 us -> 3.24 us  [project_home(): pl.pallas_call(functools.partial(home_kernel, len(own)), in_specs=[smem,...]
  transfers between devices with their start and end apart: 12 -> 12, of which waited for: 4 -> 8; matrix products, arithmetic and copies ran while one was open for 0% -> 0% of each run, Pallas kernels for 37% -> 30%
where the time goes in v4:
time: 38.3 us; the launch traced here: 38.1 us
  starting transfers between devices  13.6 us (36%)
  Pallas kernels  12.5 us (33%)
  waiting for transfers between devices  11.9 us (31%)
    ppermute x12, starting transfers between devices, swap(): return lax.ppermute(x, axis, [(i, i ^ bits) for i in range(size)])  13.6 us
    ppermute x12, waiting for transfers between devices, swap(): return lax.ppermute(x, axis, [(i, i ^ bits) for i in range(size)])  11.9 us
    pallas_call x5, Pallas kernels, attend(): pl.pallas_call(functools.partial(attend_kernel, tuple(offsets), rot.shape...  4.28 us
    pallas_call x1, Pallas kernels, project_home(): pl.pallas_call(functools.partial(home_kernel, len(own)), in_specs=[smem,...  3.24 us
    pallas_call x2, Pallas kernels, project(): pl.pallas_call(project_kernel, in_specs=[vmem] * 4, out_specs=vmem, out_s...  1.49 us
    pallas_call x1, Pallas kernels, turn(): pl.pallas_call(functools.partial(turn_kernel, kinds), in_specs=[smem, hbm...  1.47 us
    pallas_call x1, Pallas kernels, prepare(): pl.pallas_call(prepare_kernel, in_specs=[pl.BlockSpec(memory_space=pltpu....  1.13 us
    pallas_call x1, Pallas kernels, close(): pl.pallas_call(close_kernel, in_specs=[vmem] * (1 + len(landed)), out_spe...  0.84 us
  transfers between devices with their start and end apart: 12, of which 8 were waited for; matrix products, arithmetic and copies ran while one was open for 0% of the time, Pallas kernels for 30%

profile of v4, /device:TPU:0, one launch (start us, length us, event | category | flops | bytes accessed | tf_op | source)
XLA Modules:
  0.0 38.1 jit_solution(3194269363849585606)
XLA Ops:
  0.0 0.5 %collective-permute-start = (bf16[896,3584]{1,0:T(8,128)(2,1)}, bf16[896,3584]{1,0:T(8,128)(2,1)}, u32[]{:S(2)}, u32[]{:S(2)}) collective-permute-start(bf16[896,3584]{1,0:T(8,128)(2,1)} %own_hbm.1), channel_id=1, source_target_pairs={{0,1},{1,0},{2,3},{3,2},{4,5},{5,4},{6,7},{7,6},{8,9},{9,8},{10,11... | collective-permute-start | bytes 19267592 | tf_op jit(solution)/shard_map/ppermute | solution.py:382
  0.5 1.1 %rotate_keys.1.refs_0_ = bf16[512,128]{1,0:T(8,128)(2,1)S(1)} custom-call(s32[1]{0:T(128)} %bitcast.1.rank_ref, bf16[256,128]{1,0:T(8,128)(2,1)} %bitcast.6, bf16[256,128]{1,0:T(8,128)(2,1)} %bitcast.7, f32[1536,128]{1,0:T(8,128)} %constant.13.clone.cos_hbm, f32[1536,128]{1,0:T(8,128)} %constant.14.clone.sin_hbm), custom_call_target="tpu_custom_call" | custom-call | tf_op jit(solution)/shard_map/rotate_keys/pallas_call | solution.py:71
  1.6 3.7 %collective-permute-start.1 = (bf16[512,128]{1,0:T(8,128)(2,1)S(1)}, bf16[512,128]{1,0:T(8,128)(2,1)S(1)}, u32[]{:S(2)}, u32[]{:S(2)}) collective-permute-start(bf16[512,128]{1,0:T(8,128)(2,1)S(1)} %rotate_keys.1.refs_0_), channel_id=1, source_target_pairs={{0,16},{4,20},{8,24},{12,28},{16,0},{20,4},{24,8},{28,12},{1,17},{... | collective-permute-start | bytes 393224 | tf_op jit(solution)/shard_map/ppermute | solution.py:382
  5.2 1.5 %collective-permute-start.7 = (bf16[512,128]{1,0:T(8,128)(2,1)S(1)}, bf16[512,128]{1,0:T(8,128)(2,1)S(1)}, u32[]{:S(2)}, u32[]{:S(2)}) collective-permute-start(bf16[512,128]{1,0:T(8,128)(2,1)S(1)} %rotate_keys.1.refs_0_), channel_id=1, source_target_pairs={{0,4},{4,0},{8,12},{12,8},{16,20},{20,16},{24,28},{28,24},{1,5},{5... | collective-permute-start | bytes 393224 | tf_op jit(solution)/shard_map/ppermute | solution.py:382
  6.8 1.6 %collective-permute-start.5 = (bf16[512,128]{1,0:T(8,128)(2,1)S(1)}, bf16[512,128]{1,0:T(8,128)(2,1)S(1)}, u32[]{:S(2)}, u32[]{:S(2)}) collective-permute-start(bf16[512,128]{1,0:T(8,128)(2,1)S(1)} %rotate_keys.1.refs_0_), channel_id=1, source_target_pairs={{0,8},{4,12},{8,0},{12,4},{16,24},{20,28},{24,16},{28,20},{1,9},{5... | collective-permute-start | bytes 393224 | tf_op jit(solution)/shard_map/ppermute | solution.py:382
  8.3 0.4 %collective-permute-start.6 = (bf16[512,128]{1,0:T(8,128)(2,1)S(1)}, bf16[512,128]{1,0:T(8,128)(2,1)S(1)}, u32[]{:S(2)}, u32[]{:S(2)}) collective-permute-start(bf16[512,128]{1,0:T(8,128)(2,1)S(1)} %rotate_keys.1.refs_0_), channel_id=1, source_target_pairs={{0,12},{4,8},{8,4},{12,0},{16,28},{20,24},{24,20},{28,16},{1,13},{... | collective-permute-start | bytes 393224 | tf_op jit(solution)/shard_map/ppermute | solution.py:382
  8.7 1.5 %rotate_queries.1.rot_ref = bf16[2,7,256,128]{3,2,1,0:T(8,128)(2,1)S(1)} custom-call(s32[1]{0:T(128)} %bitcast.1.rank_ref, bf16[7,256,128]{2,1,0:T(8,128)(2,1)} %bitcast.5, f32[1536,128]{1,0:T(8,128)} %constant.13.clone.cos_hbm, f32[1536,128]{1,0:T(8,128)} %constant.14.clone.sin_hbm), custom_call_target="tpu_custom_call" | custom-call | flops 1 | bytes 1 | tf_op jit(solution)/shard_map/rotate_queries/pallas_call | solution.py:164
  10.2 2.1 %collective-permute-done.1.refs_0_ = bf16[512,128]{1,0:T(8,128)(2,1)S(1)} collective-permute-done((bf16[512,128]{1,0:T(8,128)(2,1)S(1)}, bf16[512,128]{1,0:T(8,128)(2,1)S(1)}, u32[]{:S(2)}, u32[]{:S(2)}) %collective-permute-start.1) | collective-permute-done | bytes 131104 | tf_op jit(solution)/shard_map/ppermute | solution.py:382
  12.3 1.6 %collective-permute-start.4 = (bf16[512,128]{1,0:T(8,128)(2,1)S(1)}, bf16[512,128]{1,0:T(8,128)(2,1)S(1)}, u32[]{:S(2)}, u32[]{:S(2)}) collective-permute-start(bf16[512,128]{1,0:T(8,128)(2,1)S(1)} %collective-permute-done.1.refs_0_), channel_id=1, source_target_pairs={{0,12},{4,8},{8,4},{12,0},{16,28},{20,24},{24,20},{28,16},{1,13},{... | collective-permute-start | bytes 393224 | tf_op jit(solution)/shard_map/ppermute | solution.py:382
  14.0 0.5 %collective-permute-start.2 = (bf16[512,128]{1,0:T(8,128)(2,1)S(1)}, bf16[512,128]{1,0:T(8,128)(2,1)S(1)}, u32[]{:S(2)}, u32[]{:S(2)}) collective-permute-start(bf16[512,128]{1,0:T(8,128)(2,1)S(1)} %collective-permute-done.1.refs_0_), channel_id=1, source_target_pairs={{0,4},{4,0},{8,12},{12,8},{16,20},{20,16},{24,28},{28,24},{1,5},{5... | collective-permute-start | bytes 393224 | tf_op jit(solution)/shard_map/ppermute | solution.py:382
  14.7 1.1 %collective-permute-start.3 = (bf16[512,128]{1,0:T(8,128)(2,1)S(1)}, bf16[512,128]{1,0:T(8,128)(2,1)S(1)}, u32[]{:S(2)}, u32[]{:S(2)}) collective-permute-start(bf16[512,128]{1,0:T(8,128)(2,1)S(1)} %collective-permute-done.1.refs_0_), channel_id=1, source_target_pairs={{0,8},{4,12},{8,0},{12,4},{16,24},{20,28},{24,16},{28,20},{1,9},{5... | collective-permute-start | bytes 393224 | tf_op jit(solution)/shard_map/ppermute | solution.py:382
  15.8 2.5 %attend_0_1.1 = (f32[7,256,128]{2,1,0:T(8,128)S(1)}, f32[7,256,128]{2,1,0:T(8,128)S(1)}, f32[7,256,128]{2,1,0:T(8,128)S(1)}, bf16[896,896]{1,0:T(8,128)(2,1)S(1)}) custom-call(s32[1]{0:T(128)} %bitcast.1.rank_ref, bf16[2,7,256,128]{3,2,1,0:T(8,128)(2,1)S(1)} %rotate_queries.1.rot_ref, bf16[512,128]{1,0:T(8,128)(2,1)S(1)} %rotate_keys.1.refs_0_, ...), custom_call_target="tpu_custom_call" | custom-call | flops 1 | bytes 1 | tf_op jit(solution)/shard_map/attend_0_1/pallas_call | solution.py:271
  18.4 1.4 %attend_2_3.1 = (f32[7,256,128]{2,1,0:T(8,128)S(1)}, f32[7,256,128]{2,1,0:T(8,128)S(1)}, f32[7,256,128]{2,1,0:T(8,128)S(1)}, bf16[896,896]{1,0:T(8,128)(2,1)S(1)}) custom-call(s32[1]{0:T(128)} %bitcast.1.rank_ref, bf16[2,7,256,128]{3,2,1,0:T(8,128)(2,1)S(1)} %rotate_queries.1.rot_ref, bf16[512,128]{1,0:T(8,128)(2,1)S(1)} %collective-permute-done.5.refs_0_, ...), custom_call_target="tpu_custom_call" | custom-call | flops 1 | bytes 1 | tf_op jit(solution)/shard_map/attend_2_3/pallas_call | solution.py:271
  20.3 1.9 %collective-permute-done.2.refs_0_ = bf16[512,128]{1,0:T(8,128)(2,1)S(1)} collective-permute-done((bf16[512,128]{1,0:T(8,128)(2,1)S(1)}, bf16[512,128]{1,0:T(8,128)(2,1)S(1)}, u32[]{:S(2)}, u32[]{:S(2)}) %collective-permute-start.2) | collective-permute-done | bytes 131104 | tf_op jit(solution)/shard_map/ppermute | solution.py:382
  22.5 0.5 %collective-permute-start.8 = (bf16[128,896]{1,0:T(8,128)(2,1)S(1)}, bf16[128,896]{1,0:T(8,128)(2,1)S(1)}, u32[]{:S(2)}, u32[]{:S(2)}) collective-permute-start(bf16[128,896]{1,0:T(8,128)(2,1)S(1)} %attend_5_6.2.refs_0_.own_ref), channel_id=1, source_target_pairs={{0,1},{1,0},{2,3},{3,2},{4,5},{5,4},{6,7},{7,6},{8,9},{9,8},{10,11... | collective-permute-start | bytes 688136 | tf_op jit(solution)/shard_map/ppermute | solution.py:382
  23.0 0.8 %collective-permute-done.9.refs_3_.twin_ref = bf16[128,896]{1,0:T(8,128)(2,1)S(1)} collective-permute-done((bf16[128,896]{1,0:T(8,128)(2,1)S(1)}, bf16[128,896]{1,0:T(8,128)(2,1)S(1)}, u32[]{:S(2)}, u32[]{:S(2)}) %collective-permute-start.9) | collective-permute-done | bytes 229408 | tf_op jit(solution)/shard_map/ppermute | solution.py:382
  23.9 0.7 %away.3 = bf16[128,896]{1,0:T(8,128)(2,1)S(1)} custom-call(bf16[128,896]{1,0:T(8,128)(2,1)S(1)} %attend_5_6.3.refs_1_.own_ref, bf16[128,896]{1,0:T(8,128)(2,1)S(1)} %collective-permute-done.9.refs_3_.twin_ref, bf16[896,896]{1,0:T(8,128)(2,1)S(1)} %get-tuple-element.27.own_weight, bf16[896,896]{1,0:T(8,128)(2,1)S(1)} %get-tuple-element.28.twin_weight), custom_call_target="tpu_custom_call" | custom-call | flops 1 | bytes 1 | tf_op jit(solution)/shard_map/away/pallas_call | solution.py:301
  24.6 1.6 %collective-permute-start.11 = (bf16[128,896]{1,0:T(8,128)(2,1)S(1)}, bf16[128,896]{1,0:T(8,128)(2,1)S(1)}, u32[]{:S(2)}, u32[]{:S(2)}) collective-permute-start(bf16[128,896]{1,0:T(8,128)(2,1)S(1)} %away.3), channel_id=1, source_target_pairs={{0,2},{1,3},{2,0},{3,1},{4,6},{5,7},{6,4},{7,5},{8,10},{9,11},{10,... | collective-permute-start | bytes 688136 | tf_op jit(solution)/shard_map/ppermute | solution.py:382
  26.2 0.7 %away.2 = bf16[128,896]{1,0:T(8,128)(2,1)S(1)} custom-call(bf16[128,896]{1,0:T(8,128)(2,1)S(1)} %attend_5_6.2.refs_0_.own_ref, bf16[128,896]{1,0:T(8,128)(2,1)S(1)} %collective-permute-done.8.refs_2_.twin_ref, bf16[896,896]{1,0:T(8,128)(2,1)S(1)} %get-tuple-element.27.own_weight, bf16[896,896]{1,0:T(8,128)(2,1)S(1)} %get-tuple-element.28.twin_weight), custom_call_target="tpu_custom_call" | custom-call | flops 1 | bytes 1 | tf_op jit(solution)/shard_map/away/pallas_call | solution.py:301
  27.0 0.5 %collective-permute-start.10 = (bf16[128,896]{1,0:T(8,128)(2,1)S(1)}, bf16[128,896]{1,0:T(8,128)(2,1)S(1)}, u32[]{:S(2)}, u32[]{:S(2)}) collective-permute-start(bf16[128,896]{1,0:T(8,128)(2,1)S(1)} %away.2), channel_id=1, source_target_pairs={{0,2},{1,3},{2,0},{3,1},{4,6},{5,7},{6,4},{7,5},{8,10},{9,11},{10,... | collective-permute-start | bytes 688136 | tf_op jit(solution)/shard_map/ppermute | solution.py:382
  27.5 3.2 %home.1.home_ref = f32[256,896]{1,0:T(8,128)S(1)} custom-call(s32[1]{0:T(128)} %bitcast.refs_2_.refs_5_.place_ref, bf16[896,3584]{1,0:T(8,128)(2,1)} %own_hbm.1, bf16[896,3584]{1,0:T(8,128)(2,1)} %collective-permute-done.refs_6_.twin_hbm, bf16[128,896]{1,0:T(8,128)(2,1)S(1)} %attend_5_6.2.refs_0_.own_ref, bf16[128,896]{1,0:T(8,128)(2,1)S(1)} %attend_5_6.3.refs_1_.own_ref, ...), custom_call_target="tpu_custom_call" | custom-call | flops 1 | bytes 1 | tf_op jit(solution)/shard_map/home/pallas_call | solution.py:335
  30.8 2.4 %collective-permute-done.11.refs_1_ = bf16[128,896]{1,0:T(8,128)(2,1)S(1)} collective-permute-done((bf16[128,896]{1,0:T(8,128)(2,1)S(1)}, bf16[128,896]{1,0:T(8,128)(2,1)S(1)}, u32[]{:S(2)}, u32[]{:S(2)}) %collective-permute-start.11) | collective-permute-done | bytes 229408 | tf_op jit(solution)/shard_map/ppermute | solution.py:382
  33.1 4.1 %collective-permute-done.10.refs_0_ = bf16[128,896]{1,0:T(8,128)(2,1)S(1)} collective-permute-done((bf16[128,896]{1,0:T(8,128)(2,1)S(1)}, bf16[128,896]{1,0:T(8,128)(2,1)S(1)}, u32[]{:S(2)}, u32[]{:S(2)}) %collective-permute-start.10) | collective-permute-done | bytes 229408 | tf_op jit(solution)/shard_map/ppermute | solution.py:382
  37.2 0.8 %close.1 = bf16[256,896]{1,0:T(8,128)(2,1)} custom-call(f32[256,896]{1,0:T(8,128)S(1)} %home.1.home_ref, bf16[128,896]{1,0:T(8,128)(2,1)S(1)} %collective-permute-done.10.refs_0_, bf16[128,896]{1,0:T(8,128)(2,1)S(1)} %collective-permute-done.11.refs_1_), custom_call_target="tpu_custom_call" | custom-call | flops 1 | bytes 1 | tf_op jit(solution)/shard_map/close/pallas_call | solution.py:366
  (11 shorter events, 1.0 us)
Async XLA Ops:
  0.0 18.4 %collective-permute-start = (bf16[896,3584]{1,0:T(8,128)(2,1)}, bf16[896,3584]{1,0:T(8,128)(2,1)}, u32[]{:S(2)}, u32[]{:S(2)}) collective-permute-start(bf16[896,3584]{1,0:T(8,128)(2,1)} %own_hbm.1), channel_id=1, source_target_pairs={{0,1},{1,0},{2,3},{3,2},{4,5},{5,4},{6,7},{7,6},{8,9},{9,8},{10,11... | collective-permute-start | bytes 19267592 | tf_op jit(solution)/shard_map/ppermute | solution.py:382
  1.6 10.7 %collective-permute-start.1 = (bf16[512,128]{1,0:T(8,128)(2,1)S(1)}, bf16[512,128]{1,0:T(8,128)(2,1)S(1)}, u32[]{:S(2)}, u32[]{:S(2)}) collective-permute-start(bf16[512,128]{1,0:T(8,128)(2,1)S(1)} %rotate_keys.1.refs_0_), channel_id=1, source_target_pairs={{0,16},{4,20},{8,24},{12,28},{16,0},{20,4},{24,8},{28,12},{1,17},{... | collective-permute-start | bytes 393224 | tf_op jit(solution)/shard_map/ppermute | solution.py:382
  5.2 8.7 %collective-permute-start.7 = (bf16[512,128]{1,0:T(8,128)(2,1)S(1)}, bf16[512,128]{1,0:T(8,128)(2,1)S(1)}, u32[]{:S(2)}, u32[]{:S(2)}) collective-permute-start(bf16[512,128]{1,0:T(8,128)(2,1)S(1)} %rotate_keys.1.refs_0_), channel_id=1, source_target_pairs={{0,4},{4,0},{8,12},{12,8},{16,20},{20,16},{24,28},{28,24},{1,5},{5... | collective-permute-start | bytes 393224 | tf_op jit(solution)/shard_map/ppermute | solution.py:382
  6.8 8.0 %collective-permute-start.5 = (bf16[512,128]{1,0:T(8,128)(2,1)S(1)}, bf16[512,128]{1,0:T(8,128)(2,1)S(1)}, u32[]{:S(2)}, u32[]{:S(2)}) collective-permute-start(bf16[512,128]{1,0:T(8,128)(2,1)S(1)} %rotate_keys.1.refs_0_), channel_id=1, source_target_pairs={{0,8},{4,12},{8,0},{12,4},{16,24},{20,28},{24,16},{28,20},{1,9},{5... | collective-permute-start | bytes 393224 | tf_op jit(solution)/shard_map/ppermute | solution.py:382
  8.3 10.0 %collective-permute-start.6 = (bf16[512,128]{1,0:T(8,128)(2,1)S(1)}, bf16[512,128]{1,0:T(8,128)(2,1)S(1)}, u32[]{:S(2)}, u32[]{:S(2)}) collective-permute-start(bf16[512,128]{1,0:T(8,128)(2,1)S(1)} %rotate_keys.1.refs_0_), channel_id=1, source_target_pairs={{0,12},{4,8},{8,4},{12,0},{16,28},{20,24},{24,20},{28,16},{1,13},{... | collective-permute-start | bytes 393224 | tf_op jit(solution)/shard_map/ppermute | solution.py:382
  12.3 7.8 %collective-permute-start.4 = (bf16[512,128]{1,0:T(8,128)(2,1)S(1)}, bf16[512,128]{1,0:T(8,128)(2,1)S(1)}, u32[]{:S(2)}, u32[]{:S(2)}) collective-permute-start(bf16[512,128]{1,0:T(8,128)(2,1)S(1)} %collective-permute-done.1.refs_0_), channel_id=1, source_target_pairs={{0,12},{4,8},{8,4},{12,0},{16,28},{20,24},{24,20},{28,16},{1,13},{... | collective-permute-start | bytes 393224 | tf_op jit(solution)/shard_map/ppermute | solution.py:382
  14.0 8.2 %collective-permute-start.2 = (bf16[512,128]{1,0:T(8,128)(2,1)S(1)}, bf16[512,128]{1,0:T(8,128)(2,1)S(1)}, u32[]{:S(2)}, u32[]{:S(2)}) collective-permute-start(bf16[512,128]{1,0:T(8,128)(2,1)S(1)} %collective-permute-done.1.refs_0_), channel_id=1, source_target_pairs={{0,4},{4,0},{8,12},{12,8},{16,20},{20,16},{24,28},{28,24},{1,5},{5... | collective-permute-start | bytes 393224 | tf_op jit(solution)/shard_map/ppermute | solution.py:382
  14.7 7.5 %collective-permute-start.3 = (bf16[512,128]{1,0:T(8,128)(2,1)S(1)}, bf16[512,128]{1,0:T(8,128)(2,1)S(1)}, u32[]{:S(2)}, u32[]{:S(2)}) collective-permute-start(bf16[512,128]{1,0:T(8,128)(2,1)S(1)} %collective-permute-done.1.refs_0_), channel_id=1, source_target_pairs={{0,8},{4,12},{8,0},{12,4},{16,24},{20,28},{24,16},{28,20},{1,9},{5... | collective-permute-start | bytes 393224 | tf_op jit(solution)/shard_map/ppermute | solution.py:382
  22.3 1.6 %collective-permute-start.9 = (bf16[128,896]{1,0:T(8,128)(2,1)S(1)}, bf16[128,896]{1,0:T(8,128)(2,1)S(1)}, u32[]{:S(2)}, u32[]{:S(2)}) collective-permute-start(bf16[128,896]{1,0:T(8,128)(2,1)S(1)} %attend_5_6.3.refs_1_.own_ref), channel_id=1, source_target_pairs={{0,1},{1,0},{2,3},{3,2},{4,5},{5,4},{6,7},{7,6},{8,9},{9,8},{10,11... | collective-permute-start | bytes 688136 | tf_op jit(solution)/shard_map/ppermute | solution.py:382
  22.5 3.7 %collective-permute-start.8 = (bf16[128,896]{1,0:T(8,128)(2,1)S(1)}, bf16[128,896]{1,0:T(8,128)(2,1)S(1)}, u32[]{:S(2)}, u32[]{:S(2)}) collective-permute-start(bf16[128,896]{1,0:T(8,128)(2,1)S(1)} %attend_5_6.2.refs_0_.own_ref), channel_id=1, source_target_pairs={{0,1},{1,0},{2,3},{3,2},{4,5},{5,4},{6,7},{7,6},{8,9},{9,8},{10,11... | collective-permute-start | bytes 688136 | tf_op jit(solution)/shard_map/ppermute | solution.py:382
  24.6 8.5 %collective-permute-start.11 = (bf16[128,896]{1,0:T(8,128)(2,1)S(1)}, bf16[128,896]{1,0:T(8,128)(2,1)S(1)}, u32[]{:S(2)}, u32[]{:S(2)}) collective-permute-start(bf16[128,896]{1,0:T(8,128)(2,1)S(1)} %away.3), channel_id=1, source_target_pairs={{0,2},{1,3},{2,0},{3,1},{4,6},{5,7},{6,4},{7,5},{8,10},{9,11},{10,... | collective-permute-start | bytes 688136 | tf_op jit(solution)/shard_map/ppermute | solution.py:382
  27.0 10.3 %collective-permute-start.10 = (bf16[128,896]{1,0:T(8,128)(2,1)S(1)}, bf16[128,896]{1,0:T(8,128)(2,1)S(1)}, u32[]{:S(2)}, u32[]{:S(2)}) collective-permute-start(bf16[128,896]{1,0:T(8,128)(2,1)S(1)} %away.2), channel_id=1, source_target_pairs={{0,2},{1,3},{2,0},{3,1},{4,6},{5,7},{6,4},{7,5},{8,10},{9,11},{10,... | collective-permute-start | bytes 688136 | tf_op jit(solution)/shard_map/ppermute | solution.py:382

commit v5 on v4

--- a/solution.py
+++ b/solution.py
@@ -17,11 +17,11 @@
 NEG = -1e30
 SCALE = math.log2(math.e) / math.sqrt(HEAD)
 ROW_CHUNKS = (128, 128)
-TURN = 4
-FIRST = [4, 1, 2, 3]
-CALLS = [[0, 1], [2, 3], [4, 7], [5, 6]]
-LATER = [7, 6, 5]
-STAGES = [[0], [1]]
+TURN = 6
+FIRST = [6, 1, 2, 3]
+CALLS = [[1, 2], [3, 6], [5], [4, 7]]
+LATER = [5, 4, 7]
+STAGES = [[], [1]]
 VMEM = pltpu.MemorySpace.VMEM
 HBM = pltpu.MemorySpace.HBM
 LIMIT = 24 * 2**20
@@ -132,10 +132,15 @@
     return copies
 
 
-def turn_kernel(kinds, rank_ref, query_hbm, cos_hbm, sin_hbm, rot_ref, query_ref, cos_ref, sin_ref, sems):
+def begin_kernel(
+    kinds, rank_ref, place_ref, query_hbm, cos_hbm, sin_hbm, weight_hbm, piece_ref,
+    rot_ref, top_ref, acc_ref, total_ref, *refs,
+):
+    away_ref, query_ref, cos_ref, sin_ref, sems, weight_sems = refs
     heads, block, _ = query_ref.shape
     per_span = SPAN // block
-    inner = rank_ref[0] % per_span
+    rank, place = rank_ref[0], place_ref[0]
+    inner = rank % per_span
     places = [inner, jnp.where(inner == 0, per_span, per_span + 1), per_span + 1][:kinds]
     copies = [pltpu.make_async_copy(query_hbm, query_ref, sems.at[0])]
     for kind, at in enumerate(places):
@@ -144,38 +149,58 @@
         copies.append(pltpu.make_async_copy(sin_hbm.at[rows], sin_ref.at[kind], sems.at[2 + 2 * kind]))
     for copy in copies:
         copy.start()
+    loads = column_copies(place ^ 2, weight_hbm, [away_ref], weight_sems)
+    for copy in loads:
+        copy.start()
     for copy in copies:
         copy.wait()
-
-    def turned(kind):
+    causal = lax.broadcasted_iota(jnp.int32, (block, block), 1) <= lax.broadcasted_iota(
+        jnp.int32, (block, block), 0
+    )
+    def turn(kind):
         for head in range(heads):
             rot_ref[kind, head] = (
                 rotated(query_ref[head], cos_ref[kind], sin_ref[kind]) * SCALE
             ).astype(jnp.bfloat16)
 
-    turned(0)
+    turn(0)
     for kind in range(1, kinds):
-        pl.when(rank_ref[0] >= kind * per_span)(functools.partial(turned, kind))
-
-
-def turn(kinds, rank, queries, tables):
+        pl.when(rank >= kind * per_span)(functools.partial(turn, kind))
+    later = scores_of([rot_ref[0, 0]], [piece_ref])
+    for head in range(heads):
+        now = later
+        if head + 1 < heads:
+            later = scores_of([rot_ref[0, head + 1]], [piece_ref])
+        now = [jnp.where(causal, now[0], NEG)]
+        top_ref[head], acc_ref[head], total_ref[head] = absorb(now, [None], [piece_ref], None)
+    for copy in loads:
+        copy.wait()
+
+
+def begin(kinds, rank, place, queries, tables, out_weight, piece):
     heads, block, _ = queries.shape
+    depth = out_weight.shape[0]
     smem, hbm, vmem = (pl.BlockSpec(memory_space=space) for space in (pltpu.SMEM, HBM, VMEM))
     return pl.pallas_call(
-        functools.partial(turn_kernel, kinds),
-        in_specs=[smem, hbm, hbm, hbm],
-        out_specs=vmem,
-        out_shape=jax.ShapeDtypeStruct((kinds, heads, block, HEAD), jnp.bfloat16),
+        functools.partial(begin_kernel, kinds),
+        in_specs=[smem, smem, hbm, hbm, hbm, hbm, vmem],
+        out_specs=[vmem] * 5,
+        out_shape=[
+            jax.ShapeDtypeStruct((kinds, heads, block, HEAD), jnp.bfloat16),
+            *[jax.ShapeDtypeStruct((heads, block, HEAD), jnp.float32)] * 3,
+            jax.ShapeDtypeStruct((depth, depth), jnp.bfloat16),
+        ],
         scratch_shapes=[
             pltpu.VMEM((heads, block, HEAD), jnp.bfloat16),
             pltpu.VMEM((kinds, block, HEAD), jnp.float32),
             pltpu.VMEM((kinds, block, HEAD), jnp.float32),
             pltpu.SemaphoreType.DMA((1 + 2 * kinds,)),
+            pltpu.SemaphoreType.DMA((1,)),
         ],
         cost_estimate=LIGHT,
         compiler_params=pltpu.CompilerParams(vmem_limit_bytes=LIMIT),
-        name="rotate_queries",
-    )(rank, *[in_hbm(x) for x in (queries, *tables)])
+        name="attend_0",
+    )(rank, place, *[in_hbm(x) for x in (queries, *tables, out_weight)], piece)
 
 
 def attend_kernel(offsets, kinds, first, last, start, rows, stages, rank_ref, rot_ref, *refs):
@@ -382,6 +407,15 @@
     return lax.ppermute(x, axis, [(i, i ^ bits) for i in range(size)])
 
 
+def swap_late(x, seq, kv, bits):
+    pairs = []
+    for rank in range(seq):
+        for place in range(kv):
+            to = (rank ^ bits, place) if 2 * rank >= seq else (rank, place ^ 1)
+            pairs.append((rank * kv + place, to[0] * kv + to[1]))
+    return lax.ppermute(x, ("seq", "kv"), pairs)
+
+
 def after(x, *others):
     return lax.optimization_barrier((x, *others))[0]
 
@@ -400,10 +434,18 @@
         def send(offset, step, *others):
             pieces[offset] = swap(after(pieces[offset ^ step], *others), "seq", seq, step)
 
+        def pass_on(offset, step, *others):
+            source = after(pieces[offset ^ step], *others)
+            late = 2 * offset >= seq
+            pieces[offset] = swap_late(source, seq, kv, step) if late else swap(source, "seq", seq, step)
+
         twin_weight = swap(out_weight, "kv", kv, 1)
         for offset in FIRST:
             send(offset, offset)
-        rot = turn(kinds, rank, by_head, tables)
+        rot, *state = begin(
+            kinds, rank, place, by_head, tables, out_weight, pieces[0]
+        )
+        state, staged = state[:3], state[3:]
         for offset in range(2 * per_span, seq, per_span):
             send(offset, offset & -offset)
             for low in range(1, per_span):
@@ -414,8 +456,7 @@
             return attend(rank, offsets, rot, [pieces[o] for o in offsets], state, *how)
 
         for offset in LATER:
-            send(offset, offset ^ TURN, rot)
-        state, staged = [], []
+            pass_on(offset, offset ^ TURN, state[0])
         for offsets, weights in zip(calls[:-1], STAGES + [[]] * len(calls)):
             stage = (place, *[(out_weight, twin_weight)[at] for at in weights]) if weights else ()
             state = blocks(offsets, state, False, 0, block, stage)

time: 38.3 us -> 36.3 us (0.948)
  the two profiles are of different devices: /device:TPU:0 before, /device:TPU:26 now
where the time goes in v5:
time: 36.3 us; the launch traced here: 36.1 us
  Pallas kernels  15.5 us (43%)
  waiting for transfers between devices  10.5 us (29%)
  starting transfers between devices  10.1 us (28%)
    ppermute x9, waiting for transfers between devices, swap(): return lax.ppermute(x, axis, [(i, i ^ bits) for i in range(size)])  8.28 us
    ppermute x9, starting transfers between devices, swap(): return lax.ppermute(x, axis, [(i, i ^ bits) for i in range(size)])  6.57 us
    pallas_call x5, Pallas kernels, attend(): pl.pallas_call(functools.partial(attend_kernel, tuple(offsets), rot.shape...  6.24 us
    ppermute x3, starting transfers between devices, swap_late(): return lax.ppermute(x, ('seq', 'kv'), pairs)  3.49 us
    pallas_call x1, Pallas kernels, project_home(): pl.pallas_call(functools.partial(home_kernel, len(own)), in_specs=[smem,...  3.23 us
    pallas_call x1, Pallas kernels, begin(): pl.pallas_call(functools.partial(begin_kernel, kinds), in_specs=[smem, sm...  2.54 us
    ppermute x3, waiting for transfers between devices, swap_late(): return lax.ppermute(x, ('seq', 'kv'), pairs)  2.23 us
    pallas_call x2, Pallas kernels, project(): pl.pallas_call(project_kernel, in_specs=[vmem] * 4, out_specs=vmem, out_s...  1.48 us
  transfers between devices with their start and end apart: 12, of which 5 were waited for; matrix products, arithmetic and copies ran while one was open for 0% of the time, Pallas kernels for 38%

profile of v5, /device:TPU:26, one launch (start us, length us, event | category | flops | bytes accessed | tf_op | source)
XLA Modules:
  0.0 36.1 jit_solution(6951192037994969098)
XLA Ops:
  0.0 1.1 %rotate_keys.1.piece_ref = bf16[512,128]{1,0:T(8,128)(2,1)S(1)} custom-call(s32[1]{0:T(128)} %bitcast.1.rank_ref, bf16[256,128]{1,0:T(8,128)(2,1)} %bitcast.6, bf16[256,128]{1,0:T(8,128)(2,1)} %bitcast.7, f32[1536,128]{1,0:T(8,128)} %constant.13.clone.cos_hbm, f32[1536,128]{1,0:T(8,128)} %constant.14.clone.sin_hbm), custom_call_target="tpu_custom_call" | custom-call | tf_op jit(solution)/shard_map/rotate_keys/pallas_call | solution.py:71
  1.4 0.7 %collective-permute-start.7 = (bf16[512,128]{1,0:T(8,128)(2,1)S(1)}, bf16[512,128]{1,0:T(8,128)(2,1)S(1)}, u32[]{:S(2)}, u32[]{:S(2)}) collective-permute-start(bf16[512,128]{1,0:T(8,128)(2,1)S(1)} %rotate_keys.1.piece_ref), channel_id=1, source_target_pairs={{0,8},{4,12},{8,0},{12,4},{16,24},{20,28},{24,16},{28,20},{1,9},{5... | collective-permute-start | bytes 393224 | tf_op jit(solution)/shard_map/ppermute | solution.py:407
  2.1 1.5 %collective-permute-start.6 = (bf16[512,128]{1,0:T(8,128)(2,1)S(1)}, bf16[512,128]{1,0:T(8,128)(2,1)S(1)}, u32[]{:S(2)}, u32[]{:S(2)}) collective-permute-start(bf16[512,128]{1,0:T(8,128)(2,1)S(1)} %rotate_keys.1.piece_ref), channel_id=1, source_target_pairs={{0,4},{4,0},{8,12},{12,8},{16,20},{20,16},{24,28},{28,24},{1,5},{5... | collective-permute-start | bytes 393224 | tf_op jit(solution)/shard_map/ppermute | solution.py:407
  3.6 1.3 %collective-permute-start.5 = (bf16[512,128]{1,0:T(8,128)(2,1)S(1)}, bf16[512,128]{1,0:T(8,128)(2,1)S(1)}, u32[]{:S(2)}, u32[]{:S(2)}) collective-permute-start(bf16[512,128]{1,0:T(8,128)(2,1)S(1)} %rotate_keys.1.piece_ref), channel_id=1, source_target_pairs={{0,12},{4,8},{8,4},{12,0},{16,28},{20,24},{24,20},{28,16},{1,13},{... | collective-permute-start | bytes 393224 | tf_op jit(solution)/shard_map/ppermute | solution.py:407
  4.9 2.5 %attend_0.1 = (bf16[2,7,256,128]{3,2,1,0:T(8,128)(2,1)S(1)}, f32[7,256,128]{2,1,0:T(8,128)S(1)}, f32[7,256,128]{2,1,0:T(8,128)S(1)}, f32[7,256,128]{2,1,0:T(8,128)S(1)}, bf16[896,896]{1,0:T(8,128)(2,1)S(1)}) custom-call(s32[1]{0:T(128)} %bitcast.1.rank_ref, s32[1]{0:T(128)} %bitcast.place_ref.refs_5_, bf16[7,256,128]{2,1,0:T(8,128)(2,1)} %bitcast.5, ...), custom_call_target="tpu_custom_call" | custom-call | flops 1 | bytes 1 | tf_op jit(solution)/shard_map/attend_0/pallas_call | solution.py:184
  7.5 1.9 %collective-permute-done.1.refs_1_ = bf16[512,128]{1,0:T(8,128)(2,1)S(1)} collective-permute-done((bf16[512,128]{1,0:T(8,128)(2,1)S(1)}, bf16[512,128]{1,0:T(8,128)(2,1)S(1)}, u32[]{:S(2)}, u32[]{:S(2)}) %collective-permute-start.1) | collective-permute-done | bytes 131104 | tf_op jit(solution)/shard_map/ppermute | solution.py:407
  9.3 2.0 %collective-permute-start.4 = (bf16[512,128]{1,0:T(8,128)(2,1)S(1)}, bf16[512,128]{1,0:T(8,128)(2,1)S(1)}, u32[]{:S(2)}, u32[]{:S(2)}) collective-permute-start(bf16[512,128]{1,0:T(8,128)(2,1)S(1)} %collective-permute-done.1.refs_1_), channel_id=1, source_target_pairs={{0,1},{1,0},{2,3},{3,2},{4,5},{5,4},{6,7},{7,6},{8,9},{9,8},{10,11... | collective-permute-start | bytes 393224 | tf_op jit(solution)/shard_map/ppermute | solution.py:416
  11.3 0.8 %collective-permute-start.3 = (bf16[512,128]{1,0:T(8,128)(2,1)S(1)}, bf16[512,128]{1,0:T(8,128)(2,1)S(1)}, u32[]{:S(2)}, u32[]{:S(2)}) collective-permute-start(bf16[512,128]{1,0:T(8,128)(2,1)S(1)} %collective-permute-done.1.refs_1_), channel_id=1, source_target_pairs={{0,1},{1,0},{2,3},{3,2},{4,5},{5,4},{6,7},{7,6},{8,9},{9,8},{10,11... | collective-permute-start | bytes 393224 | tf_op jit(solution)/shard_map/ppermute | solution.py:416
  12.1 0.8 %collective-permute-start.2 = (bf16[512,128]{1,0:T(8,128)(2,1)S(1)}, bf16[512,128]{1,0:T(8,128)(2,1)S(1)}, u32[]{:S(2)}, u32[]{:S(2)}) collective-permute-start(bf16[512,128]{1,0:T(8,128)(2,1)S(1)} %collective-permute-done.1.refs_1_), channel_id=1, source_target_pairs={{0,1},{1,0},{2,3},{3,2},{4,5},{5,4},{6,7},{7,6},{8,9},{9,8},{10,11... | collective-permute-start | bytes 393224 | tf_op jit(solution)/shard_map/ppermute | solution.py:416
  12.8 1.6 %attend_1_2.1 = (f32[7,256,128]{2,1,0:T(8,128)S(1)}, f32[7,256,128]{2,1,0:T(8,128)S(1)}, f32[7,256,128]{2,1,0:T(8,128)S(1)}) custom-call(s32[1]{0:T(128)} %bitcast.1.rank_ref, bf16[2,7,256,128]{3,2,1,0:T(8,128)(2,1)S(1)} %get-tuple-element.21.rot_ref, bf16[512,128]{1,0:T(8,128)(2,1)S(1)} %collective-permute-done.6.refs_0_, ...), custom_call_target="tpu_custom_call" | custom-call | flops 1 | bytes 1 | tf_op jit(solution)/shard_map/attend_1_2/pallas_call | solution.py:296
  14.5 1.6 %attend_3_6.1 = (f32[7,256,128]{2,1,0:T(8,128)S(1)}, f32[7,256,128]{2,1,0:T(8,128)S(1)}, f32[7,256,128]{2,1,0:T(8,128)S(1)}, bf16[896,896]{1,0:T(8,128)(2,1)S(1)}) custom-call(s32[1]{0:T(128)} %bitcast.1.rank_ref, bf16[2,7,256,128]{3,2,1,0:T(8,128)(2,1)S(1)} %get-tuple-element.21.rot_ref, bf16[512,128]{1,0:T(8,128)(2,1)S(1)} %collective-permute-done.5.refs_0_, ...), custom_call_target="tpu_custom_call" | custom-call | flops 1 | bytes 1 | tf_op jit(solution)/shard_map/attend_3_6/pallas_call | solution.py:296
  16.2 1.0 %collective-permute-done.4.refs_0_ = bf16[512,128]{1,0:T(8,128)(2,1)S(1)} collective-permute-done((bf16[512,128]{1,0:T(8,128)(2,1)S(1)}, bf16[512,128]{1,0:T(8,128)(2,1)S(1)}, u32[]{:S(2)}, u32[]{:S(2)}) %collective-permute-start.4) | collective-permute-done | bytes 131104 | tf_op jit(solution)/shard_map/ppermute | solution.py:416
  17.2 1.0 %attend_5.1 = (f32[7,256,128]{2,1,0:T(8,128)S(1)}, f32[7,256,128]{2,1,0:T(8,128)S(1)}, f32[7,256,128]{2,1,0:T(8,128)S(1)}) custom-call(s32[1]{0:T(128)} %bitcast.1.rank_ref, bf16[2,7,256,128]{3,2,1,0:T(8,128)(2,1)S(1)} %get-tuple-element.21.rot_ref, bf16[512,128]{1,0:T(8,128)(2,1)S(1)} %collective-permute-done.4.refs_0_, ...), custom_call_target="tpu_custom_call" | custom-call | flops 1 | bytes 1 | tf_op jit(solution)/shard_map/attend_5/pallas_call | solution.py:296
  18.2 1.2 %collective-permute-done.3.refs_1_ = bf16[512,128]{1,0:T(8,128)(2,1)S(1)} collective-permute-done((bf16[512,128]{1,0:T(8,128)(2,1)S(1)}, bf16[512,128]{1,0:T(8,128)(2,1)S(1)}, u32[]{:S(2)}, u32[]{:S(2)}) %collective-permute-start.3) | collective-permute-done | bytes 131104 | tf_op jit(solution)/shard_map/ppermute | solution.py:416
  19.4 1.0 %attend_4_7.2.refs_0_.own_ref = bf16[128,896]{1,0:T(8,128)(2,1)S(1)} custom-call(s32[1]{0:T(128)} %bitcast.1.rank_ref, bf16[2,7,256,128]{3,2,1,0:T(8,128)(2,1)S(1)} %get-tuple-element.21.rot_ref, bf16[512,128]{1,0:T(8,128)(2,1)S(1)} %collective-permute-done.2.refs_0_, bf16[512,128]{1,0:T(8,128)(2,1)S(1)} %collective-permute-done.3.refs_1_, ...), custom_call_target="tpu_custom_call" | custom-call | flops 1 | bytes 1 | tf_op jit(solution)/shard_map/attend_4_7/pallas_call | solution.py:296
  20.5 1.0 %attend_4_7.3.refs_1_.own_ref = bf16[128,896]{1,0:T(8,128)(2,1)S(1)} custom-call(s32[1]{0:T(128)} %bitcast.1.rank_ref, bf16[2,7,256,128]{3,2,1,0:T(8,128)(2,1)S(1)} %get-tuple-element.21.rot_ref, bf16[512,128]{1,0:T(8,128)(2,1)S(1)} %collective-permute-done.2.refs_0_, bf16[512,128]{1,0:T(8,128)(2,1)S(1)} %collective-permute-done.3.refs_1_, ...), custom_call_target="tpu_custom_call" | custom-call | flops 1 | bytes 1 | tf_op jit(solution)/shard_map/attend_4_7/pallas_call | solution.py:296
  22.0 0.7 %away.2 = bf16[128,896]{1,0:T(8,128)(2,1)S(1)} custom-call(bf16[128,896]{1,0:T(8,128)(2,1)S(1)} %attend_4_7.2.refs_0_.own_ref, bf16[128,896]{1,0:T(8,128)(2,1)S(1)} %collective-permute-done.8.refs_2_.twin_ref, bf16[896,896]{1,0:T(8,128)(2,1)S(1)} %get-tuple-element.35.own_weight, bf16[896,896]{1,0:T(8,128)(2,1)S(1)} %get-tuple-element.36.twin_weight), custom_call_target="tpu_custom_call" | custom-call | flops 1 | bytes 1 | tf_op jit(solution)/shard_map/away/pallas_call | solution.py:326
  22.8 0.6 %collective-permute-start.10 = (bf16[128,896]{1,0:T(8,128)(2,1)S(1)}, bf16[128,896]{1,0:T(8,128)(2,1)S(1)}, u32[]{:S(2)}, u32[]{:S(2)}) collective-permute-start(bf16[128,896]{1,0:T(8,128)(2,1)S(1)} %away.2), channel_id=1, source_target_pairs={{0,2},{1,3},{2,0},{3,1},{4,6},{5,7},{6,4},{7,5},{8,10},{9,11},{10,... | collective-permute-start | bytes 688136 | tf_op jit(solution)/shard_map/ppermute | solution.py:407
  23.4 0.7 %away.3 = bf16[128,896]{1,0:T(8,128)(2,1)S(1)} custom-call(bf16[128,896]{1,0:T(8,128)(2,1)S(1)} %attend_4_7.3.refs_1_.own_ref, bf16[128,896]{1,0:T(8,128)(2,1)S(1)} %collective-permute-done.9.refs_3_.twin_ref, bf16[896,896]{1,0:T(8,128)(2,1)S(1)} %get-tuple-element.35.own_weight, bf16[896,896]{1,0:T(8,128)(2,1)S(1)} %get-tuple-element.36.twin_weight), custom_call_target="tpu_custom_call" | custom-call | flops 1 | bytes 1 | tf_op jit(solution)/shard_map/away/pallas_call | solution.py:326
  24.1 1.6 %collective-permute-start.11 = (bf16[128,896]{1,0:T(8,128)(2,1)S(1)}, bf16[128,896]{1,0:T(8,128)(2,1)S(1)}, u32[]{:S(2)}, u32[]{:S(2)}) collective-permute-start(bf16[128,896]{1,0:T(8,128)(2,1)S(1)} %away.3), channel_id=1, source_target_pairs={{0,2},{1,3},{2,0},{3,1},{4,6},{5,7},{6,4},{7,5},{8,10},{9,11},{10,... | collective-permute-start | bytes 688136 | tf_op jit(solution)/shard_map/ppermute | solution.py:407
  25.7 3.2 %home.1.home_ref = f32[256,896]{1,0:T(8,128)S(1)} custom-call(s32[1]{0:T(128)} %bitcast.place_ref.refs_5_, bf16[896,3584]{1,0:T(8,128)(2,1)} %own_hbm.1, bf16[896,3584]{1,0:T(8,128)(2,1)} %collective-permute-done.refs_6_.twin_hbm, bf16[128,896]{1,0:T(8,128)(2,1)S(1)} %attend_4_7.2.refs_0_.own_ref, bf16[128,896]{1,0:T(8,128)(2,1)S(1)} %attend_4_7.3.refs_1_.own_ref, ...), custom_call_target="tpu_custom_call" | custom-call | flops 1 | bytes 1 | tf_op jit(solution)/shard_map/home/pallas_call | solution.py:360
  28.9 2.4 %collective-permute-done.10.refs_0_ = bf16[128,896]{1,0:T(8,128)(2,1)S(1)} collective-permute-done((bf16[128,896]{1,0:T(8,128)(2,1)S(1)}, bf16[128,896]{1,0:T(8,128)(2,1)S(1)}, u32[]{:S(2)}, u32[]{:S(2)}) %collective-permute-start.10) | collective-permute-done | bytes 229408 | tf_op jit(solution)/shard_map/ppermute | solution.py:407
  31.3 4.0 %collective-permute-done.11.refs_1_ = bf16[128,896]{1,0:T(8,128)(2,1)S(1)} collective-permute-done((bf16[128,896]{1,0:T(8,128)(2,1)S(1)}, bf16[128,896]{1,0:T(8,128)(2,1)S(1)}, u32[]{:S(2)}, u32[]{:S(2)}) %collective-permute-start.11) | collective-permute-done | bytes 229408 | tf_op jit(solution)/shard_map/ppermute | solution.py:407
  35.3 0.8 %close.1 = bf16[256,896]{1,0:T(8,128)(2,1)} custom-call(f32[256,896]{1,0:T(8,128)S(1)} %home.1.home_ref, bf16[128,896]{1,0:T(8,128)(2,1)S(1)} %collective-permute-done.10.refs_0_, bf16[128,896]{1,0:T(8,128)(2,1)S(1)} %collective-permute-done.11.refs_1_), custom_call_target="tpu_custom_call" | custom-call | flops 1 | bytes 1 | tf_op jit(solution)/shard_map/close/pallas_call | solution.py:391
  (11 shorter events, 0.9 us)
Async XLA Ops:
  0.0 14.5 %collective-permute-start = (bf16[896,3584]{1,0:T(8,128)(2,1)}, bf16[896,3584]{1,0:T(8,128)(2,1)}, u32[]{:S(2)}, u32[]{:S(2)}) collective-permute-start(bf16[896,3584]{1,0:T(8,128)(2,1)} %own_hbm.1), channel_id=1, source_target_pairs={{0,1},{1,0},{2,3},{3,2},{4,5},{5,4},{6,7},{7,6},{8,9},{9,8},{10,11... | collective-permute-start | bytes 19267592 | tf_op jit(solution)/shard_map/ppermute | solution.py:407
  1.1 8.2 %collective-permute-start.1 = (bf16[512,128]{1,0:T(8,128)(2,1)S(1)}, bf16[512,128]{1,0:T(8,128)(2,1)S(1)}, u32[]{:S(2)}, u32[]{:S(2)}) collective-permute-start(bf16[512,128]{1,0:T(8,128)(2,1)S(1)} %rotate_keys.1.piece_ref), channel_id=1, source_target_pairs={{0,24},{4,28},{8,16},{12,20},{16,8},{20,12},{24,0},{28,4},{1,25},{... | collective-permute-start | bytes 393224 | tf_op jit(solution)/shard_map/ppermute | solution.py:407
  1.4 9.9 %collective-permute-start.7 = (bf16[512,128]{1,0:T(8,128)(2,1)S(1)}, bf16[512,128]{1,0:T(8,128)(2,1)S(1)}, u32[]{:S(2)}, u32[]{:S(2)}) collective-permute-start(bf16[512,128]{1,0:T(8,128)(2,1)S(1)} %rotate_keys.1.piece_ref), channel_id=1, source_target_pairs={{0,8},{4,12},{8,0},{12,4},{16,24},{20,28},{24,16},{28,20},{1,9},{5... | collective-permute-start | bytes 393224 | tf_op jit(solution)/shard_map/ppermute | solution.py:407
  2.1 10.0 %collective-permute-start.6 = (bf16[512,128]{1,0:T(8,128)(2,1)S(1)}, bf16[512,128]{1,0:T(8,128)(2,1)S(1)}, u32[]{:S(2)}, u32[]{:S(2)}) collective-permute-start(bf16[512,128]{1,0:T(8,128)(2,1)S(1)} %rotate_keys.1.piece_ref), channel_id=1, source_target_pairs={{0,4},{4,0},{8,12},{12,8},{16,20},{20,16},{24,28},{28,24},{1,5},{5... | collective-permute-start | bytes 393224 | tf_op jit(solution)/shard_map/ppermute | solution.py:407
  3.6 10.9 %collective-permute-start.5 = (bf16[512,128]{1,0:T(8,128)(2,1)S(1)}, bf16[512,128]{1,0:T(8,128)(2,1)S(1)}, u32[]{:S(2)}, u32[]{:S(2)}) collective-permute-start(bf16[512,128]{1,0:T(8,128)(2,1)S(1)} %rotate_keys.1.piece_ref), channel_id=1, source_target_pairs={{0,12},{4,8},{8,4},{12,0},{16,28},{20,24},{24,20},{28,16},{1,13},{... | collective-permute-start | bytes 393224 | tf_op jit(solution)/shard_map/ppermute | solution.py:407
  9.3 7.8 %collective-permute-start.4 = (bf16[512,128]{1,0:T(8,128)(2,1)S(1)}, bf16[512,128]{1,0:T(8,128)(2,1)S(1)}, u32[]{:S(2)}, u32[]{:S(2)}) collective-permute-start(bf16[512,128]{1,0:T(8,128)(2,1)S(1)} %collective-permute-done.1.refs_1_), channel_id=1, source_target_pairs={{0,1},{1,0},{2,3},{3,2},{4,5},{5,4},{6,7},{7,6},{8,9},{9,8},{10,11... | collective-permute-start | bytes 393224 | tf_op jit(solution)/shard_map/ppermute | solution.py:416
  11.3 8.1 %collective-permute-start.3 = (bf16[512,128]{1,0:T(8,128)(2,1)S(1)}, bf16[512,128]{1,0:T(8,128)(2,1)S(1)}, u32[]{:S(2)}, u32[]{:S(2)}) collective-permute-start(bf16[512,128]{1,0:T(8,128)(2,1)S(1)} %collective-permute-done.1.refs_1_), channel_id=1, source_target_pairs={{0,1},{1,0},{2,3},{3,2},{4,5},{5,4},{6,7},{7,6},{8,9},{9,8},{10,11... | collective-permute-start | bytes 393224 | tf_op jit(solution)/shard_map/ppermute | solution.py:416
  12.1 7.3 %collective-permute-start.2 = (bf16[512,128]{1,0:T(8,128)(2,1)S(1)}, bf16[512,128]{1,0:T(8,128)(2,1)S(1)}, u32[]{:S(2)}, u32[]{:S(2)}) collective-permute-start(bf16[512,128]{1,0:T(8,128)(2,1)S(1)} %collective-permute-done.1.refs_1_), channel_id=1, source_target_pairs={{0,1},{1,0},{2,3},{3,2},{4,5},{5,4},{6,7},{7,6},{8,9},{9,8},{10,11... | collective-permute-start | bytes 393224 | tf_op jit(solution)/shard_map/ppermute | solution.py:416
  20.4 1.6 %collective-permute-start.8 = (bf16[128,896]{1,0:T(8,128)(2,1)S(1)}, bf16[128,896]{1,0:T(8,128)(2,1)S(1)}, u32[]{:S(2)}, u32[]{:S(2)}) collective-permute-start(bf16[128,896]{1,0:T(8,128)(2,1)S(1)} %attend_4_7.2.refs_0_.own_ref), channel_id=1, source_target_pairs={{0,1},{1,0},{2,3},{3,2},{4,5},{5,4},{6,7},{7,6},{8,9},{9,8},{10,11... | collective-permute-start | bytes 688136 | tf_op jit(solution)/shard_map/ppermute | solution.py:407
  21.5 1.9 %collective-permute-start.9 = (bf16[128,896]{1,0:T(8,128)(2,1)S(1)}, bf16[128,896]{1,0:T(8,128)(2,1)S(1)}, u32[]{:S(2)}, u32[]{:S(2)}) collective-permute-start(bf16[128,896]{1,0:T(8,128)(2,1)S(1)} %attend_4_7.3.refs_1_.own_ref), channel_id=1, source_target_pairs={{0,1},{1,0},{2,3},{3,2},{4,5},{5,4},{6,7},{7,6},{8,9},{9,8},{10,11... | collective-permute-start | bytes 688136 | tf_op jit(solution)/shard_map/ppermute | solution.py:407
  22.8 8.5 %collective-permute-start.10 = (bf16[128,896]{1,0:T(8,128)(2,1)S(1)}, bf16[128,896]{1,0:T(8,128)(2,1)S(1)}, u32[]{:S(2)}, u32[]{:S(2)}) collective-permute-start(bf16[128,896]{1,0:T(8,128)(2,1)S(1)} %away.2), channel_id=1, source_target_pairs={{0,2},{1,3},{2,0},{3,1},{4,6},{5,7},{6,4},{7,5},{8,10},{9,11},{10,... | collective-permute-start | bytes 688136 | tf_op jit(solution)/shard_map/ppermute | solution.py:407
  24.1 11.2 %collective-permute-start.11 = (bf16[128,896]{1,0:T(8,128)(2,1)S(1)}, bf16[128,896]{1,0:T(8,128)(2,1)S(1)}, u32[]{:S(2)}, u32[]{:S(2)}) collective-permute-start(bf16[128,896]{1,0:T(8,128)(2,1)S(1)} %away.3), channel_id=1, source_target_pairs={{0,2},{1,3},{2,0},{3,1},{4,6},{5,7},{6,4},{7,5},{8,10},{9,11},{10,... | collective-permute-start | bytes 688136 | tf_op jit(solution)/shard_map/ppermute | solution.py:407

commit v6 on v5

--- a/solution.py
+++ b/solution.py
@@ -163,9 +163,13 @@
                 rotated(query_ref[head], cos_ref[kind], sin_ref[kind]) * SCALE
             ).astype(jnp.bfloat16)
 
+    def blank(kind):
+        rot_ref[kind] = jnp.zeros(rot_ref.shape[1:], rot_ref.dtype)
+
     turn(0)
     for kind in range(1, kinds):
         pl.when(rank >= kind * per_span)(functools.partial(turn, kind))
+        pl.when(rank < kind * per_span)(functools.partial(blank, kind))
     later = scores_of([rot_ref[0, 0]], [piece_ref])
     for head in range(heads):
         now = later

time: 36.3 us -> 36.3 us (level)
  no operation moved by 1% of the time
where the time goes in v6:
time: 36.3 us; the launch traced here: 36.1 us
  Pallas kernels  15.5 us (43%)
  waiting for transfers between devices  10.5 us (29%)
  starting transfers between devices  10.1 us (28%)
    ppermute x9, waiting for transfers between devices, swap(): return lax.ppermute(x, axis, [(i, i ^ bits) for i in range(size)])  8.28 us
    ppermute x9, starting transfers between devices, swap(): return lax.ppermute(x, axis, [(i, i ^ bits) for i in range(size)])  6.57 us
    pallas_call x5, Pallas kernels, attend(): pl.pallas_call(functools.partial(attend_kernel, tuple(offsets), rot.shape...  6.24 us
    ppermute x3, starting transfers between devices, swap_late(): return lax.ppermute(x, ('seq', 'kv'), pairs)  3.49 us
    pallas_call x1, Pallas kernels, project_home(): pl.pallas_call(functools.partial(home_kernel, len(own)), in_specs=[smem,...  3.23 us
    pallas_call x1, Pallas kernels, begin(): pl.pallas_call(functools.partial(begin_kernel, kinds), in_specs=[smem, sm...  2.54 us
    ppermute x3, waiting for transfers between devices, swap_late(): return lax.ppermute(x, ('seq', 'kv'), pairs)  2.23 us
    pallas_call x2, Pallas kernels, project(): pl.pallas_call(project_kernel, in_specs=[vmem] * 4, out_specs=vmem, out_s...  1.48 us
  transfers between devices with their start and end apart: 12, of which 5 were waited for; matrix products, arithmetic and copies ran while one was open for 0% of the time, Pallas kernels for 38%

profile of v6, /device:TPU:26, one launch (start us, length us, event | category | flops | bytes accessed | tf_op | source)
XLA Modules:
  0.0 36.1 jit_solution(5183752197006545862)
XLA Ops:
  0.0 1.1 %rotate_keys.1.piece_ref = bf16[512,128]{1,0:T(8,128)(2,1)S(1)} custom-call(s32[1]{0:T(128)} %bitcast.1.rank_ref, bf16[256,128]{1,0:T(8,128)(2,1)} %bitcast.6, bf16[256,128]{1,0:T(8,128)(2,1)} %bitcast.7, f32[1536,128]{1,0:T(8,128)} %constant.13.clone.cos_hbm, f32[1536,128]{1,0:T(8,128)} %constant.14.clone.sin_hbm), custom_call_target="tpu_custom_call" | custom-call | tf_op jit(solution)/shard_map/rotate_keys/pallas_call | solution.py:71
  1.4 0.7 %collective-permute-start.7 = (bf16[512,128]{1,0:T(8,128)(2,1)S(1)}, bf16[512,128]{1,0:T(8,128)(2,1)S(1)}, u32[]{:S(2)}, u32[]{:S(2)}) collective-permute-start(bf16[512,128]{1,0:T(8,128)(2,1)S(1)} %rotate_keys.1.piece_ref), channel_id=1, source_target_pairs={{0,8},{4,12},{8,0},{12,4},{16,24},{20,28},{24,16},{28,20},{1,9},{5... | collective-permute-start | bytes 393224 | tf_op jit(solution)/shard_map/ppermute | solution.py:411
  2.1 1.5 %collective-permute-start.6 = (bf16[512,128]{1,0:T(8,128)(2,1)S(1)}, bf16[512,128]{1,0:T(8,128)(2,1)S(1)}, u32[]{:S(2)}, u32[]{:S(2)}) collective-permute-start(bf16[512,128]{1,0:T(8,128)(2,1)S(1)} %rotate_keys.1.piece_ref), channel_id=1, source_target_pairs={{0,4},{4,0},{8,12},{12,8},{16,20},{20,16},{24,28},{28,24},{1,5},{5... | collective-permute-start | bytes 393224 | tf_op jit(solution)/shard_map/ppermute | solution.py:411
  3.6 1.3 %collective-permute-start.5 = (bf16[512,128]{1,0:T(8,128)(2,1)S(1)}, bf16[512,128]{1,0:T(8,128)(2,1)S(1)}, u32[]{:S(2)}, u32[]{:S(2)}) collective-permute-start(bf16[512,128]{1,0:T(8,128)(2,1)S(1)} %rotate_keys.1.piece_ref), channel_id=1, source_target_pairs={{0,12},{4,8},{8,4},{12,0},{16,28},{20,24},{24,20},{28,16},{1,13},{... | collective-permute-start | bytes 393224 | tf_op jit(solution)/shard_map/ppermute | solution.py:411
  4.9 2.5 %attend_0.1 = (bf16[2,7,256,128]{3,2,1,0:T(8,128)(2,1)S(1)}, f32[7,256,128]{2,1,0:T(8,128)S(1)}, f32[7,256,128]{2,1,0:T(8,128)S(1)}, f32[7,256,128]{2,1,0:T(8,128)S(1)}, bf16[896,896]{1,0:T(8,128)(2,1)S(1)}) custom-call(s32[1]{0:T(128)} %bitcast.1.rank_ref, s32[1]{0:T(128)} %bitcast.place_ref.refs_5_, bf16[7,256,128]{2,1,0:T(8,128)(2,1)} %bitcast.5, ...), custom_call_target="tpu_custom_call" | custom-call | flops 1 | bytes 1 | tf_op jit(solution)/shard_map/attend_0/pallas_call | solution.py:188
  7.5 1.9 %collective-permute-done.1.refs_1_ = bf16[512,128]{1,0:T(8,128)(2,1)S(1)} collective-permute-done((bf16[512,128]{1,0:T(8,128)(2,1)S(1)}, bf16[512,128]{1,0:T(8,128)(2,1)S(1)}, u32[]{:S(2)}, u32[]{:S(2)}) %collective-permute-start.1) | collective-permute-done | bytes 131104 | tf_op jit(solution)/shard_map/ppermute | solution.py:411
  9.3 2.0 %collective-permute-start.4 = (bf16[512,128]{1,0:T(8,128)(2,1)S(1)}, bf16[512,128]{1,0:T(8,128)(2,1)S(1)}, u32[]{:S(2)}, u32[]{:S(2)}) collective-permute-start(bf16[512,128]{1,0:T(8,128)(2,1)S(1)} %collective-permute-done.1.refs_1_), channel_id=1, source_target_pairs={{0,1},{1,0},{2,3},{3,2},{4,5},{5,4},{6,7},{7,6},{8,9},{9,8},{10,11... | collective-permute-start | bytes 393224 | tf_op jit(solution)/shard_map/ppermute | solution.py:420
  11.3 0.8 %collective-permute-start.3 = (bf16[512,128]{1,0:T(8,128)(2,1)S(1)}, bf16[512,128]{1,0:T(8,128)(2,1)S(1)}, u32[]{:S(2)}, u32[]{:S(2)}) collective-permute-start(bf16[512,128]{1,0:T(8,128)(2,1)S(1)} %collective-permute-done.1.refs_1_), channel_id=1, source_target_pairs={{0,1},{1,0},{2,3},{3,2},{4,5},{5,4},{6,7},{7,6},{8,9},{9,8},{10,11... | collective-permute-start | bytes 393224 | tf_op jit(solution)/shard_map/ppermute | solution.py:420
  12.1 0.8 %collective-permute-start.2 = (bf16[512,128]{1,0:T(8,128)(2,1)S(1)}, bf16[512,128]{1,0:T(8,128)(2,1)S(1)}, u32[]{:S(2)}, u32[]{:S(2)}) collective-permute-start(bf16[512,128]{1,0:T(8,128)(2,1)S(1)} %collective-permute-done.1.refs_1_), channel_id=1, source_target_pairs={{0,1},{1,0},{2,3},{3,2},{4,5},{5,4},{6,7},{7,6},{8,9},{9,8},{10,11... | collective-permute-start | bytes 393224 | tf_op jit(solution)/shard_map/ppermute | solution.py:420
  12.8 1.6 %attend_1_2.1 = (f32[7,256,128]{2,1,0:T(8,128)S(1)}, f32[7,256,128]{2,1,0:T(8,128)S(1)}, f32[7,256,128]{2,1,0:T(8,128)S(1)}) custom-call(s32[1]{0:T(128)} %bitcast.1.rank_ref, bf16[2,7,256,128]{3,2,1,0:T(8,128)(2,1)S(1)} %get-tuple-element.21.rot_ref, bf16[512,128]{1,0:T(8,128)(2,1)S(1)} %collective-permute-done.6.refs_0_, ...), custom_call_target="tpu_custom_call" | custom-call | flops 1 | bytes 1 | tf_op jit(solution)/shard_map/attend_1_2/pallas_call | solution.py:300
  14.5 1.6 %attend_3_6.1 = (f32[7,256,128]{2,1,0:T(8,128)S(1)}, f32[7,256,128]{2,1,0:T(8,128)S(1)}, f32[7,256,128]{2,1,0:T(8,128)S(1)}, bf16[896,896]{1,0:T(8,128)(2,1)S(1)}) custom-call(s32[1]{0:T(128)} %bitcast.1.rank_ref, bf16[2,7,256,128]{3,2,1,0:T(8,128)(2,1)S(1)} %get-tuple-element.21.rot_ref, bf16[512,128]{1,0:T(8,128)(2,1)S(1)} %collective-permute-done.5.refs_0_, ...), custom_call_target="tpu_custom_call" | custom-call | flops 1 | bytes 1 | tf_op jit(solution)/shard_map/attend_3_6/pallas_call | solution.py:300
  16.2 1.0 %collective-permute-done.4.refs_0_ = bf16[512,128]{1,0:T(8,128)(2,1)S(1)} collective-permute-done((bf16[512,128]{1,0:T(8,128)(2,1)S(1)}, bf16[512,128]{1,0:T(8,128)(2,1)S(1)}, u32[]{:S(2)}, u32[]{:S(2)}) %collective-permute-start.4) | collective-permute-done | bytes 131104 | tf_op jit(solution)/shard_map/ppermute | solution.py:420
  17.2 1.0 %attend_5.1 = (f32[7,256,128]{2,1,0:T(8,128)S(1)}, f32[7,256,128]{2,1,0:T(8,128)S(1)}, f32[7,256,128]{2,1,0:T(8,128)S(1)}) custom-call(s32[1]{0:T(128)} %bitcast.1.rank_ref, bf16[2,7,256,128]{3,2,1,0:T(8,128)(2,1)S(1)} %get-tuple-element.21.rot_ref, bf16[512,128]{1,0:T(8,128)(2,1)S(1)} %collective-permute-done.4.refs_0_, ...), custom_call_target="tpu_custom_call" | custom-call | flops 1 | bytes 1 | tf_op jit(solution)/shard_map/attend_5/pallas_call | solution.py:300
  18.2 1.2 %collective-permute-done.3.refs_1_ = bf16[512,128]{1,0:T(8,128)(2,1)S(1)} collective-permute-done((bf16[512,128]{1,0:T(8,128)(2,1)S(1)}, bf16[512,128]{1,0:T(8,128)(2,1)S(1)}, u32[]{:S(2)}, u32[]{:S(2)}) %collective-permute-start.3) | collective-permute-done | bytes 131104 | tf_op jit(solution)/shard_map/ppermute | solution.py:420
  19.4 1.0 %attend_4_7.2.refs_0_.own_ref = bf16[128,896]{1,0:T(8,128)(2,1)S(1)} custom-call(s32[1]{0:T(128)} %bitcast.1.rank_ref, bf16[2,7,256,128]{3,2,1,0:T(8,128)(2,1)S(1)} %get-tuple-element.21.rot_ref, bf16[512,128]{1,0:T(8,128)(2,1)S(1)} %collective-permute-done.2.refs_0_, bf16[512,128]{1,0:T(8,128)(2,1)S(1)} %collective-permute-done.3.refs_1_, ...), custom_call_target="tpu_custom_call" | custom-call | flops 1 | bytes 1 | tf_op jit(solution)/shard_map/attend_4_7/pallas_call | solution.py:300
  20.5 1.0 %attend_4_7.3.refs_1_.own_ref = bf16[128,896]{1,0:T(8,128)(2,1)S(1)} custom-call(s32[1]{0:T(128)} %bitcast.1.rank_ref, bf16[2,7,256,128]{3,2,1,0:T(8,128)(2,1)S(1)} %get-tuple-element.21.rot_ref, bf16[512,128]{1,0:T(8,128)(2,1)S(1)} %collective-permute-done.2.refs_0_, bf16[512,128]{1,0:T(8,128)(2,1)S(1)} %collective-permute-done.3.refs_1_, ...), custom_call_target="tpu_custom_call" | custom-call | flops 1 | bytes 1 | tf_op jit(solution)/shard_map/attend_4_7/pallas_call | solution.py:300
  22.0 0.7 %away.2 = bf16[128,896]{1,0:T(8,128)(2,1)S(1)} custom-call(bf16[128,896]{1,0:T(8,128)(2,1)S(1)} %attend_4_7.2.refs_0_.own_ref, bf16[128,896]{1,0:T(8,128)(2,1)S(1)} %collective-permute-done.8.refs_2_.twin_ref, bf16[896,896]{1,0:T(8,128)(2,1)S(1)} %get-tuple-element.35.own_weight, bf16[896,896]{1,0:T(8,128)(2,1)S(1)} %get-tuple-element.36.twin_weight), custom_call_target="tpu_custom_call" | custom-call | flops 1 | bytes 1 | tf_op jit(solution)/shard_map/away/pallas_call | solution.py:330
  22.8 0.6 %collective-permute-start.10 = (bf16[128,896]{1,0:T(8,128)(2,1)S(1)}, bf16[128,896]{1,0:T(8,128)(2,1)S(1)}, u32[]{:S(2)}, u32[]{:S(2)}) collective-permute-start(bf16[128,896]{1,0:T(8,128)(2,1)S(1)} %away.2), channel_id=1, source_target_pairs={{0,2},{1,3},{2,0},{3,1},{4,6},{5,7},{6,4},{7,5},{8,10},{9,11},{10,... | collective-permute-start | bytes 688136 | tf_op jit(solution)/shard_map/ppermute | solution.py:411
  23.4 0.7 %away.3 = bf16[128,896]{1,0:T(8,128)(2,1)S(1)} custom-call(bf16[128,896]{1,0:T(8,128)(2,1)S(1)} %attend_4_7.3.refs_1_.own_ref, bf16[128,896]{1,0:T(8,128)(2,1)S(1)} %collective-permute-done.9.refs_3_.twin_ref, bf16[896,896]{1,0:T(8,128)(2,1)S(1)} %get-tuple-element.35.own_weight, bf16[896,896]{1,0:T(8,128)(2,1)S(1)} %get-tuple-element.36.twin_weight), custom_call_target="tpu_custom_call" | custom-call | flops 1 | bytes 1 | tf_op jit(solution)/shard_map/away/pallas_call | solution.py:330
  24.1 1.6 %collective-permute-start.11 = (bf16[128,896]{1,0:T(8,128)(2,1)S(1)}, bf16[128,896]{1,0:T(8,128)(2,1)S(1)}, u32[]{:S(2)}, u32[]{:S(2)}) collective-permute-start(bf16[128,896]{1,0:T(8,128)(2,1)S(1)} %away.3), channel_id=1, source_target_pairs={{0,2},{1,3},{2,0},{3,1},{4,6},{5,7},{6,4},{7,5},{8,10},{9,11},{10,... | collective-permute-start | bytes 688136 | tf_op jit(solution)/shard_map/ppermute | solution.py:411
  25.7 3.2 %home.1.home_ref = f32[256,896]{1,0:T(8,128)S(1)} custom-call(s32[1]{0:T(128)} %bitcast.place_ref.refs_5_, bf16[896,3584]{1,0:T(8,128)(2,1)} %own_hbm.1, bf16[896,3584]{1,0:T(8,128)(2,1)} %collective-permute-done.refs_6_.twin_hbm, bf16[128,896]{1,0:T(8,128)(2,1)S(1)} %attend_4_7.2.refs_0_.own_ref, bf16[128,896]{1,0:T(8,128)(2,1)S(1)} %attend_4_7.3.refs_1_.own_ref, ...), custom_call_target="tpu_custom_call" | custom-call | flops 1 | bytes 1 | tf_op jit(solution)/shard_map/home/pallas_call | solution.py:364
  28.9 2.4 %collective-permute-done.10.refs_0_ = bf16[128,896]{1,0:T(8,128)(2,1)S(1)} collective-permute-done((bf16[128,896]{1,0:T(8,128)(2,1)S(1)}, bf16[128,896]{1,0:T(8,128)(2,1)S(1)}, u32[]{:S(2)}, u32[]{:S(2)}) %collective-permute-start.10) | collective-permute-done | bytes 229408 | tf_op jit(solution)/shard_map/ppermute | solution.py:411
  31.3 4.0 %collective-permute-done.11.refs_1_ = bf16[128,896]{1,0:T(8,128)(2,1)S(1)} collective-permute-done((bf16[128,896]{1,0:T(8,128)(2,1)S(1)}, bf16[128,896]{1,0:T(8,128)(2,1)S(1)}, u32[]{:S(2)}, u32[]{:S(2)}) %collective-permute-start.11) | collective-permute-done | bytes 229408 | tf_op jit(solution)/shard_map/ppermute | solution.py:411
  35.3 0.8 %close.1 = bf16[256,896]{1,0:T(8,128)(2,1)} custom-call(f32[256,896]{1,0:T(8,128)S(1)} %home.1.home_ref, bf16[128,896]{1,0:T(8,128)(2,1)S(1)} %collective-permute-done.10.refs_0_, bf16[128,896]{1,0:T(8,128)(2,1)S(1)} %collective-permute-done.11.refs_1_), custom_call_target="tpu_custom_call" | custom-call | flops 1 | bytes 1 | tf_op jit(solution)/shard_map/close/pallas_call | solution.py:395
  (11 shorter events, 0.9 us)
Async XLA Ops:
  0.0 14.5 %collective-permute-start = (bf16[896,3584]{1,0:T(8,128)(2,1)}, bf16[896,3584]{1,0:T(8,128)(2,1)}, u32[]{:S(2)}, u32[]{:S(2)}) collective-permute-start(bf16[896,3584]{1,0:T(8,128)(2,1)} %own_hbm.1), channel_id=1, source_target_pairs={{0,1},{1,0},{2,3},{3,2},{4,5},{5,4},{6,7},{7,6},{8,9},{9,8},{10,11... | collective-permute-start | bytes 19267592 | tf_op jit(solution)/shard_map/ppermute | solution.py:411
  1.1 8.2 %collective-permute-start.1 = (bf16[512,128]{1,0:T(8,128)(2,1)S(1)}, bf16[512,128]{1,0:T(8,128)(2,1)S(1)}, u32[]{:S(2)}, u32[]{:S(2)}) collective-permute-start(bf16[512,128]{1,0:T(8,128)(2,1)S(1)} %rotate_keys.1.piece_ref), channel_id=1, source_target_pairs={{0,24},{4,28},{8,16},{12,20},{16,8},{20,12},{24,0},{28,4},{1,25},{... | collective-permute-start | bytes 393224 | tf_op jit(solution)/shard_map/ppermute | solution.py:411
  1.4 9.9 %collective-permute-start.7 = (bf16[512,128]{1,0:T(8,128)(2,1)S(1)}, bf16[512,128]{1,0:T(8,128)(2,1)S(1)}, u32[]{:S(2)}, u32[]{:S(2)}) collective-permute-start(bf16[512,128]{1,0:T(8,128)(2,1)S(1)} %rotate_keys.1.piece_ref), channel_id=1, source_target_pairs={{0,8},{4,12},{8,0},{12,4},{16,24},{20,28},{24,16},{28,20},{1,9},{5... | collective-permute-start | bytes 393224 | tf_op jit(solution)/shard_map/ppermute | solution.py:411
  2.1 10.0 %collective-permute-start.6 = (bf16[512,128]{1,0:T(8,128)(2,1)S(1)}, bf16[512,128]{1,0:T(8,128)(2,1)S(1)}, u32[]{:S(2)}, u32[]{:S(2)}) collective-permute-start(bf16[512,128]{1,0:T(8,128)(2,1)S(1)} %rotate_keys.1.piece_ref), channel_id=1, source_target_pairs={{0,4},{4,0},{8,12},{12,8},{16,20},{20,16},{24,28},{28,24},{1,5},{5... | collective-permute-start | bytes 393224 | tf_op jit(solution)/shard_map/ppermute | solution.py:411
  3.6 10.9 %collective-permute-start.5 = (bf16[512,128]{1,0:T(8,128)(2,1)S(1)}, bf16[512,128]{1,0:T(8,128)(2,1)S(1)}, u32[]{:S(2)}, u32[]{:S(2)}) collective-permute-start(bf16[512,128]{1,0:T(8,128)(2,1)S(1)} %rotate_keys.1.piece_ref), channel_id=1, source_target_pairs={{0,12},{4,8},{8,4},{12,0},{16,28},{20,24},{24,20},{28,16},{1,13},{... | collective-permute-start | bytes 393224 | tf_op jit(solution)/shard_map/ppermute | solution.py:411
  9.3 7.8 %collective-permute-start.4 = (bf16[512,128]{1,0:T(8,128)(2,1)S(1)}, bf16[512,128]{1,0:T(8,128)(2,1)S(1)}, u32[]{:S(2)}, u32[]{:S(2)}) collective-permute-start(bf16[512,128]{1,0:T(8,128)(2,1)S(1)} %collective-permute-done.1.refs_1_), channel_id=1, source_target_pairs={{0,1},{1,0},{2,3},{3,2},{4,5},{5,4},{6,7},{7,6},{8,9},{9,8},{10,11... | collective-permute-start | bytes 393224 | tf_op jit(solution)/shard_map/ppermute | solution.py:420
  11.3 8.1 %collective-permute-start.3 = (bf16[512,128]{1,0:T(8,128)(2,1)S(1)}, bf16[512,128]{1,0:T(8,128)(2,1)S(1)}, u32[]{:S(2)}, u32[]{:S(2)}) collective-permute-start(bf16[512,128]{1,0:T(8,128)(2,1)S(1)} %collective-permute-done.1.refs_1_), channel_id=1, source_target_pairs={{0,1},{1,0},{2,3},{3,2},{4,5},{5,4},{6,7},{7,6},{8,9},{9,8},{10,11... | collective-permute-start | bytes 393224 | tf_op jit(solution)/shard_map/ppermute | solution.py:420
  12.1 7.3 %collective-permute-start.2 = (bf16[512,128]{1,0:T(8,128)(2,1)S(1)}, bf16[512,128]{1,0:T(8,128)(2,1)S(1)}, u32[]{:S(2)}, u32[]{:S(2)}) collective-permute-start(bf16[512,128]{1,0:T(8,128)(2,1)S(1)} %collective-permute-done.1.refs_1_), channel_id=1, source_target_pairs={{0,1},{1,0},{2,3},{3,2},{4,5},{5,4},{6,7},{7,6},{8,9},{9,8},{10,11... | collective-permute-start | bytes 393224 | tf_op jit(solution)/shard_map/ppermute | solution.py:420
  20.4 1.6 %collective-permute-start.8 = (bf16[128,896]{1,0:T(8,128)(2,1)S(1)}, bf16[128,896]{1,0:T(8,128)(2,1)S(1)}, u32[]{:S(2)}, u32[]{:S(2)}) collective-permute-start(bf16[128,896]{1,0:T(8,128)(2,1)S(1)} %attend_4_7.2.refs_0_.own_ref), channel_id=1, source_target_pairs={{0,1},{1,0},{2,3},{3,2},{4,5},{5,4},{6,7},{7,6},{8,9},{9,8},{10,11... | collective-permute-start | bytes 688136 | tf_op jit(solution)/shard_map/ppermute | solution.py:411
  21.5 1.9 %collective-permute-start.9 = (bf16[128,896]{1,0:T(8,128)(2,1)S(1)}, bf16[128,896]{1,0:T(8,128)(2,1)S(1)}, u32[]{:S(2)}, u32[]{:S(2)}) collective-permute-start(bf16[128,896]{1,0:T(8,128)(2,1)S(1)} %attend_4_7.3.refs_1_.own_ref), channel_id=1, source_target_pairs={{0,1},{1,0},{2,3},{3,2},{4,5},{5,4},{6,7},{7,6},{8,9},{9,8},{10,11... | collective-permute-start | bytes 688136 | tf_op jit(solution)/shard_map/ppermute | solution.py:411
  22.8 8.5 %collective-permute-start.10 = (bf16[128,896]{1,0:T(8,128)(2,1)S(1)}, bf16[128,896]{1,0:T(8,128)(2,1)S(1)}, u32[]{:S(2)}, u32[]{:S(2)}) collective-permute-start(bf16[128,896]{1,0:T(8,128)(2,1)S(1)} %away.2), channel_id=1, source_target_pairs={{0,2},{1,3},{2,0},{3,1},{4,6},{5,7},{6,4},{7,5},{8,10},{9,11},{10,... | collective-permute-start | bytes 688136 | tf_op jit(solution)/shard_map/ppermute | solution.py:411
  24.1 11.2 %collective-permute-start.11 = (bf16[128,896]{1,0:T(8,128)(2,1)S(1)}, bf16[128,896]{1,0:T(8,128)(2,1)S(1)}, u32[]{:S(2)}, u32[]{:S(2)}) collective-permute-start(bf16[128,896]{1,0:T(8,128)(2,1)S(1)} %away.3), channel_id=1, source_target_pairs={{0,2},{1,3},{2,0},{3,1},{4,6},{5,7},{6,4},{7,5},{8,10},{9,11},{10,... | collective-permute-start | bytes 688136 | tf_op jit(solution)/shard_map/ppermute | solution.py:411

commit v7 on v6

--- a/solution.py
+++ b/solution.py
@@ -109,12 +109,12 @@
         acc, total = None, None
     else:
         top = jnp.maximum(top, old[0])
-        factor = jnp.exp2(old[0] - top)
+        factor = jnp.exp2((old[0] - top) * SCALE)
         acc, total = factor * old[1], factor * old[2]
     ones = jnp.ones((block, HEAD), jnp.bfloat16)
     for score, lift, piece in zip(scores, lifts, pieces):
         base = top if lift is None else top + lift
-        weight = jnp.exp2(score - jnp.concatenate([base] * len(lanes), 1)).astype(jnp.bfloat16)
+        weight = jnp.exp2((score - jnp.concatenate([base] * len(lanes), 1)) * SCALE).astype(jnp.bfloat16)
         both = jnp.dot(
             weight, jnp.concatenate([piece[block:], ones], 1), preferred_element_type=jnp.float32
         )
@@ -159,9 +159,9 @@
     )
     def turn(kind):
         for head in range(heads):
-            rot_ref[kind, head] = (
-                rotated(query_ref[head], cos_ref[kind], sin_ref[kind]) * SCALE
-            ).astype(jnp.bfloat16)
+            rot_ref[kind, head] = rotated(query_ref[head], cos_ref[kind], sin_ref[kind]).astype(
+                jnp.bfloat16
+            )
 
     def blank(kind):
         rot_ref[kind] = jnp.zeros(rot_ref.shape[1:], rot_ref.dtype)

time: 36.3 us -> 36.3 us (level)
  no operation moved by 1% of the time
where the time goes in v7:
time: 36.3 us; the launch traced here: 36.1 us
  Pallas kernels  15.4 us (42%)
  waiting for transfers between devices  10.5 us (29%)
  starting transfers between devices  10.1 us (28%)
    ppermute x9, waiting for transfers between devices, swap(): return lax.ppermute(x, axis, [(i, i ^ bits) for i in range(size)])  8.31 us
    ppermute x9, starting transfers between devices, swap(): return lax.ppermute(x, axis, [(i, i ^ bits) for i in range(size)])  6.6 us
    pallas_call x5, Pallas kernels, attend(): pl.pallas_call(functools.partial(attend_kernel, tuple(offsets), rot.shape...  6.24 us
    ppermute x3, starting transfers between devices, swap_late(): return lax.ppermute(x, ('seq', 'kv'), pairs)  3.49 us
    pallas_call x1, Pallas kernels, project_home(): pl.pallas_call(functools.partial(home_kernel, len(own)), in_specs=[smem,...  3.24 us
    pallas_call x1, Pallas kernels, begin(): pl.pallas_call(functools.partial(begin_kernel, kinds), in_specs=[smem, sm...  2.5 us
    ppermute x3, waiting for transfers between devices, swap_late(): return lax.ppermute(x, ('seq', 'kv'), pairs)  2.2 us
    pallas_call x2, Pallas kernels, project(): pl.pallas_call(project_kernel, in_specs=[vmem] * 4, out_specs=vmem, out_s...  1.48 us
  transfers between devices with their start and end apart: 12, of which 5 were waited for; matrix products, arithmetic and copies ran while one was open for 0% of the time, Pallas kernels for 38%

profile of v7, /device:TPU:26, one launch (start us, length us, event | category | flops | bytes accessed | tf_op | source)
XLA Modules:
  0.0 36.1 jit_solution(17028758487585838456)
XLA Ops:
  0.0 1.1 %rotate_keys.1.piece_ref = bf16[512,128]{1,0:T(8,128)(2,1)S(1)} custom-call(s32[1]{0:T(128)} %bitcast.1.rank_ref, bf16[256,128]{1,0:T(8,128)(2,1)} %bitcast.6, bf16[256,128]{1,0:T(8,128)(2,1)} %bitcast.7, f32[1536,128]{1,0:T(8,128)} %constant.13.clone.cos_hbm, f32[1536,128]{1,0:T(8,128)} %constant.14.clone.sin_hbm), custom_call_target="tpu_custom_call" | custom-call | tf_op jit(solution)/shard_map/rotate_keys/pallas_call | solution.py:71
  1.4 0.7 %collective-permute-start.7 = (bf16[512,128]{1,0:T(8,128)(2,1)S(1)}, bf16[512,128]{1,0:T(8,128)(2,1)S(1)}, u32[]{:S(2)}, u32[]{:S(2)}) collective-permute-start(bf16[512,128]{1,0:T(8,128)(2,1)S(1)} %rotate_keys.1.piece_ref), channel_id=1, source_target_pairs={{0,8},{4,12},{8,0},{12,4},{16,24},{20,28},{24,16},{28,20},{1,9},{5... | collective-permute-start | bytes 393224 | tf_op jit(solution)/shard_map/ppermute | solution.py:411
  2.1 1.5 %collective-permute-start.6 = (bf16[512,128]{1,0:T(8,128)(2,1)S(1)}, bf16[512,128]{1,0:T(8,128)(2,1)S(1)}, u32[]{:S(2)}, u32[]{:S(2)}) collective-permute-start(bf16[512,128]{1,0:T(8,128)(2,1)S(1)} %rotate_keys.1.piece_ref), channel_id=1, source_target_pairs={{0,4},{4,0},{8,12},{12,8},{16,20},{20,16},{24,28},{28,24},{1,5},{5... | collective-permute-start | bytes 393224 | tf_op jit(solution)/shard_map/ppermute | solution.py:411
  3.6 1.3 %collective-permute-start.5 = (bf16[512,128]{1,0:T(8,128)(2,1)S(1)}, bf16[512,128]{1,0:T(8,128)(2,1)S(1)}, u32[]{:S(2)}, u32[]{:S(2)}) collective-permute-start(bf16[512,128]{1,0:T(8,128)(2,1)S(1)} %rotate_keys.1.piece_ref), channel_id=1, source_target_pairs={{0,12},{4,8},{8,4},{12,0},{16,28},{20,24},{24,20},{28,16},{1,13},{... | collective-permute-start | bytes 393224 | tf_op jit(solution)/shard_map/ppermute | solution.py:411
  4.9 2.5 %attend_0.1 = (bf16[2,7,256,128]{3,2,1,0:T(8,128)(2,1)S(1)}, f32[7,256,128]{2,1,0:T(8,128)S(1)}, f32[7,256,128]{2,1,0:T(8,128)S(1)}, f32[7,256,128]{2,1,0:T(8,128)S(1)}, bf16[896,896]{1,0:T(8,128)(2,1)S(1)}) custom-call(s32[1]{0:T(128)} %bitcast.1.rank_ref, s32[1]{0:T(128)} %bitcast.place_ref.refs_5_, bf16[7,256,128]{2,1,0:T(8,128)(2,1)} %bitcast.5, ...), custom_call_target="tpu_custom_call" | custom-call | flops 1 | bytes 1 | tf_op jit(solution)/shard_map/attend_0/pallas_call | solution.py:188
  7.4 1.9 %collective-permute-done.1.refs_1_ = bf16[512,128]{1,0:T(8,128)(2,1)S(1)} collective-permute-done((bf16[512,128]{1,0:T(8,128)(2,1)S(1)}, bf16[512,128]{1,0:T(8,128)(2,1)S(1)}, u32[]{:S(2)}, u32[]{:S(2)}) %collective-permute-start.1) | collective-permute-done | bytes 131104 | tf_op jit(solution)/shard_map/ppermute | solution.py:411
  9.3 2.0 %collective-permute-start.4 = (bf16[512,128]{1,0:T(8,128)(2,1)S(1)}, bf16[512,128]{1,0:T(8,128)(2,1)S(1)}, u32[]{:S(2)}, u32[]{:S(2)}) collective-permute-start(bf16[512,128]{1,0:T(8,128)(2,1)S(1)} %collective-permute-done.1.refs_1_), channel_id=1, source_target_pairs={{0,1},{1,0},{2,3},{3,2},{4,5},{5,4},{6,7},{7,6},{8,9},{9,8},{10,11... | collective-permute-start | bytes 393224 | tf_op jit(solution)/shard_map/ppermute | solution.py:420
  11.3 0.8 %collective-permute-start.3 = (bf16[512,128]{1,0:T(8,128)(2,1)S(1)}, bf16[512,128]{1,0:T(8,128)(2,1)S(1)}, u32[]{:S(2)}, u32[]{:S(2)}) collective-permute-start(bf16[512,128]{1,0:T(8,128)(2,1)S(1)} %collective-permute-done.1.refs_1_), channel_id=1, source_target_pairs={{0,1},{1,0},{2,3},{3,2},{4,5},{5,4},{6,7},{7,6},{8,9},{9,8},{10,11... | collective-permute-start | bytes 393224 | tf_op jit(solution)/shard_map/ppermute | solution.py:420
  12.1 0.8 %collective-permute-start.2 = (bf16[512,128]{1,0:T(8,128)(2,1)S(1)}, bf16[512,128]{1,0:T(8,128)(2,1)S(1)}, u32[]{:S(2)}, u32[]{:S(2)}) collective-permute-start(bf16[512,128]{1,0:T(8,128)(2,1)S(1)} %collective-permute-done.1.refs_1_), channel_id=1, source_target_pairs={{0,1},{1,0},{2,3},{3,2},{4,5},{5,4},{6,7},{7,6},{8,9},{9,8},{10,11... | collective-permute-start | bytes 393224 | tf_op jit(solution)/shard_map/ppermute | solution.py:420
  12.8 1.6 %attend_1_2.1 = (f32[7,256,128]{2,1,0:T(8,128)S(1)}, f32[7,256,128]{2,1,0:T(8,128)S(1)}, f32[7,256,128]{2,1,0:T(8,128)S(1)}) custom-call(s32[1]{0:T(128)} %bitcast.1.rank_ref, bf16[2,7,256,128]{3,2,1,0:T(8,128)(2,1)S(1)} %get-tuple-element.21.rot_ref, bf16[512,128]{1,0:T(8,128)(2,1)S(1)} %collective-permute-done.6.refs_0_, ...), custom_call_target="tpu_custom_call" | custom-call | flops 1 | bytes 1 | tf_op jit(solution)/shard_map/attend_1_2/pallas_call | solution.py:300
  14.5 1.6 %attend_3_6.1 = (f32[7,256,128]{2,1,0:T(8,128)S(1)}, f32[7,256,128]{2,1,0:T(8,128)S(1)}, f32[7,256,128]{2,1,0:T(8,128)S(1)}, bf16[896,896]{1,0:T(8,128)(2,1)S(1)}) custom-call(s32[1]{0:T(128)} %bitcast.1.rank_ref, bf16[2,7,256,128]{3,2,1,0:T(8,128)(2,1)S(1)} %get-tuple-element.21.rot_ref, bf16[512,128]{1,0:T(8,128)(2,1)S(1)} %collective-permute-done.5.refs_0_, ...), custom_call_target="tpu_custom_call" | custom-call | flops 1 | bytes 1 | tf_op jit(solution)/shard_map/attend_3_6/pallas_call | solution.py:300
  16.1 1.1 %collective-permute-done.4.refs_0_ = bf16[512,128]{1,0:T(8,128)(2,1)S(1)} collective-permute-done((bf16[512,128]{1,0:T(8,128)(2,1)S(1)}, bf16[512,128]{1,0:T(8,128)(2,1)S(1)}, u32[]{:S(2)}, u32[]{:S(2)}) %collective-permute-start.4) | collective-permute-done | bytes 131104 | tf_op jit(solution)/shard_map/ppermute | solution.py:420
  17.2 1.1 %attend_5.1 = (f32[7,256,128]{2,1,0:T(8,128)S(1)}, f32[7,256,128]{2,1,0:T(8,128)S(1)}, f32[7,256,128]{2,1,0:T(8,128)S(1)}) custom-call(s32[1]{0:T(128)} %bitcast.1.rank_ref, bf16[2,7,256,128]{3,2,1,0:T(8,128)(2,1)S(1)} %get-tuple-element.21.rot_ref, bf16[512,128]{1,0:T(8,128)(2,1)S(1)} %collective-permute-done.4.refs_0_, ...), custom_call_target="tpu_custom_call" | custom-call | flops 1 | bytes 1 | tf_op jit(solution)/shard_map/attend_5/pallas_call | solution.py:300
  18.3 1.1 %collective-permute-done.3.refs_1_ = bf16[512,128]{1,0:T(8,128)(2,1)S(1)} collective-permute-done((bf16[512,128]{1,0:T(8,128)(2,1)S(1)}, bf16[512,128]{1,0:T(8,128)(2,1)S(1)}, u32[]{:S(2)}, u32[]{:S(2)}) %collective-permute-start.3) | collective-permute-done | bytes 131104 | tf_op jit(solution)/shard_map/ppermute | solution.py:420
  19.4 1.0 %attend_4_7.2.refs_0_.own_ref = bf16[128,896]{1,0:T(8,128)(2,1)S(1)} custom-call(s32[1]{0:T(128)} %bitcast.1.rank_ref, bf16[2,7,256,128]{3,2,1,0:T(8,128)(2,1)S(1)} %get-tuple-element.21.rot_ref, bf16[512,128]{1,0:T(8,128)(2,1)S(1)} %collective-permute-done.2.refs_0_, bf16[512,128]{1,0:T(8,128)(2,1)S(1)} %collective-permute-done.3.refs_1_, ...), custom_call_target="tpu_custom_call" | custom-call | flops 1 | bytes 1 | tf_op jit(solution)/shard_map/attend_4_7/pallas_call | solution.py:300
  20.5 1.0 %attend_4_7.3.refs_1_.own_ref = bf16[128,896]{1,0:T(8,128)(2,1)S(1)} custom-call(s32[1]{0:T(128)} %bitcast.1.rank_ref, bf16[2,7,256,128]{3,2,1,0:T(8,128)(2,1)S(1)} %get-tuple-element.21.rot_ref, bf16[512,128]{1,0:T(8,128)(2,1)S(1)} %collective-permute-done.2.refs_0_, bf16[512,128]{1,0:T(8,128)(2,1)S(1)} %collective-permute-done.3.refs_1_, ...), custom_call_target="tpu_custom_call" | custom-call | flops 1 | bytes 1 | tf_op jit(solution)/shard_map/attend_4_7/pallas_call | solution.py:300
  22.0 0.7 %away.2 = bf16[128,896]{1,0:T(8,128)(2,1)S(1)} custom-call(bf16[128,896]{1,0:T(8,128)(2,1)S(1)} %attend_4_7.2.refs_0_.own_ref, bf16[128,896]{1,0:T(8,128)(2,1)S(1)} %collective-permute-done.8.refs_2_.twin_ref, bf16[896,896]{1,0:T(8,128)(2,1)S(1)} %get-tuple-element.35.own_weight, bf16[896,896]{1,0:T(8,128)(2,1)S(1)} %get-tuple-element.36.twin_weight), custom_call_target="tpu_custom_call" | custom-call | flops 1 | bytes 1 | tf_op jit(solution)/shard_map/away/pallas_call | solution.py:330
  22.7 0.6 %collective-permute-start.10 = (bf16[128,896]{1,0:T(8,128)(2,1)S(1)}, bf16[128,896]{1,0:T(8,128)(2,1)S(1)}, u32[]{:S(2)}, u32[]{:S(2)}) collective-permute-start(bf16[128,896]{1,0:T(8,128)(2,1)S(1)} %away.2), channel_id=1, source_target_pairs={{0,2},{1,3},{2,0},{3,1},{4,6},{5,7},{6,4},{7,5},{8,10},{9,11},{10,... | collective-permute-start | bytes 688136 | tf_op jit(solution)/shard_map/ppermute | solution.py:411
  23.3 0.7 %away.3 = bf16[128,896]{1,0:T(8,128)(2,1)S(1)} custom-call(bf16[128,896]{1,0:T(8,128)(2,1)S(1)} %attend_4_7.3.refs_1_.own_ref, bf16[128,896]{1,0:T(8,128)(2,1)S(1)} %collective-permute-done.9.refs_3_.twin_ref, bf16[896,896]{1,0:T(8,128)(2,1)S(1)} %get-tuple-element.35.own_weight, bf16[896,896]{1,0:T(8,128)(2,1)S(1)} %get-tuple-element.36.twin_weight), custom_call_target="tpu_custom_call" | custom-call | flops 1 | bytes 1 | tf_op jit(solution)/shard_map/away/pallas_call | solution.py:330
  24.1 1.6 %collective-permute-start.11 = (bf16[128,896]{1,0:T(8,128)(2,1)S(1)}, bf16[128,896]{1,0:T(8,128)(2,1)S(1)}, u32[]{:S(2)}, u32[]{:S(2)}) collective-permute-start(bf16[128,896]{1,0:T(8,128)(2,1)S(1)} %away.3), channel_id=1, source_target_pairs={{0,2},{1,3},{2,0},{3,1},{4,6},{5,7},{6,4},{7,5},{8,10},{9,11},{10,... | collective-permute-start | bytes 688136 | tf_op jit(solution)/shard_map/ppermute | solution.py:411
  25.7 3.2 %home.1.home_ref = f32[256,896]{1,0:T(8,128)S(1)} custom-call(s32[1]{0:T(128)} %bitcast.place_ref.refs_5_, bf16[896,3584]{1,0:T(8,128)(2,1)} %own_hbm.1, bf16[896,3584]{1,0:T(8,128)(2,1)} %collective-permute-done.refs_6_.twin_hbm, bf16[128,896]{1,0:T(8,128)(2,1)S(1)} %attend_4_7.2.refs_0_.own_ref, bf16[128,896]{1,0:T(8,128)(2,1)S(1)} %attend_4_7.3.refs_1_.own_ref, ...), custom_call_target="tpu_custom_call" | custom-call | flops 1 | bytes 1 | tf_op jit(solution)/shard_map/home/pallas_call | solution.py:364
  28.9 2.4 %collective-permute-done.10.refs_0_ = bf16[128,896]{1,0:T(8,128)(2,1)S(1)} collective-permute-done((bf16[128,896]{1,0:T(8,128)(2,1)S(1)}, bf16[128,896]{1,0:T(8,128)(2,1)S(1)}, u32[]{:S(2)}, u32[]{:S(2)}) %collective-permute-start.10) | collective-permute-done | bytes 229408 | tf_op jit(solution)/shard_map/ppermute | solution.py:411
  31.3 4.0 %collective-permute-done.11.refs_1_ = bf16[128,896]{1,0:T(8,128)(2,1)S(1)} collective-permute-done((bf16[128,896]{1,0:T(8,128)(2,1)S(1)}, bf16[128,896]{1,0:T(8,128)(2,1)S(1)}, u32[]{:S(2)}, u32[]{:S(2)}) %collective-permute-start.11) | collective-permute-done | bytes 229408 | tf_op jit(solution)/shard_map/ppermute | solution.py:411
  35.3 0.8 %close.1 = bf16[256,896]{1,0:T(8,128)(2,1)} custom-call(f32[256,896]{1,0:T(8,128)S(1)} %home.1.home_ref, bf16[128,896]{1,0:T(8,128)(2,1)S(1)} %collective-permute-done.10.refs_0_, bf16[128,896]{1,0:T(8,128)(2,1)S(1)} %collective-permute-done.11.refs_1_), custom_call_target="tpu_custom_call" | custom-call | flops 1 | bytes 1 | tf_op jit(solution)/shard_map/close/pallas_call | solution.py:395
  (11 shorter events, 0.9 us)
Async XLA Ops:
  0.0 14.5 %collective-permute-start = (bf16[896,3584]{1,0:T(8,128)(2,1)}, bf16[896,3584]{1,0:T(8,128)(2,1)}, u32[]{:S(2)}, u32[]{:S(2)}) collective-permute-start(bf16[896,3584]{1,0:T(8,128)(2,1)} %own_hbm.1), channel_id=1, source_target_pairs={{0,1},{1,0},{2,3},{3,2},{4,5},{5,4},{6,7},{7,6},{8,9},{9,8},{10,11... | collective-permute-start | bytes 19267592 | tf_op jit(solution)/shard_map/ppermute | solution.py:411
  1.1 8.2 %collective-permute-start.1 = (bf16[512,128]{1,0:T(8,128)(2,1)S(1)}, bf16[512,128]{1,0:T(8,128)(2,1)S(1)}, u32[]{:S(2)}, u32[]{:S(2)}) collective-permute-start(bf16[512,128]{1,0:T(8,128)(2,1)S(1)} %rotate_keys.1.piece_ref), channel_id=1, source_target_pairs={{0,24},{4,28},{8,16},{12,20},{16,8},{20,12},{24,0},{28,4},{1,25},{... | collective-permute-start | bytes 393224 | tf_op jit(solution)/shard_map/ppermute | solution.py:411
  1.4 9.9 %collective-permute-start.7 = (bf16[512,128]{1,0:T(8,128)(2,1)S(1)}, bf16[512,128]{1,0:T(8,128)(2,1)S(1)}, u32[]{:S(2)}, u32[]{:S(2)}) collective-permute-start(bf16[512,128]{1,0:T(8,128)(2,1)S(1)} %rotate_keys.1.piece_ref), channel_id=1, source_target_pairs={{0,8},{4,12},{8,0},{12,4},{16,24},{20,28},{24,16},{28,20},{1,9},{5... | collective-permute-start | bytes 393224 | tf_op jit(solution)/shard_map/ppermute | solution.py:411
  2.1 10.0 %collective-permute-start.6 = (bf16[512,128]{1,0:T(8,128)(2,1)S(1)}, bf16[512,128]{1,0:T(8,128)(2,1)S(1)}, u32[]{:S(2)}, u32[]{:S(2)}) collective-permute-start(bf16[512,128]{1,0:T(8,128)(2,1)S(1)} %rotate_keys.1.piece_ref), channel_id=1, source_target_pairs={{0,4},{4,0},{8,12},{12,8},{16,20},{20,16},{24,28},{28,24},{1,5},{5... | collective-permute-start | bytes 393224 | tf_op jit(solution)/shard_map/ppermute | solution.py:411
  3.6 10.8 %collective-permute-start.5 = (bf16[512,128]{1,0:T(8,128)(2,1)S(1)}, bf16[512,128]{1,0:T(8,128)(2,1)S(1)}, u32[]{:S(2)}, u32[]{:S(2)}) collective-permute-start(bf16[512,128]{1,0:T(8,128)(2,1)S(1)} %rotate_keys.1.piece_ref), channel_id=1, source_target_pairs={{0,12},{4,8},{8,4},{12,0},{16,28},{20,24},{24,20},{28,16},{1,13},{... | collective-permute-start | bytes 393224 | tf_op jit(solution)/shard_map/ppermute | solution.py:411
  9.3 7.8 %collective-permute-start.4 = (bf16[512,128]{1,0:T(8,128)(2,1)S(1)}, bf16[512,128]{1,0:T(8,128)(2,1)S(1)}, u32[]{:S(2)}, u32[]{:S(2)}) collective-permute-start(bf16[512,128]{1,0:T(8,128)(2,1)S(1)} %collective-permute-done.1.refs_1_), channel_id=1, source_target_pairs={{0,1},{1,0},{2,3},{3,2},{4,5},{5,4},{6,7},{7,6},{8,9},{9,8},{10,11... | collective-permute-start | bytes 393224 | tf_op jit(solution)/shard_map/ppermute | solution.py:420
  11.3 8.1 %collective-permute-start.3 = (bf16[512,128]{1,0:T(8,128)(2,1)S(1)}, bf16[512,128]{1,0:T(8,128)(2,1)S(1)}, u32[]{:S(2)}, u32[]{:S(2)}) collective-permute-start(bf16[512,128]{1,0:T(8,128)(2,1)S(1)} %collective-permute-done.1.refs_1_), channel_id=1, source_target_pairs={{0,1},{1,0},{2,3},{3,2},{4,5},{5,4},{6,7},{7,6},{8,9},{9,8},{10,11... | collective-permute-start | bytes 393224 | tf_op jit(solution)/shard_map/ppermute | solution.py:420
  12.1 7.3 %collective-permute-start.2 = (bf16[512,128]{1,0:T(8,128)(2,1)S(1)}, bf16[512,128]{1,0:T(8,128)(2,1)S(1)}, u32[]{:S(2)}, u32[]{:S(2)}) collective-permute-start(bf16[512,128]{1,0:T(8,128)(2,1)S(1)} %collective-permute-done.1.refs_1_), channel_id=1, source_target_pairs={{0,1},{1,0},{2,3},{3,2},{4,5},{5,4},{6,7},{7,6},{8,9},{9,8},{10,11... | collective-permute-start | bytes 393224 | tf_op jit(solution)/shard_map/ppermute | solution.py:420
  20.4 1.6 %collective-permute-start.8 = (bf16[128,896]{1,0:T(8,128)(2,1)S(1)}, bf16[128,896]{1,0:T(8,128)(2,1)S(1)}, u32[]{:S(2)}, u32[]{:S(2)}) collective-permute-start(bf16[128,896]{1,0:T(8,128)(2,1)S(1)} %attend_4_7.2.refs_0_.own_ref), channel_id=1, source_target_pairs={{0,1},{1,0},{2,3},{3,2},{4,5},{5,4},{6,7},{7,6},{8,9},{9,8},{10,11... | collective-permute-start | bytes 688136 | tf_op jit(solution)/shard_map/ppermute | solution.py:411
  21.4 1.9 %collective-permute-start.9 = (bf16[128,896]{1,0:T(8,128)(2,1)S(1)}, bf16[128,896]{1,0:T(8,128)(2,1)S(1)}, u32[]{:S(2)}, u32[]{:S(2)}) collective-permute-start(bf16[128,896]{1,0:T(8,128)(2,1)S(1)} %attend_4_7.3.refs_1_.own_ref), channel_id=1, source_target_pairs={{0,1},{1,0},{2,3},{3,2},{4,5},{5,4},{6,7},{7,6},{8,9},{9,8},{10,11... | collective-permute-start | bytes 688136 | tf_op jit(solution)/shard_map/ppermute | solution.py:411
  22.7 8.5 %collective-permute-start.10 = (bf16[128,896]{1,0:T(8,128)(2,1)S(1)}, bf16[128,896]{1,0:T(8,128)(2,1)S(1)}, u32[]{:S(2)}, u32[]{:S(2)}) collective-permute-start(bf16[128,896]{1,0:T(8,128)(2,1)S(1)} %away.2), channel_id=1, source_target_pairs={{0,2},{1,3},{2,0},{3,1},{4,6},{5,7},{6,4},{7,5},{8,10},{9,11},{10,... | collective-permute-start | bytes 688136 | tf_op jit(solution)/shard_map/ppermute | solution.py:411
  24.1 11.2 %collective-permute-start.11 = (bf16[128,896]{1,0:T(8,128)(2,1)S(1)}, bf16[128,896]{1,0:T(8,128)(2,1)S(1)}, u32[]{:S(2)}, u32[]{:S(2)}) collective-permute-start(bf16[128,896]{1,0:T(8,128)(2,1)S(1)} %away.3), channel_id=1, source_target_pairs={{0,2},{1,3},{2,0},{3,1},{4,6},{5,7},{6,4},{7,5},{8,10},{9,11},{10,... | collective-permute-start | bytes 688136 | tf_op jit(solution)/shard_map/ppermute | solution.py:411

commit v8 on v7

--- a/solution.py
+++ b/solution.py
@@ -377,34 +377,29 @@
     )(place, in_hbm(own_weight), in_hbm(twin_weight), *own, *twin)
 
 
-def close_kernel(home_ref, *refs):
-    *landed_refs, out_hbm, sum_ref, sems = refs
-    copies, start = [], 0
-    for at, landed in enumerate(landed_refs):
-        rows = pl.ds(start, landed.shape[0])
-        sum_ref[rows] = (home_ref[rows] + landed[...].astype(jnp.float32)).astype(sum_ref.dtype)
-        copies.append(pltpu.make_async_copy(sum_ref.at[rows], out_hbm.at[rows], sems.at[at]))
-        copies[-1].start()
-        start += landed.shape[0]
-    for copy in copies:
-        copy.wait()
-
-
-def close(home, landed):
+def close_kernel(start, home_ref, landed_ref, *refs):
+    out_hbm, sum_ref, sem = refs[-3:]
+    rows = pl.ds(start, sum_ref.shape[0])
+    sum_ref[...] = (home_ref[rows] + landed_ref[...].astype(jnp.float32)).astype(sum_ref.dtype)
+    copy = pltpu.make_async_copy(sum_ref, out_hbm.at[rows], sem)
+    copy.start()
+    copy.wait()
+
+
+def close(start, home, landed, out):
+    rows, columns = landed.shape
     vmem, hbm = (pl.BlockSpec(memory_space=space) for space in (VMEM, HBM))
     return pl.pallas_call(
-        close_kernel,
-        in_specs=[vmem] * (1 + len(landed)),
+        functools.partial(close_kernel, start),
+        in_specs=[vmem, vmem] + ([] if out is None else [hbm]),
         out_specs=hbm,
-        out_shape=jax.ShapeDtypeStruct(home.shape, jnp.bfloat16),
-        scratch_shapes=[
-            pltpu.VMEM(home.shape, jnp.bfloat16),
-            pltpu.SemaphoreType.DMA((len(landed),)),
-        ],
+        out_shape=HBM(home.shape, jnp.bfloat16),
+        input_output_aliases={} if out is None else {2: 0},
+        scratch_shapes=[pltpu.VMEM((rows, columns), jnp.bfloat16), pltpu.SemaphoreType.DMA],
         cost_estimate=LIGHT,
         compiler_params=pltpu.CompilerParams(vmem_limit_bytes=LIMIT),
-        name="close",
-    )(home, *landed)
+        name="close_%d" % start,
+    )(home, landed, *([] if out is None else [out]))
 
 
 def swap(x, axis, size, bits):
@@ -443,7 +438,7 @@
             late = 2 * offset >= seq
             pieces[offset] = swap_late(source, seq, kv, step) if late else swap(source, "seq", seq, step)
 
-        twin_weight = swap(out_weight, "kv", kv, 1)
+        twin_weight = swap(after(out_weight, pieces[0]), "kv", kv, 1)
         for offset in FIRST:
             send(offset, offset)
         rot, *state = begin(
@@ -477,7 +472,11 @@
             )
             landed.append(swap(away, "kv", kv, 2))
         home = project_home(place, own, twin, out_weight, twin_weight)
-        return close(home, landed)
+        out, start = None, 0
+        for rows in landed:
+            out = close(start, home, rows, out)
+            start += rows.shape[0]
+        return out
 
     return shards
 

time: 36.3 us -> 36.1 us (level)
  waiting for transfers between devices: 10.5 us -> 10.1 us
    pallas_call x1 -> x2, Pallas kernels: 0.84 us -> 1.47 us  [close(): pl.pallas_call(functools.partial(close_kernel, start), in_specs=[vmem, vm...]
    ppermute x9, waiting for transfers between devices: 8.31 us -> 7.83 us  [swap(): return lax.ppermute(x, axis, [(i, i ^ bits) for i in range(size)])]
    pallas_call x5, Pallas kernels: 6.24 us -> 5.81 us  [attend(): pl.pallas_call(functools.partial(attend_kernel, tuple(offsets), rot.shape...]
  transfers between devices with their start and end apart: 12 -> 12, of which waited for: 5 -> 6; matrix products, arithmetic and copies ran while one was open for 0% -> 0% of each run, Pallas kernels for 38% -> 36%
where the time goes in v8:
time: 36.1 us; the launch traced here: 35.9 us
  Pallas kernels  15.5 us (43%)
  starting transfers between devices  10.1 us (28%)
  waiting for transfers between devices  10.1 us (28%)
    ppermute x9, waiting for transfers between devices, swap(): return lax.ppermute(x, axis, [(i, i ^ bits) for i in range(size)])  7.83 us
    ppermute x9, starting transfers between devices, swap(): return lax.ppermute(x, axis, [(i, i ^ bits) for i in range(size)])  6.63 us
    pallas_call x5, Pallas kernels, attend(): pl.pallas_call(functools.partial(attend_kernel, tuple(offsets), rot.shape...  5.81 us
    ppermute x3, starting transfers between devices, swap_late(): return lax.ppermute(x, ('seq', 'kv'), pairs)  3.49 us
    pallas_call x1, Pallas kernels, project_home(): pl.pallas_call(functools.partial(home_kernel, len(own)), in_specs=[smem,...  3.2 us
    pallas_call x1, Pallas kernels, begin(): pl.pallas_call(functools.partial(begin_kernel, kinds), in_specs=[smem, sm...  2.5 us
    ppermute x3, waiting for transfers between devices, swap_late(): return lax.ppermute(x, ('seq', 'kv'), pairs)  2.28 us
    pallas_call x2, Pallas kernels, close(): pl.pallas_call(functools.partial(close_kernel, start), in_specs=[vmem, vm...  1.47 us
  transfers between devices with their start and end apart: 12, of which 6 were waited for; matrix products, arithmetic and copies ran while one was open for 0% of the time, Pallas kernels for 36%

profile of v8, /device:TPU:26, one launch (start us, length us, event | category | flops | bytes accessed | tf_op | source)
XLA Modules:
  0.0 35.9 jit_solution(14298348418007025944)
XLA Ops:
  0.0 1.1 %rotate_keys.1.piece_ref = bf16[512,128]{1,0:T(8,128)(2,1)S(1)} custom-call(s32[1]{0:T(128)} %bitcast.1.rank_ref, bf16[256,128]{1,0:T(8,128)(2,1)} %bitcast.6, bf16[256,128]{1,0:T(8,128)(2,1)} %bitcast.7, f32[1536,128]{1,0:T(8,128)} %constant.13.clone.cos_hbm, f32[1536,128]{1,0:T(8,128)} %constant.14.clone.sin_hbm), custom_call_target="tpu_custom_call" | custom-call | tf_op jit(solution)/shard_map/rotate_keys/pallas_call | solution.py:71
  1.5 0.7 %collective-permute-start.7 = (bf16[512,128]{1,0:T(8,128)(2,1)S(1)}, bf16[512,128]{1,0:T(8,128)(2,1)S(1)}, u32[]{:S(2)}, u32[]{:S(2)}) collective-permute-start(bf16[512,128]{1,0:T(8,128)(2,1)S(1)} %rotate_keys.1.piece_ref), channel_id=1, source_target_pairs={{0,8},{4,12},{8,0},{12,4},{16,24},{20,28},{24,16},{28,20},{1,9},{5... | collective-permute-start | bytes 393224 | tf_op jit(solution)/shard_map/ppermute | solution.py:406
  2.2 1.5 %collective-permute-start.6 = (bf16[512,128]{1,0:T(8,128)(2,1)S(1)}, bf16[512,128]{1,0:T(8,128)(2,1)S(1)}, u32[]{:S(2)}, u32[]{:S(2)}) collective-permute-start(bf16[512,128]{1,0:T(8,128)(2,1)S(1)} %rotate_keys.1.piece_ref), channel_id=1, source_target_pairs={{0,4},{4,0},{8,12},{12,8},{16,20},{20,16},{24,28},{28,24},{1,5},{5... | collective-permute-start | bytes 393224 | tf_op jit(solution)/shard_map/ppermute | solution.py:406
  3.7 1.3 %collective-permute-start.5 = (bf16[512,128]{1,0:T(8,128)(2,1)S(1)}, bf16[512,128]{1,0:T(8,128)(2,1)S(1)}, u32[]{:S(2)}, u32[]{:S(2)}) collective-permute-start(bf16[512,128]{1,0:T(8,128)(2,1)S(1)} %rotate_keys.1.piece_ref), channel_id=1, source_target_pairs={{0,12},{4,8},{8,4},{12,0},{16,28},{20,24},{24,20},{28,16},{1,13},{... | collective-permute-start | bytes 393224 | tf_op jit(solution)/shard_map/ppermute | solution.py:406
  5.0 2.5 %attend_0.1 = (bf16[2,7,256,128]{3,2,1,0:T(8,128)(2,1)S(1)}, f32[7,256,128]{2,1,0:T(8,128)S(1)}, f32[7,256,128]{2,1,0:T(8,128)S(1)}, f32[7,256,128]{2,1,0:T(8,128)S(1)}, bf16[896,896]{1,0:T(8,128)(2,1)S(1)}) custom-call(s32[1]{0:T(128)} %bitcast.1.rank_ref, s32[1]{0:T(128)} %bitcast.place_ref.refs_5_, bf16[7,256,128]{2,1,0:T(8,128)(2,1)} %bitcast.5, ...), custom_call_target="tpu_custom_call" | custom-call | flops 1 | bytes 1 | tf_op jit(solution)/shard_map/attend_0/pallas_call | solution.py:188
  7.5 1.9 %collective-permute-done.1.refs_1_ = bf16[512,128]{1,0:T(8,128)(2,1)S(1)} collective-permute-done((bf16[512,128]{1,0:T(8,128)(2,1)S(1)}, bf16[512,128]{1,0:T(8,128)(2,1)S(1)}, u32[]{:S(2)}, u32[]{:S(2)}) %collective-permute-start.1) | collective-permute-done | bytes 131104 | tf_op jit(solution)/shard_map/ppermute | solution.py:406
  9.4 1.9 %collective-permute-start.4 = (bf16[512,128]{1,0:T(8,128)(2,1)S(1)}, bf16[512,128]{1,0:T(8,128)(2,1)S(1)}, u32[]{:S(2)}, u32[]{:S(2)}) collective-permute-start(bf16[512,128]{1,0:T(8,128)(2,1)S(1)} %collective-permute-done.1.refs_1_), channel_id=1, source_target_pairs={{0,1},{1,0},{2,3},{3,2},{4,5},{5,4},{6,7},{7,6},{8,9},{9,8},{10,11... | collective-permute-start | bytes 393224 | tf_op jit(solution)/shard_map/ppermute | solution.py:415
  11.3 0.8 %collective-permute-start.3 = (bf16[512,128]{1,0:T(8,128)(2,1)S(1)}, bf16[512,128]{1,0:T(8,128)(2,1)S(1)}, u32[]{:S(2)}, u32[]{:S(2)}) collective-permute-start(bf16[512,128]{1,0:T(8,128)(2,1)S(1)} %collective-permute-done.1.refs_1_), channel_id=1, source_target_pairs={{0,1},{1,0},{2,3},{3,2},{4,5},{5,4},{6,7},{7,6},{8,9},{9,8},{10,11... | collective-permute-start | bytes 393224 | tf_op jit(solution)/shard_map/ppermute | solution.py:415
  12.2 0.8 %collective-permute-start.2 = (bf16[512,128]{1,0:T(8,128)(2,1)S(1)}, bf16[512,128]{1,0:T(8,128)(2,1)S(1)}, u32[]{:S(2)}, u32[]{:S(2)}) collective-permute-start(bf16[512,128]{1,0:T(8,128)(2,1)S(1)} %collective-permute-done.1.refs_1_), channel_id=1, source_target_pairs={{0,1},{1,0},{2,3},{3,2},{4,5},{5,4},{6,7},{7,6},{8,9},{9,8},{10,11... | collective-permute-start | bytes 393224 | tf_op jit(solution)/shard_map/ppermute | solution.py:415
  12.9 1.5 %attend_1_2.1 = (f32[7,256,128]{2,1,0:T(8,128)S(1)}, f32[7,256,128]{2,1,0:T(8,128)S(1)}, f32[7,256,128]{2,1,0:T(8,128)S(1)}) custom-call(s32[1]{0:T(128)} %bitcast.1.rank_ref, bf16[2,7,256,128]{3,2,1,0:T(8,128)(2,1)S(1)} %get-tuple-element.23.rot_ref, bf16[512,128]{1,0:T(8,128)(2,1)S(1)} %collective-permute-done.6.refs_0_, ...), custom_call_target="tpu_custom_call" | custom-call | flops 1 | bytes 1 | tf_op jit(solution)/shard_map/attend_1_2/pallas_call | solution.py:300
  14.5 1.5 %attend_3_6.1 = (f32[7,256,128]{2,1,0:T(8,128)S(1)}, f32[7,256,128]{2,1,0:T(8,128)S(1)}, f32[7,256,128]{2,1,0:T(8,128)S(1)}, bf16[896,896]{1,0:T(8,128)(2,1)S(1)}) custom-call(s32[1]{0:T(128)} %bitcast.1.rank_ref, bf16[2,7,256,128]{3,2,1,0:T(8,128)(2,1)S(1)} %get-tuple-element.23.rot_ref, bf16[512,128]{1,0:T(8,128)(2,1)S(1)} %collective-permute-done.5.refs_0_, ...), custom_call_target="tpu_custom_call" | custom-call | flops 1 | bytes 1 | tf_op jit(solution)/shard_map/attend_3_6/pallas_call | solution.py:300
  16.1 1.2 %collective-permute-done.4.refs_0_ = bf16[512,128]{1,0:T(8,128)(2,1)S(1)} collective-permute-done((bf16[512,128]{1,0:T(8,128)(2,1)S(1)}, bf16[512,128]{1,0:T(8,128)(2,1)S(1)}, u32[]{:S(2)}, u32[]{:S(2)}) %collective-permute-start.4) | collective-permute-done | bytes 131104 | tf_op jit(solution)/shard_map/ppermute | solution.py:415
  17.3 1.0 %attend_5.1 = (f32[7,256,128]{2,1,0:T(8,128)S(1)}, f32[7,256,128]{2,1,0:T(8,128)S(1)}, f32[7,256,128]{2,1,0:T(8,128)S(1)}) custom-call(s32[1]{0:T(128)} %bitcast.1.rank_ref, bf16[2,7,256,128]{3,2,1,0:T(8,128)(2,1)S(1)} %get-tuple-element.23.rot_ref, bf16[512,128]{1,0:T(8,128)(2,1)S(1)} %collective-permute-done.4.refs_0_, ...), custom_call_target="tpu_custom_call" | custom-call | flops 1 | bytes 1 | tf_op jit(solution)/shard_map/attend_5/pallas_call | solution.py:300
  18.2 1.1 %collective-permute-done.3.refs_1_ = bf16[512,128]{1,0:T(8,128)(2,1)S(1)} collective-permute-done((bf16[512,128]{1,0:T(8,128)(2,1)S(1)}, bf16[512,128]{1,0:T(8,128)(2,1)S(1)}, u32[]{:S(2)}, u32[]{:S(2)}) %collective-permute-start.3) | collective-permute-done | bytes 131104 | tf_op jit(solution)/shard_map/ppermute | solution.py:415
  19.3 0.9 %attend_4_7.2.refs_0_.own_ref = bf16[128,896]{1,0:T(8,128)(2,1)S(1)} custom-call(s32[1]{0:T(128)} %bitcast.1.rank_ref, bf16[2,7,256,128]{3,2,1,0:T(8,128)(2,1)S(1)} %get-tuple-element.23.rot_ref, bf16[512,128]{1,0:T(8,128)(2,1)S(1)} %collective-permute-done.2.refs_0_, bf16[512,128]{1,0:T(8,128)(2,1)S(1)} %collective-permute-done.3.refs_1_, ...), custom_call_target="tpu_custom_call" | custom-call | flops 1 | bytes 1 | tf_op jit(solution)/shard_map/attend_4_7/pallas_call | solution.py:300
  20.3 0.9 %attend_4_7.3.refs_1_.own_ref = bf16[128,896]{1,0:T(8,128)(2,1)S(1)} custom-call(s32[1]{0:T(128)} %bitcast.1.rank_ref, bf16[2,7,256,128]{3,2,1,0:T(8,128)(2,1)S(1)} %get-tuple-element.23.rot_ref, bf16[512,128]{1,0:T(8,128)(2,1)S(1)} %collective-permute-done.2.refs_0_, bf16[512,128]{1,0:T(8,128)(2,1)S(1)} %collective-permute-done.3.refs_1_, ...), custom_call_target="tpu_custom_call" | custom-call | flops 1 | bytes 1 | tf_op jit(solution)/shard_map/attend_4_7/pallas_call | solution.py:300
  21.8 0.7 %away.3 = bf16[128,896]{1,0:T(8,128)(2,1)S(1)} custom-call(bf16[128,896]{1,0:T(8,128)(2,1)S(1)} %attend_4_7.2.refs_0_.own_ref, bf16[128,896]{1,0:T(8,128)(2,1)S(1)} %collective-permute-done.8.refs_2_.twin_ref, bf16[896,896]{1,0:T(8,128)(2,1)S(1)} %get-tuple-element.37.own_weight, bf16[896,896]{1,0:T(8,128)(2,1)S(1)} %get-tuple-element.38.twin_weight), custom_call_target="tpu_custom_call" | custom-call | flops 1 | bytes 1 | tf_op jit(solution)/shard_map/away/pallas_call | solution.py:330
  23.1 0.7 %away.2 = bf16[128,896]{1,0:T(8,128)(2,1)S(1)} custom-call(bf16[128,896]{1,0:T(8,128)(2,1)S(1)} %attend_4_7.3.refs_1_.own_ref, bf16[128,896]{1,0:T(8,128)(2,1)S(1)} %collective-permute-done.9.refs_3_.twin_ref, bf16[896,896]{1,0:T(8,128)(2,1)S(1)} %get-tuple-element.37.own_weight, bf16[896,896]{1,0:T(8,128)(2,1)S(1)} %get-tuple-element.38.twin_weight), custom_call_target="tpu_custom_call" | custom-call | flops 1 | bytes 1 | tf_op jit(solution)/shard_map/away/pallas_call | solution.py:330
  23.8 1.6 %collective-permute-start.10 = (bf16[128,896]{1,0:T(8,128)(2,1)S(1)}, bf16[128,896]{1,0:T(8,128)(2,1)S(1)}, u32[]{:S(2)}, u32[]{:S(2)}) collective-permute-start(bf16[128,896]{1,0:T(8,128)(2,1)S(1)} %away.2), channel_id=1, source_target_pairs={{0,2},{1,3},{2,0},{3,1},{4,6},{5,7},{6,4},{7,5},{8,10},{9,11},{10,... | collective-permute-start | bytes 688136 | tf_op jit(solution)/shard_map/ppermute | solution.py:406
  25.4 3.2 %home.1.home_ref = f32[256,896]{1,0:T(8,128)S(1)} custom-call(s32[1]{0:T(128)} %bitcast.place_ref.refs_5_, bf16[896,3584]{1,0:T(8,128)(2,1)} %own_hbm.1, bf16[896,3584]{1,0:T(8,128)(2,1)} %collective-permute-done.refs_6_.twin_hbm, bf16[128,896]{1,0:T(8,128)(2,1)S(1)} %attend_4_7.2.refs_0_.own_ref, bf16[128,896]{1,0:T(8,128)(2,1)S(1)} %attend_4_7.3.refs_1_.own_ref, ...), custom_call_target="tpu_custom_call" | custom-call | flops 1 | bytes 1 | tf_op jit(solution)/shard_map/home/pallas_call | solution.py:364
  28.6 2.4 %collective-permute-done.11.landed_ref = bf16[128,896]{1,0:T(8,128)(2,1)S(1)} collective-permute-done((bf16[128,896]{1,0:T(8,128)(2,1)S(1)}, bf16[128,896]{1,0:T(8,128)(2,1)S(1)}, u32[]{:S(2)}, u32[]{:S(2)}) %collective-permute-start.11) | collective-permute-done | bytes 229408 | tf_op jit(solution)/shard_map/ppermute | solution.py:406
  31.0 0.7 %close_0.1.refs_0_ = bf16[256,896]{1,0:T(8,128)(2,1)} custom-call(f32[256,896]{1,0:T(8,128)S(1)} %home.1.home_ref, bf16[128,896]{1,0:T(8,128)(2,1)S(1)} %collective-permute-done.11.landed_ref), custom_call_target="tpu_custom_call" | custom-call | flops 1 | bytes 1 | tf_op jit(solution)/shard_map/close_0/pallas_call | solution.py:392
  31.8 3.4 %collective-permute-done.10.landed_ref = bf16[128,896]{1,0:T(8,128)(2,1)S(1)} collective-permute-done((bf16[128,896]{1,0:T(8,128)(2,1)S(1)}, bf16[128,896]{1,0:T(8,128)(2,1)S(1)}, u32[]{:S(2)}, u32[]{:S(2)}) %collective-permute-start.10) | collective-permute-done | bytes 229408 | tf_op jit(solution)/shard_map/ppermute | solution.py:406
  35.1 0.7 %close_128.1 = bf16[256,896]{1,0:T(8,128)(2,1)} custom-call(f32[256,896]{1,0:T(8,128)S(1)} %home.1.home_ref, bf16[128,896]{1,0:T(8,128)(2,1)S(1)} %collective-permute-done.10.landed_ref, bf16[256,896]{1,0:T(8,128)(2,1)} %close_0.1.refs_0_), custom_call_target="tpu_custom_call", output_to_operand_aliasing={{}: (2, {})} | custom-call | flops 1 | bytes 1 | tf_op jit(solution)/shard_map/close_128/pallas_call | solution.py:392
  (12 shorter events, 1.7 us)
Async XLA Ops:
  1.1 13.4 %collective-permute-start = (bf16[896,3584]{1,0:T(8,128)(2,1)}, bf16[896,3584]{1,0:T(8,128)(2,1)}, u32[]{:S(2)}, u32[]{:S(2)}) collective-permute-start(bf16[896,3584]{1,0:T(8,128)(2,1)} %own_hbm.1), channel_id=1, source_target_pairs={{0,1},{1,0},{2,3},{3,2},{4,5},{5,4},{6,7},{7,6},{8,9},{9,8},{10,11... | collective-permute-start | bytes 19267592 | tf_op jit(solution)/shard_map/ppermute | solution.py:406
  1.2 8.2 %collective-permute-start.1 = (bf16[512,128]{1,0:T(8,128)(2,1)S(1)}, bf16[512,128]{1,0:T(8,128)(2,1)S(1)}, u32[]{:S(2)}, u32[]{:S(2)}) collective-permute-start(bf16[512,128]{1,0:T(8,128)(2,1)S(1)} %rotate_keys.1.piece_ref), channel_id=1, source_target_pairs={{0,24},{4,28},{8,16},{12,20},{16,8},{20,12},{24,0},{28,4},{1,25},{... | collective-permute-start | bytes 393224 | tf_op jit(solution)/shard_map/ppermute | solution.py:406
  1.5 9.8 %collective-permute-start.7 = (bf16[512,128]{1,0:T(8,128)(2,1)S(1)}, bf16[512,128]{1,0:T(8,128)(2,1)S(1)}, u32[]{:S(2)}, u32[]{:S(2)}) collective-permute-start(bf16[512,128]{1,0:T(8,128)(2,1)S(1)} %rotate_keys.1.piece_ref), channel_id=1, source_target_pairs={{0,8},{4,12},{8,0},{12,4},{16,24},{20,28},{24,16},{28,20},{1,9},{5... | collective-permute-start | bytes 393224 | tf_op jit(solution)/shard_map/ppermute | solution.py:406
  2.2 10.0 %collective-permute-start.6 = (bf16[512,128]{1,0:T(8,128)(2,1)S(1)}, bf16[512,128]{1,0:T(8,128)(2,1)S(1)}, u32[]{:S(2)}, u32[]{:S(2)}) collective-permute-start(bf16[512,128]{1,0:T(8,128)(2,1)S(1)} %rotate_keys.1.piece_ref), channel_id=1, source_target_pairs={{0,4},{4,0},{8,12},{12,8},{16,20},{20,16},{24,28},{28,24},{1,5},{5... | collective-permute-start | bytes 393224 | tf_op jit(solution)/shard_map/ppermute | solution.py:406
  3.7 10.8 %collective-permute-start.5 = (bf16[512,128]{1,0:T(8,128)(2,1)S(1)}, bf16[512,128]{1,0:T(8,128)(2,1)S(1)}, u32[]{:S(2)}, u32[]{:S(2)}) collective-permute-start(bf16[512,128]{1,0:T(8,128)(2,1)S(1)} %rotate_keys.1.piece_ref), channel_id=1, source_target_pairs={{0,12},{4,8},{8,4},{12,0},{16,28},{20,24},{24,20},{28,16},{1,13},{... | collective-permute-start | bytes 393224 | tf_op jit(solution)/shard_map/ppermute | solution.py:406
  9.4 7.8 %collective-permute-start.4 = (bf16[512,128]{1,0:T(8,128)(2,1)S(1)}, bf16[512,128]{1,0:T(8,128)(2,1)S(1)}, u32[]{:S(2)}, u32[]{:S(2)}) collective-permute-start(bf16[512,128]{1,0:T(8,128)(2,1)S(1)} %collective-permute-done.1.refs_1_), channel_id=1, source_target_pairs={{0,1},{1,0},{2,3},{3,2},{4,5},{5,4},{6,7},{7,6},{8,9},{9,8},{10,11... | collective-permute-start | bytes 393224 | tf_op jit(solution)/shard_map/ppermute | solution.py:415
  11.3 8.0 %collective-permute-start.3 = (bf16[512,128]{1,0:T(8,128)(2,1)S(1)}, bf16[512,128]{1,0:T(8,128)(2,1)S(1)}, u32[]{:S(2)}, u32[]{:S(2)}) collective-permute-start(bf16[512,128]{1,0:T(8,128)(2,1)S(1)} %collective-permute-done.1.refs_1_), channel_id=1, source_target_pairs={{0,1},{1,0},{2,3},{3,2},{4,5},{5,4},{6,7},{7,6},{8,9},{9,8},{10,11... | collective-permute-start | bytes 393224 | tf_op jit(solution)/shard_map/ppermute | solution.py:415
  12.2 7.1 %collective-permute-start.2 = (bf16[512,128]{1,0:T(8,128)(2,1)S(1)}, bf16[512,128]{1,0:T(8,128)(2,1)S(1)}, u32[]{:S(2)}, u32[]{:S(2)}) collective-permute-start(bf16[512,128]{1,0:T(8,128)(2,1)S(1)} %collective-permute-done.1.refs_1_), channel_id=1, source_target_pairs={{0,1},{1,0},{2,3},{3,2},{4,5},{5,4},{6,7},{7,6},{8,9},{9,8},{10,11... | collective-permute-start | bytes 393224 | tf_op jit(solution)/shard_map/ppermute | solution.py:415
  20.2 1.6 %collective-permute-start.8 = (bf16[128,896]{1,0:T(8,128)(2,1)S(1)}, bf16[128,896]{1,0:T(8,128)(2,1)S(1)}, u32[]{:S(2)}, u32[]{:S(2)}) collective-permute-start(bf16[128,896]{1,0:T(8,128)(2,1)S(1)} %attend_4_7.2.refs_0_.own_ref), channel_id=1, source_target_pairs={{0,1},{1,0},{2,3},{3,2},{4,5},{5,4},{6,7},{7,6},{8,9},{9,8},{10,11... | collective-permute-start | bytes 688136 | tf_op jit(solution)/shard_map/ppermute | solution.py:406
  21.2 1.9 %collective-permute-start.9 = (bf16[128,896]{1,0:T(8,128)(2,1)S(1)}, bf16[128,896]{1,0:T(8,128)(2,1)S(1)}, u32[]{:S(2)}, u32[]{:S(2)}) collective-permute-start(bf16[128,896]{1,0:T(8,128)(2,1)S(1)} %attend_4_7.3.refs_1_.own_ref), channel_id=1, source_target_pairs={{0,1},{1,0},{2,3},{3,2},{4,5},{5,4},{6,7},{7,6},{8,9},{9,8},{10,11... | collective-permute-start | bytes 688136 | tf_op jit(solution)/shard_map/ppermute | solution.py:406
  22.5 8.5 %collective-permute-start.11 = (bf16[128,896]{1,0:T(8,128)(2,1)S(1)}, bf16[128,896]{1,0:T(8,128)(2,1)S(1)}, u32[]{:S(2)}, u32[]{:S(2)}) collective-permute-start(bf16[128,896]{1,0:T(8,128)(2,1)S(1)} %away.3), channel_id=1, source_target_pairs={{0,2},{1,3},{2,0},{3,1},{4,6},{5,7},{6,4},{7,5},{8,10},{9,11},{10,... | collective-permute-start | bytes 688136 | tf_op jit(solution)/shard_map/ppermute | solution.py:406
  23.8 11.3 %collective-permute-start.10 = (bf16[128,896]{1,0:T(8,128)(2,1)S(1)}, bf16[128,896]{1,0:T(8,128)(2,1)S(1)}, u32[]{:S(2)}, u32[]{:S(2)}) collective-permute-start(bf16[128,896]{1,0:T(8,128)(2,1)S(1)} %away.2), channel_id=1, source_target_pairs={{0,2},{1,3},{2,0},{3,1},{4,6},{5,7},{6,4},{7,5},{8,10},{9,11},{10,... | collective-permute-start | bytes 688136 | tf_op jit(solution)/shard_map/ppermute | solution.py:406

commit v9 on v8

--- a/solution.py
+++ b/solution.py
@@ -18,7 +18,7 @@
 SCALE = math.log2(math.e) / math.sqrt(HEAD)
 ROW_CHUNKS = (128, 128)
 TURN = 6
-FIRST = [6, 1, 2, 3]
+FIRST = [6, 1, 2]
 CALLS = [[1, 2], [3, 6], [5], [4, 7]]
 LATER = [5, 4, 7]
 STAGES = [[], [1]]
@@ -445,6 +445,7 @@
             kinds, rank, place, by_head, tables, out_weight, pieces[0]
         )
         state, staged = state[:3], state[3:]
+        send(3, 3, state[0])
         for offset in range(2 * per_span, seq, per_span):
             send(offset, offset & -offset)
             for low in range(1, per_span):

time: 36.1 us -> 36.1 us (level)
  no operation moved by 1% of the time
where the time goes in v9:
time: 36.1 us; the launch traced here: 35.9 us
  Pallas kernels  15.5 us (43%)
  starting transfers between devices  10.2 us (28%)
  waiting for transfers between devices  10 us (28%)
    ppermute x9, waiting for transfers between devices, swap(): return lax.ppermute(x, axis, [(i, i ^ bits) for i in range(size)])  7.76 us
    ppermute x9, starting transfers between devices, swap(): return lax.ppermute(x, axis, [(i, i ^ bits) for i in range(size)])  6.7 us
    pallas_call x5, Pallas kernels, attend(): pl.pallas_call(functools.partial(attend_kernel, tuple(offsets), rot.shape...  5.81 us
    ppermute x3, starting transfers between devices, swap_late(): return lax.ppermute(x, ('seq', 'kv'), pairs)  3.49 us
    pallas_call x1, Pallas kernels, project_home(): pl.pallas_call(functools.partial(home_kernel, len(own)), in_specs=[smem,...  3.2 us
    pallas_call x1, Pallas kernels, begin(): pl.pallas_call(functools.partial(begin_kernel, kinds), in_specs=[smem, sm...  2.5 us
    ppermute x3, waiting for transfers between devices, swap_late(): return lax.ppermute(x, ('seq', 'kv'), pairs)  2.28 us
    pallas_call x2, Pallas kernels, close(): pl.pallas_call(functools.partial(close_kernel, start), in_specs=[vmem, vm...  1.47 us
  transfers between devices with their start and end apart: 12, of which 6 were waited for; matrix products, arithmetic and copies ran while one was open for 0% of the time, Pallas kernels for 36%

profile of v9, /device:TPU:26, one launch (start us, length us, event | category | flops | bytes accessed | tf_op | source)
XLA Modules:
  0.0 35.9 jit_solution(193406352166622685)
XLA Ops:
  0.0 1.1 %rotate_keys.1.piece_ref = bf16[512,128]{1,0:T(8,128)(2,1)S(1)} custom-call(s32[1]{0:T(128)} %bitcast.1.rank_ref, bf16[256,128]{1,0:T(8,128)(2,1)} %bitcast.6, bf16[256,128]{1,0:T(8,128)(2,1)} %bitcast.7, f32[1536,128]{1,0:T(8,128)} %constant.13.clone.cos_hbm, f32[1536,128]{1,0:T(8,128)} %constant.14.clone.sin_hbm), custom_call_target="tpu_custom_call" | custom-call | tf_op jit(solution)/shard_map/rotate_keys/pallas_call | solution.py:71
  1.5 0.7 %collective-permute-start.7 = (bf16[512,128]{1,0:T(8,128)(2,1)S(1)}, bf16[512,128]{1,0:T(8,128)(2,1)S(1)}, u32[]{:S(2)}, u32[]{:S(2)}) collective-permute-start(bf16[512,128]{1,0:T(8,128)(2,1)S(1)} %rotate_keys.1.piece_ref), channel_id=1, source_target_pairs={{0,8},{4,12},{8,0},{12,4},{16,24},{20,28},{24,16},{28,20},{1,9},{5... | collective-permute-start | bytes 393224 | tf_op jit(solution)/shard_map/ppermute | solution.py:406
  2.2 1.5 %collective-permute-start.6 = (bf16[512,128]{1,0:T(8,128)(2,1)S(1)}, bf16[512,128]{1,0:T(8,128)(2,1)S(1)}, u32[]{:S(2)}, u32[]{:S(2)}) collective-permute-start(bf16[512,128]{1,0:T(8,128)(2,1)S(1)} %rotate_keys.1.piece_ref), channel_id=1, source_target_pairs={{0,4},{4,0},{8,12},{12,8},{16,20},{20,16},{24,28},{28,24},{1,5},{5... | collective-permute-start | bytes 393224 | tf_op jit(solution)/shard_map/ppermute | solution.py:406
  3.7 2.5 %attend_0.1 = (bf16[2,7,256,128]{3,2,1,0:T(8,128)(2,1)S(1)}, f32[7,256,128]{2,1,0:T(8,128)S(1)}, f32[7,256,128]{2,1,0:T(8,128)S(1)}, f32[7,256,128]{2,1,0:T(8,128)S(1)}, bf16[896,896]{1,0:T(8,128)(2,1)S(1)}) custom-call(s32[1]{0:T(128)} %bitcast.1.rank_ref, s32[1]{0:T(128)} %bitcast.place_ref.refs_5_, bf16[7,256,128]{2,1,0:T(8,128)(2,1)} %bitcast.5, ...), custom_call_target="tpu_custom_call" | custom-call | flops 1 | bytes 1 | tf_op jit(solution)/shard_map/attend_0/pallas_call | solution.py:188
  6.2 1.4 %collective-permute-start.5 = (bf16[512,128]{1,0:T(8,128)(2,1)S(1)}, bf16[512,128]{1,0:T(8,128)(2,1)S(1)}, u32[]{:S(2)}, u32[]{:S(2)}) collective-permute-start(bf16[512,128]{1,0:T(8,128)(2,1)S(1)} %rotate_keys.1.piece_ref), channel_id=1, source_target_pairs={{0,12},{4,8},{8,4},{12,0},{16,28},{20,24},{24,20},{28,16},{1,13},{... | collective-permute-start | bytes 393224 | tf_op jit(solution)/shard_map/ppermute | solution.py:406
  7.6 1.9 %collective-permute-done.1.refs_1_ = bf16[512,128]{1,0:T(8,128)(2,1)S(1)} collective-permute-done((bf16[512,128]{1,0:T(8,128)(2,1)S(1)}, bf16[512,128]{1,0:T(8,128)(2,1)S(1)}, u32[]{:S(2)}, u32[]{:S(2)}) %collective-permute-start.1) | collective-permute-done | bytes 131104 | tf_op jit(solution)/shard_map/ppermute | solution.py:406
  9.4 1.9 %collective-permute-start.4 = (bf16[512,128]{1,0:T(8,128)(2,1)S(1)}, bf16[512,128]{1,0:T(8,128)(2,1)S(1)}, u32[]{:S(2)}, u32[]{:S(2)}) collective-permute-start(bf16[512,128]{1,0:T(8,128)(2,1)S(1)} %collective-permute-done.1.refs_1_), channel_id=1, source_target_pairs={{0,1},{1,0},{2,3},{3,2},{4,5},{5,4},{6,7},{7,6},{8,9},{9,8},{10,11... | collective-permute-start | bytes 393224 | tf_op jit(solution)/shard_map/ppermute | solution.py:415
  11.3 0.8 %collective-permute-start.3 = (bf16[512,128]{1,0:T(8,128)(2,1)S(1)}, bf16[512,128]{1,0:T(8,128)(2,1)S(1)}, u32[]{:S(2)}, u32[]{:S(2)}) collective-permute-start(bf16[512,128]{1,0:T(8,128)(2,1)S(1)} %collective-permute-done.1.refs_1_), channel_id=1, source_target_pairs={{0,1},{1,0},{2,3},{3,2},{4,5},{5,4},{6,7},{7,6},{8,9},{9,8},{10,11... | collective-permute-start | bytes 393224 | tf_op jit(solution)/shard_map/ppermute | solution.py:415
  12.2 0.8 %collective-permute-start.2 = (bf16[512,128]{1,0:T(8,128)(2,1)S(1)}, bf16[512,128]{1,0:T(8,128)(2,1)S(1)}, u32[]{:S(2)}, u32[]{:S(2)}) collective-permute-start(bf16[512,128]{1,0:T(8,128)(2,1)S(1)} %collective-permute-done.1.refs_1_), channel_id=1, source_target_pairs={{0,1},{1,0},{2,3},{3,2},{4,5},{5,4},{6,7},{7,6},{8,9},{9,8},{10,11... | collective-permute-start | bytes 393224 | tf_op jit(solution)/shard_map/ppermute | solution.py:415
  12.9 1.5 %attend_1_2.1 = (f32[7,256,128]{2,1,0:T(8,128)S(1)}, f32[7,256,128]{2,1,0:T(8,128)S(1)}, f32[7,256,128]{2,1,0:T(8,128)S(1)}) custom-call(s32[1]{0:T(128)} %bitcast.1.rank_ref, bf16[2,7,256,128]{3,2,1,0:T(8,128)(2,1)S(1)} %get-tuple-element.24.rot_ref, bf16[512,128]{1,0:T(8,128)(2,1)S(1)} %collective-permute-done.6.refs_0_, ...), custom_call_target="tpu_custom_call" | custom-call | flops 1 | bytes 1 | tf_op jit(solution)/shard_map/attend_1_2/pallas_call | solution.py:300
  14.5 1.5 %attend_3_6.1 = (f32[7,256,128]{2,1,0:T(8,128)S(1)}, f32[7,256,128]{2,1,0:T(8,128)S(1)}, f32[7,256,128]{2,1,0:T(8,128)S(1)}, bf16[896,896]{1,0:T(8,128)(2,1)S(1)}) custom-call(s32[1]{0:T(128)} %bitcast.1.rank_ref, bf16[2,7,256,128]{3,2,1,0:T(8,128)(2,1)S(1)} %get-tuple-element.24.rot_ref, bf16[512,128]{1,0:T(8,128)(2,1)S(1)} %collective-permute-done.5.refs_0_, ...), custom_call_target="tpu_custom_call" | custom-call | flops 1 | bytes 1 | tf_op jit(solution)/shard_map/attend_3_6/pallas_call | solution.py:300
  16.1 1.2 %collective-permute-done.4.refs_0_ = bf16[512,128]{1,0:T(8,128)(2,1)S(1)} collective-permute-done((bf16[512,128]{1,0:T(8,128)(2,1)S(1)}, bf16[512,128]{1,0:T(8,128)(2,1)S(1)}, u32[]{:S(2)}, u32[]{:S(2)}) %collective-permute-start.4) | collective-permute-done | bytes 131104 | tf_op jit(solution)/shard_map/ppermute | solution.py:415
  17.3 1.0 %attend_5.1 = (f32[7,256,128]{2,1,0:T(8,128)S(1)}, f32[7,256,128]{2,1,0:T(8,128)S(1)}, f32[7,256,128]{2,1,0:T(8,128)S(1)}) custom-call(s32[1]{0:T(128)} %bitcast.1.rank_ref, bf16[2,7,256,128]{3,2,1,0:T(8,128)(2,1)S(1)} %get-tuple-element.24.rot_ref, bf16[512,128]{1,0:T(8,128)(2,1)S(1)} %collective-permute-done.4.refs_0_, ...), custom_call_target="tpu_custom_call" | custom-call | flops 1 | bytes 1 | tf_op jit(solution)/shard_map/attend_5/pallas_call | solution.py:300
  18.2 1.1 %collective-permute-done.3.refs_1_ = bf16[512,128]{1,0:T(8,128)(2,1)S(1)} collective-permute-done((bf16[512,128]{1,0:T(8,128)(2,1)S(1)}, bf16[512,128]{1,0:T(8,128)(2,1)S(1)}, u32[]{:S(2)}, u32[]{:S(2)}) %collective-permute-start.3) | collective-permute-done | bytes 131104 | tf_op jit(solution)/shard_map/ppermute | solution.py:415
  19.3 0.9 %attend_4_7.2.refs_0_.own_ref = bf16[128,896]{1,0:T(8,128)(2,1)S(1)} custom-call(s32[1]{0:T(128)} %bitcast.1.rank_ref, bf16[2,7,256,128]{3,2,1,0:T(8,128)(2,1)S(1)} %get-tuple-element.24.rot_ref, bf16[512,128]{1,0:T(8,128)(2,1)S(1)} %collective-permute-done.2.refs_0_, bf16[512,128]{1,0:T(8,128)(2,1)S(1)} %collective-permute-done.3.refs_1_, ...), custom_call_target="tpu_custom_call" | custom-call | flops 1 | bytes 1 | tf_op jit(solution)/shard_map/attend_4_7/pallas_call | solution.py:300
  20.3 0.9 %attend_4_7.3.refs_1_.own_ref = bf16[128,896]{1,0:T(8,128)(2,1)S(1)} custom-call(s32[1]{0:T(128)} %bitcast.1.rank_ref, bf16[2,7,256,128]{3,2,1,0:T(8,128)(2,1)S(1)} %get-tuple-element.24.rot_ref, bf16[512,128]{1,0:T(8,128)(2,1)S(1)} %collective-permute-done.2.refs_0_, bf16[512,128]{1,0:T(8,128)(2,1)S(1)} %collective-permute-done.3.refs_1_, ...), custom_call_target="tpu_custom_call" | custom-call | flops 1 | bytes 1 | tf_op jit(solution)/shard_map/attend_4_7/pallas_call | solution.py:300
  21.8 0.7 %away.3 = bf16[128,896]{1,0:T(8,128)(2,1)S(1)} custom-call(bf16[128,896]{1,0:T(8,128)(2,1)S(1)} %attend_4_7.2.refs_0_.own_ref, bf16[128,896]{1,0:T(8,128)(2,1)S(1)} %collective-permute-done.8.refs_2_.twin_ref, bf16[896,896]{1,0:T(8,128)(2,1)S(1)} %get-tuple-element.39.own_weight, bf16[896,896]{1,0:T(8,128)(2,1)S(1)} %get-tuple-element.40.twin_weight), custom_call_target="tpu_custom_call" | custom-call | flops 1 | bytes 1 | tf_op jit(solution)/shard_map/away/pallas_call | solution.py:330
  23.1 0.7 %away.2 = bf16[128,896]{1,0:T(8,128)(2,1)S(1)} custom-call(bf16[128,896]{1,0:T(8,128)(2,1)S(1)} %attend_4_7.3.refs_1_.own_ref, bf16[128,896]{1,0:T(8,128)(2,1)S(1)} %collective-permute-done.9.refs_3_.twin_ref, bf16[896,896]{1,0:T(8,128)(2,1)S(1)} %get-tuple-element.39.own_weight, bf16[896,896]{1,0:T(8,128)(2,1)S(1)} %get-tuple-element.40.twin_weight), custom_call_target="tpu_custom_call" | custom-call | flops 1 | bytes 1 | tf_op jit(solution)/shard_map/away/pallas_call | solution.py:330
  23.8 1.6 %collective-permute-start.10 = (bf16[128,896]{1,0:T(8,128)(2,1)S(1)}, bf16[128,896]{1,0:T(8,128)(2,1)S(1)}, u32[]{:S(2)}, u32[]{:S(2)}) collective-permute-start(bf16[128,896]{1,0:T(8,128)(2,1)S(1)} %away.2), channel_id=1, source_target_pairs={{0,2},{1,3},{2,0},{3,1},{4,6},{5,7},{6,4},{7,5},{8,10},{9,11},{10,... | collective-permute-start | bytes 688136 | tf_op jit(solution)/shard_map/ppermute | solution.py:406
  25.4 3.2 %home.1.home_ref = f32[256,896]{1,0:T(8,128)S(1)} custom-call(s32[1]{0:T(128)} %bitcast.place_ref.refs_5_, bf16[896,3584]{1,0:T(8,128)(2,1)} %own_hbm.1, bf16[896,3584]{1,0:T(8,128)(2,1)} %collective-permute-done.refs_6_.twin_hbm, bf16[128,896]{1,0:T(8,128)(2,1)S(1)} %attend_4_7.2.refs_0_.own_ref, bf16[128,896]{1,0:T(8,128)(2,1)S(1)} %attend_4_7.3.refs_1_.own_ref, ...), custom_call_target="tpu_custom_call" | custom-call | flops 1 | bytes 1 | tf_op jit(solution)/shard_map/home/pallas_call | solution.py:364
  28.6 2.4 %collective-permute-done.11.landed_ref = bf16[128,896]{1,0:T(8,128)(2,1)S(1)} collective-permute-done((bf16[128,896]{1,0:T(8,128)(2,1)S(1)}, bf16[128,896]{1,0:T(8,128)(2,1)S(1)}, u32[]{:S(2)}, u32[]{:S(2)}) %collective-permute-start.11) | collective-permute-done | bytes 229408 | tf_op jit(solution)/shard_map/ppermute | solution.py:406
  31.0 0.7 %close_0.1.refs_0_ = bf16[256,896]{1,0:T(8,128)(2,1)} custom-call(f32[256,896]{1,0:T(8,128)S(1)} %home.1.home_ref, bf16[128,896]{1,0:T(8,128)(2,1)S(1)} %collective-permute-done.11.landed_ref), custom_call_target="tpu_custom_call" | custom-call | flops 1 | bytes 1 | tf_op jit(solution)/shard_map/close_0/pallas_call | solution.py:392
  31.8 3.4 %collective-permute-done.10.landed_ref = bf16[128,896]{1,0:T(8,128)(2,1)S(1)} collective-permute-done((bf16[128,896]{1,0:T(8,128)(2,1)S(1)}, bf16[128,896]{1,0:T(8,128)(2,1)S(1)}, u32[]{:S(2)}, u32[]{:S(2)}) %collective-permute-start.10) | collective-permute-done | bytes 229408 | tf_op jit(solution)/shard_map/ppermute | solution.py:406
  35.1 0.7 %close_128.1 = bf16[256,896]{1,0:T(8,128)(2,1)} custom-call(f32[256,896]{1,0:T(8,128)S(1)} %home.1.home_ref, bf16[128,896]{1,0:T(8,128)(2,1)S(1)} %collective-permute-done.10.landed_ref, bf16[256,896]{1,0:T(8,128)(2,1)} %close_0.1.refs_0_), custom_call_target="tpu_custom_call", output_to_operand_aliasing={{}: (2, {})} | custom-call | flops 1 | bytes 1 | tf_op jit(solution)/shard_map/close_128/pallas_call | solution.py:392
  (12 shorter events, 1.7 us)
Async XLA Ops:
  1.1 13.4 %collective-permute-start = (bf16[896,3584]{1,0:T(8,128)(2,1)}, bf16[896,3584]{1,0:T(8,128)(2,1)}, u32[]{:S(2)}, u32[]{:S(2)}) collective-permute-start(bf16[896,3584]{1,0:T(8,128)(2,1)} %own_hbm.1), channel_id=1, source_target_pairs={{0,1},{1,0},{2,3},{3,2},{4,5},{5,4},{6,7},{7,6},{8,9},{9,8},{10,11... | collective-permute-start | bytes 19267592 | tf_op jit(solution)/shard_map/ppermute | solution.py:406
  1.2 8.2 %collective-permute-start.1 = (bf16[512,128]{1,0:T(8,128)(2,1)S(1)}, bf16[512,128]{1,0:T(8,128)(2,1)S(1)}, u32[]{:S(2)}, u32[]{:S(2)}) collective-permute-start(bf16[512,128]{1,0:T(8,128)(2,1)S(1)} %rotate_keys.1.piece_ref), channel_id=1, source_target_pairs={{0,24},{4,28},{8,16},{12,20},{16,8},{20,12},{24,0},{28,4},{1,25},{... | collective-permute-start | bytes 393224 | tf_op jit(solution)/shard_map/ppermute | solution.py:406
  1.5 9.8 %collective-permute-start.7 = (bf16[512,128]{1,0:T(8,128)(2,1)S(1)}, bf16[512,128]{1,0:T(8,128)(2,1)S(1)}, u32[]{:S(2)}, u32[]{:S(2)}) collective-permute-start(bf16[512,128]{1,0:T(8,128)(2,1)S(1)} %rotate_keys.1.piece_ref), channel_id=1, source_target_pairs={{0,8},{4,12},{8,0},{12,4},{16,24},{20,28},{24,16},{28,20},{1,9},{5... | collective-permute-start | bytes 393224 | tf_op jit(solution)/shard_map/ppermute | solution.py:406
  2.2 10.0 %collective-permute-start.6 = (bf16[512,128]{1,0:T(8,128)(2,1)S(1)}, bf16[512,128]{1,0:T(8,128)(2,1)S(1)}, u32[]{:S(2)}, u32[]{:S(2)}) collective-permute-start(bf16[512,128]{1,0:T(8,128)(2,1)S(1)} %rotate_keys.1.piece_ref), channel_id=1, source_target_pairs={{0,4},{4,0},{8,12},{12,8},{16,20},{20,16},{24,28},{28,24},{1,5},{5... | collective-permute-start | bytes 393224 | tf_op jit(solution)/shard_map/ppermute | solution.py:406
  6.2 8.3 %collective-permute-start.5 = (bf16[512,128]{1,0:T(8,128)(2,1)S(1)}, bf16[512,128]{1,0:T(8,128)(2,1)S(1)}, u32[]{:S(2)}, u32[]{:S(2)}) collective-permute-start(bf16[512,128]{1,0:T(8,128)(2,1)S(1)} %rotate_keys.1.piece_ref), channel_id=1, source_target_pairs={{0,12},{4,8},{8,4},{12,0},{16,28},{20,24},{24,20},{28,16},{1,13},{... | collective-permute-start | bytes 393224 | tf_op jit(solution)/shard_map/ppermute | solution.py:406
  9.4 7.8 %collective-permute-start.4 = (bf16[512,128]{1,0:T(8,128)(2,1)S(1)}, bf16[512,128]{1,0:T(8,128)(2,1)S(1)}, u32[]{:S(2)}, u32[]{:S(2)}) collective-permute-start(bf16[512,128]{1,0:T(8,128)(2,1)S(1)} %collective-permute-done.1.refs_1_), channel_id=1, source_target_pairs={{0,1},{1,0},{2,3},{3,2},{4,5},{5,4},{6,7},{7,6},{8,9},{9,8},{10,11... | collective-permute-start | bytes 393224 | tf_op jit(solution)/shard_map/ppermute | solution.py:415
  11.3 8.0 %collective-permute-start.3 = (bf16[512,128]{1,0:T(8,128)(2,1)S(1)}, bf16[512,128]{1,0:T(8,128)(2,1)S(1)}, u32[]{:S(2)}, u32[]{:S(2)}) collective-permute-start(bf16[512,128]{1,0:T(8,128)(2,1)S(1)} %collective-permute-done.1.refs_1_), channel_id=1, source_target_pairs={{0,1},{1,0},{2,3},{3,2},{4,5},{5,4},{6,7},{7,6},{8,9},{9,8},{10,11... | collective-permute-start | bytes 393224 | tf_op jit(solution)/shard_map/ppermute | solution.py:415
  12.2 7.1 %collective-permute-start.2 = (bf16[512,128]{1,0:T(8,128)(2,1)S(1)}, bf16[512,128]{1,0:T(8,128)(2,1)S(1)}, u32[]{:S(2)}, u32[]{:S(2)}) collective-permute-start(bf16[512,128]{1,0:T(8,128)(2,1)S(1)} %collective-permute-done.1.refs_1_), channel_id=1, source_target_pairs={{0,1},{1,0},{2,3},{3,2},{4,5},{5,4},{6,7},{7,6},{8,9},{9,8},{10,11... | collective-permute-start | bytes 393224 | tf_op jit(solution)/shard_map/ppermute | solution.py:415
  20.2 1.6 %collective-permute-start.8 = (bf16[128,896]{1,0:T(8,128)(2,1)S(1)}, bf16[128,896]{1,0:T(8,128)(2,1)S(1)}, u32[]{:S(2)}, u32[]{:S(2)}) collective-permute-start(bf16[128,896]{1,0:T(8,128)(2,1)S(1)} %attend_4_7.2.refs_0_.own_ref), channel_id=1, source_target_pairs={{0,1},{1,0},{2,3},{3,2},{4,5},{5,4},{6,7},{7,6},{8,9},{9,8},{10,11... | collective-permute-start | bytes 688136 | tf_op jit(solution)/shard_map/ppermute | solution.py:406
  21.2 1.9 %collective-permute-start.9 = (bf16[128,896]{1,0:T(8,128)(2,1)S(1)}, bf16[128,896]{1,0:T(8,128)(2,1)S(1)}, u32[]{:S(2)}, u32[]{:S(2)}) collective-permute-start(bf16[128,896]{1,0:T(8,128)(2,1)S(1)} %attend_4_7.3.refs_1_.own_ref), channel_id=1, source_target_pairs={{0,1},{1,0},{2,3},{3,2},{4,5},{5,4},{6,7},{7,6},{8,9},{9,8},{10,11... | collective-permute-start | bytes 688136 | tf_op jit(solution)/shard_map/ppermute | solution.py:406
  22.5 8.5 %collective-permute-start.11 = (bf16[128,896]{1,0:T(8,128)(2,1)S(1)}, bf16[128,896]{1,0:T(8,128)(2,1)S(1)}, u32[]{:S(2)}, u32[]{:S(2)}) collective-permute-start(bf16[128,896]{1,0:T(8,128)(2,1)S(1)} %away.3), channel_id=1, source_target_pairs={{0,2},{1,3},{2,0},{3,1},{4,6},{5,7},{6,4},{7,5},{8,10},{9,11},{10,... | collective-permute-start | bytes 688136 | tf_op jit(solution)/shard_map/ppermute | solution.py:406
  23.8 11.3 %collective-permute-start.10 = (bf16[128,896]{1,0:T(8,128)(2,1)S(1)}, bf16[128,896]{1,0:T(8,128)(2,1)S(1)}, u32[]{:S(2)}, u32[]{:S(2)}) collective-permute-start(bf16[128,896]{1,0:T(8,128)(2,1)S(1)} %away.2), channel_id=1, source_target_pairs={{0,2},{1,3},{2,0},{3,1},{4,6},{5,7},{6,4},{7,5},{8,10},{9,11},{10,... | collective-permute-start | bytes 688136 | tf_op jit(solution)/shard_map/ppermute | solution.py:406
